TPU v7x, 128 devices: a whole 4x4x4 slice. The times are simulated.
128 devices in a mesh: ma: 32 (over y, x, core), oct: 4 (over z).
Axes of the slice: x: 4, y: 4, z: 4, core: 2. Of those that a mesh axis runs over, the one named last changes fastest.
Arguments:
- fourier_wind: bfloat16 [2560, 64, 512], P(('ma', 'oct')), may hold values from -6 to 6
- quad_weight: float32 [2560], P('oct'), may hold values from 0.3 to 3
- p_table: bfloat16 [64, 2560, 2560], P('ma', 'oct'), may hold values from -0.125 to 0.125
- h_table: bfloat16 [64, 2560, 2560], P('ma', 'oct'), may hold values from -0.125 to 0.125
- wavenumbers: int32 [64], P('ma'), may hold values from 639 to 1921, as said below
- row_latitude: int32 [2560], replicated, may hold values from 0 to 2559, as said below
Outputs:
- rotational: bfloat16 [2560, 64, 512], P(('ma', 'oct'))
- divergent: bfloat16 [2560, 64, 512], P(('ma', 'oct'))
Inputs may be any that keep to these rules, and one draw needn't show every extreme that they name: Slots come in pairs 2 d and 2 d + 1 holding wavenumbers w and 2560 - w, with w between 639 and 1278; all wavenumbers distinct. `row_latitude`: A permutation; the rows of index o along oct (rows i with (i // 20) % (2560 // 640) == o) hold exactly the latitudes o * 640 to (o + 1) * 640 - 1.
All inputs are finite; a program needn't handle non-finite values.
Results may differ from a plain program's by a relative error of at most 0.0056.
Values may be sent and summed in bfloat16 or wider, within the bound.
No kernel may reach another device: no remote copies, remote signals or barrier semaphores. Data moves between devices by JAX's collectives and lax.ppermute only.
A program may use at most 128 MiB of HBM per device.

v0:
```python
import jax
import jax.numpy as jnp
from jax import lax
from jax.sharding import PartitionSpec as P

LMAX = 2559


def degree_factor(numbers, count):
    degree = jnp.arange(count).astype(jnp.float32)
    limit = numbers.astype(jnp.float32)[:, None]
    return jnp.where(
        degree[None, :] >= limit,
        -(LMAX * LMAX * 1.0) / jnp.maximum(degree * (degree + 1.0), 1.0)[None, :],
        0.0,
    )


def on_device(fourier_wind, quad_weight, p_table, h_table, wavenumbers, row_latitude):
    received = lax.all_to_all(fourier_wind, "ma", split_axis=1, concat_axis=0, tiled=True)
    n_owners = lax.axis_size("ma")
    n_groups = lax.axis_size("oct")
    group = lax.axis_index("oct")
    rows_dev = fourier_wind.shape[0]
    quarter = p_table.shape[1]
    degrees = p_table.shape[2]
    slots = p_table.shape[0]
    levels = fourier_wind.shape[2] // 4
    global_rows = (
        jnp.arange(n_owners)[:, None] * (n_groups * rows_dev)
        + group * rows_dev
        + jnp.arange(rows_dev)[None, :]
    ).reshape(-1)
    local_lat = row_latitude[global_rows] - group * quarter
    ordered = jnp.zeros((quarter,) + received.shape[1:], received.dtype).at[local_lat].set(received)
    weighted = (quad_weight[:, None, None] * ordered.astype(jnp.float32)).astype(jnp.bfloat16)
    proj_p = jnp.einsum("sjl,jsx->slx", p_table, weighted, preferred_element_type=jnp.float32)
    proj_h = jnp.einsum("sjl,jsx->slx", h_table, weighted, preferred_element_type=jnp.float32)
    proj_p = proj_p.reshape(slots, degrees, 4, levels)
    proj_h = proj_h.reshape(slots, degrees, 4, levels)
    rate = (wavenumbers.astype(jnp.float32) / LMAX)[:, None, None]
    spectra = jnp.stack(
        [
            -rate * proj_p[:, :, 3] + proj_h[:, :, 0],
            rate * proj_p[:, :, 2] + proj_h[:, :, 1],
            -rate * proj_p[:, :, 1] - proj_h[:, :, 2],
            rate * proj_p[:, :, 0] - proj_h[:, :, 3],
        ],
        axis=2,
    ).reshape(slots, degrees, 4 * levels)
    total = lax.psum(spectra, "oct")
    factor = degree_factor(wavenumbers, degrees)
    potentials = (total * factor[:, :, None]).astype(jnp.bfloat16)
    back_p = jnp.einsum("sjl,slx->jsx", p_table, potentials, preferred_element_type=jnp.float32)
    back_h = jnp.einsum("sjl,slx->jsx", h_table, potentials, preferred_element_type=jnp.float32)
    back_p = back_p.reshape(quarter, slots, 4, levels)
    back_h = back_h.reshape(quarter, slots, 4, levels)
    rate_rows = (wavenumbers.astype(jnp.float32) / LMAX)[None, :, None]
    rot = jnp.stack(
        [
            -back_h[:, :, 0],
            -back_h[:, :, 1],
            -rate_rows * back_p[:, :, 1],
            rate_rows * back_p[:, :, 0],
        ],
        axis=2,
    )
    div = jnp.stack(
        [
            -rate_rows * back_p[:, :, 3],
            rate_rows * back_p[:, :, 2],
            back_h[:, :, 2],
            back_h[:, :, 3],
        ],
        axis=2,
    )
    rot = rot.reshape(quarter, slots, 4 * levels).astype(jnp.bfloat16)[local_lat]
    div = div.reshape(quarter, slots, 4 * levels).astype(jnp.bfloat16)[local_lat]
    rotational, divergent = (
        lax.all_to_all(rot, "ma", split_axis=0, concat_axis=1, tiled=True),
        lax.all_to_all(div, "ma", split_axis=0, concat_axis=1, tiled=True),
    )
    return (rotational, divergent)


def solution(mesh):
    placed = (
        P(("ma", "oct"), None, None),
        P("oct"),
        P("ma", "oct", None),
        P("ma", "oct", None),
        P("ma"),
        P(),
    )
    return jax.shard_map(
        on_device,
        mesh=mesh,
        in_specs=placed,
        out_specs=(P(("ma", "oct"), None, None), P(("ma", "oct"), None, None)),
        check_vma=False,
    )
```

profile of v0, /device:TPU:0, one launch (start us, length us, event | category | flops | bytes accessed | tf_op | source)
XLA Modules:
  0.0 373.6 jit_solution(17592744431500836515)
XLA Ops:
  7.2 3.2 copy.29
  10.4 7.4 %all-to-all-start = ((bf16[20,64,512]{2,0,1:T(8,128)(2,1)}), bf16[20,64,512]{2,0,1:T(8,128)(2,1)S(1)}, u32[]{:S(2)}, u32[]{:S(2)}) async-start(bf16[20,64,512]{2,0,1:T(8,128)(2,1)} %copy.29), calls=%async_computation | async-start | bytes 3145728 | tf_op jit(solution)/shard_map/all_to_all | solution.py:20
  18.1 3.9 %gather_fusion = s32[640]{0:T(1024)S(1)} fusion(s32[2560]{0:T(1024)S(1)} %copy-done, s32[1024]{0:T(1024)S(1)} %pad_clamp_fusion.1), kind=kCustom, calls=%fused_computation | custom fusion | bytes 7680 | tf_op jit(solution)/shard_map/gather | solution.py:34
  22.0 19.7 %all-to-all-done = bf16[20,64,512]{2,0,1:T(8,128)(2,1)S(1)} async-done(((bf16[20,64,512]{2,0,1:T(8,128)(2,1)}), bf16[20,64,512]{2,0,1:T(8,128)(2,1)S(1)}, u32[]{:S(2)}, u32[]{:S(2)}) %all-to-all-start) | async-done | bytes 1310752 | tf_op jit(solution)/shard_map/all_to_all | solution.py:20
  43.4 19.4 %scatter_fusion = bf16[640,2,512]{2,1,0:T(2,128)(2,1)S(1)} fusion(bf16[640,2,512]{2,1,0:T(2,128)(2,1)S(1)} %broadcast_in_dim.10, s32[640]{0:T(1024)S(1)} %fusion.13, bf16[640,2,512]{2,1,0:T(2,128)(2,1)S(1)} %bitcast.37), kind=kCustom, calls=%fused_computation.3 | custom fusion | bytes 3934720 | tf_op jit(solution)/shard_map/scatter | solution.py:35
  62.8 6.8 %fusion.9 = f32[2,512,2560]{2,1,0:T(8,128)S(1)} fusion(bf16[2,640,2560]{2,1,0:T(8,128)(2,1)} %param.8, bf16[640,2,512]{2,1,0:T(2,128)(2,1)S(1)} %scatter_fusion, f32[640]{0:T(1024)S(1)} %copy-done.2), kind=kOutput, calls=%fused_computation.33 | convolution fusion | flops 3357409280 | bytes 18352640 | tf_op jit(solution)/shard_map/sjl,jsx->slx/dot_general | solution.py:37
  69.6 10.0 %fusion.8 = f32[2,512,2560]{2,1,0:T(8,128)} fusion(bf16[2,640,2560]{2,1,0:T(8,128)(2,1)} %param.9, bf16[640,2,512]{2,1,0:T(2,128)(2,1)S(1)} %scatter_fusion, f32[640]{0:T(1024)S(1)} %copy-done.2), kind=kOutput, calls=%fused_computation.32 | convolution fusion | flops 3357409280 | bytes 18352640 | tf_op jit(solution)/shard_map/sjl,jsx->slx/dot_general | solution.py:38
  79.6 5.3 %slice_add_fusion.1 = (f32[2,2560,1,128]{1,3,2,0:T(8,128)S(1)}, f32[2,2560,1,128]{1,3,2,0:T(8,128)S(1)}, f32[2,2560,1,128]{1,3,2,0:T(8,128)S(1)}, f32[2,2560,1,128]{1,3,2,0:T(8,128)S(1)}) fusion(f32[2,2560,4,128]{1,3,2,0:T(8,128)} %bitcast.31, f32[2,2560,4,128]{1,3,2,0:T(8,128)S(1)} %bitcast.30, f32[2]{0:T(128)S(1)} %get-tuple-element.16, ...), kind=kLoop, calls=%fused_computation.12 | loop fusion | flops 5242880 | bytes 31457296 | tf_op jit(solution)/shard_map/add | solution.py:44
  84.9 4.3 %pad_maximum_fusion = f32[2,2560,4,128]{1,3,2,0:T(8,128)} fusion(f32[2,2560,1,128]{1,3,2,0:T(8,128)S(1)} %get-tuple-element.6, f32[2,2560,1,128]{1,3,2,0:T(8,128)S(1)} %get-tuple-element.3, f32[2,2560,1,128]{1,3,2,0:T(8,128)S(1)} %get-tuple-element.7, f32[2,2560,1,128]{1,3,2,0:T(8,128)S(1)} %get-tuple-element.2), kind=kLoop, calls=%fused_computation.4 | loop fusion | flops 7864320 | bytes 20971520 | tf_op jit(solution)/shard_map/stack | solution.py:42
  89.4 192.3 %all-reduce.2.cloned.1.call-done = f32[2,2560,512]{1,2,0:T(8,128)} async-done(((f32[2,2560,512]{1,2,0:T(8,128)}), f32[2,2560,512]{1,2,0:T(8,128)}) %all-reduce.2.cloned.1.call-update) | async-done | bytes 10485776 | tf_op jit(solution)/shard_map/psum | solution.py:51
  281.7 8.9 %fusion.1 = f32[2,512,640]{2,1,0:T(8,128)S(1)} fusion(bf16[2,640,2560]{2,1,0:T(8,128)(2,1)} %param.9, f32[2,2560,512]{1,2,0:T(8,128)} %all-reduce.2.cloned.1.call-done, f32[2,2560]{1,0:T(2,128)S(1)} %compare_select_fusion), kind=kOutput, calls=%fused_computation.16 | convolution fusion | flops 3360686080 | bytes 19681280 | tf_op jit(solution)/shard_map/sjl,slx->jsx/dot_general | solution.py:55
  290.8 9.1 %fusion = f32[2,512,640]{2,1,0:T(8,128)S(1)} fusion(bf16[2,640,2560]{2,1,0:T(8,128)(2,1)} %param.8, f32[2,2560,512]{1,2,0:T(8,128)} %all-reduce.2.cloned.1.call-done, f32[2,2560]{1,0:T(2,128)S(1)} %compare_select_fusion), kind=kOutput, calls=%fused_computation.15 | convolution fusion | flops 3360686080 | bytes 19681280 | tf_op jit(solution)/shard_map/sjl,slx->jsx/dot_general | solution.py:54
  300.6 2.8 copy.41
  303.4 8.1 %gather_fusion.2 = bf16[640,2,512]{2,1,0:T(2,128)(2,1)} fusion(bf16[640,2,512]{2,1,0:T(2,128)(2,1)} %copy.41, s32[1024]{0:T(1024)S(1)} %pad_clamp_fusion), kind=kCustom, calls=%fused_computation.2 | custom fusion | bytes 2624000 | tf_op jit(solution)/shard_map/gather | solution.py:78
  311.5 7.1 %all-to-all-start.2 = ((bf16[640,2,512]{2,1,0:T(2,128)(2,1)}), bf16[640,2,512]{2,1,0:T(2,128)(2,1)S(1)}, u32[]{:S(2)}, u32[]{:S(2)}) async-start(bf16[640,2,512]{2,1,0:T(2,128)(2,1)} %gather_fusion.2), calls=%async_computation.2 | async-start | bytes 2621440 | tf_op jit(solution)/shard_map/all_to_all | solution.py:81
  318.5 2.8 copy.40
  321.3 8.1 %gather_fusion.1 = bf16[640,2,512]{2,1,0:T(2,128)(2,1)} fusion(bf16[640,2,512]{2,1,0:T(2,128)(2,1)} %copy.40, s32[1024]{0:T(1024)S(1)} %pad_clamp_fusion), kind=kCustom, calls=%fused_computation.1 | custom fusion | bytes 2624000 | tf_op jit(solution)/shard_map/gather | solution.py:77
  329.4 9.9 %all-to-all-done.2 = bf16[640,2,512]{2,1,0:T(2,128)(2,1)S(1)} async-done(((bf16[640,2,512]{2,1,0:T(2,128)(2,1)}), bf16[640,2,512]{2,1,0:T(2,128)(2,1)S(1)}, u32[]{:S(2)}, u32[]{:S(2)}) %all-to-all-start.2) | async-done | bytes 1310752 | tf_op jit(solution)/shard_map/all_to_all | solution.py:81
  339.3 4.0 %all-to-all-start.1 = ((bf16[640,2,512]{2,1,0:T(2,128)(2,1)}), bf16[640,2,512]{2,1,0:T(2,128)(2,1)S(1)}, u32[]{:S(2)}, u32[]{:S(2)}) async-start(bf16[640,2,512]{2,1,0:T(2,128)(2,1)} %gather_fusion.1), calls=%async_computation.1 | async-start | bytes 2621440 | tf_op jit(solution)/shard_map/all_to_all | solution.py:80
  343.3 2.4 copy.37
  345.7 4.1 %all_to_all.50 = bf16[20,64,512]{2,1,0:T(8,128)(2,1)} reshape(bf16[20,32,2,512]{3,2,1,0:T(2,128)(2,1)} %copy.37) | data formatting | bytes 2621440 | tf_op jit(solution)/shard_map/all_to_all | solution.py:81
  349.8 14.3 %all-to-all-done.1 = bf16[640,2,512]{2,1,0:T(2,128)(2,1)S(1)} async-done(((bf16[640,2,512]{2,1,0:T(2,128)(2,1)}), bf16[640,2,512]{2,1,0:T(2,128)(2,1)S(1)}, u32[]{:S(2)}, u32[]{:S(2)}) %all-to-all-start.1) | async-done | bytes 1310752 | tf_op jit(solution)/shard_map/all_to_all | solution.py:80
  364.1 1.3 copy.35
  365.4 1.4 all_to_all.46
  (29 shorter events, 2.9 us)
Async XLA Ops:
  7.2 10.9 %copy-start = (s32[2560]{0:T(1024)S(1)}, s32[2560]{0:T(1024)}, u32[]{:S(2)}) copy-start(s32[2560]{0:T(1024)} %param.11) | copy-start | bytes 30724
  10.4 31.3 %all-to-all-start = ((bf16[20,64,512]{2,0,1:T(8,128)(2,1)}), bf16[20,64,512]{2,0,1:T(8,128)(2,1)S(1)}, u32[]{:S(2)}, u32[]{:S(2)}) async-start(bf16[20,64,512]{2,0,1:T(8,128)(2,1)} %copy.29), calls=%async_computation | async-start | bytes 3145728 | tf_op jit(solution)/shard_map/all_to_all | solution.py:20
  17.8 4.2 %copy-start.3 = (s32[2]{0:T(128)S(1)}, s32[2]{0:T(128)}, u32[]{:S(2)}) copy-start(s32[2]{0:T(128)} %param.10) | copy-start | bytes 28
  17.8 263.9 %all-reduce.2.cloned.1.call-start = ((), (), s32[]{:S(2)}) async-start(), calls=%async_computation.3 | async-start | bytes 20971520 | tf_op jit(solution)/shard_map/psum | solution.py:51
  42.7 20.1 %copy-start.2 = (f32[640]{0:T(1024)S(1)}, f32[640]{0:T(1024)}, u32[]{:S(2)}) copy-start(f32[640]{0:T(1024)} %param.7) | copy-start | bytes 7684
  311.5 27.9 %all-to-all-start.2 = ((bf16[640,2,512]{2,1,0:T(2,128)(2,1)}), bf16[640,2,512]{2,1,0:T(2,128)(2,1)S(1)}, u32[]{:S(2)}, u32[]{:S(2)}) async-start(bf16[640,2,512]{2,1,0:T(2,128)(2,1)} %gather_fusion.2), calls=%async_computation.2 | async-start | bytes 2621440 | tf_op jit(solution)/shard_map/all_to_all | solution.py:81
  339.3 24.8 %all-to-all-start.1 = ((bf16[640,2,512]{2,1,0:T(2,128)(2,1)}), bf16[640,2,512]{2,1,0:T(2,128)(2,1)S(1)}, u32[]{:S(2)}, u32[]{:S(2)}) async-start(bf16[640,2,512]{2,1,0:T(2,128)(2,1)} %gather_fusion.1), calls=%async_computation.1 | async-start | bytes 2621440 | tf_op jit(solution)/shard_map/all_to_all | solution.py:80
  364.1 2.7 copy-start.1
Sparse Core Ops, SparseCore 0:
  89.4 192.3 all-reduce.1
where the time goes:
time: 374 us
  waiting for transfers between devices  236 us (63%)
  local copies, waits for them, and re-layouts  59.1 us (16%)
  matrix products  34.8 us (9%)
  starting transfers between devices  18.5 us (5%)
  between operations  14.3 us (4%)
  other arithmetic  10.6 us (3%)
    psum x1, waiting for transfers between devices, on_device(): total = lax.psum(spectra, 'oct')  192 us
    all_to_all x1, waiting for transfers between devices, on_device(): lax.all_to_all(fourier_wind, 'ma', split_axis=1, concat_axis=0, tiled=True)  19.7 us
    scatter x1, local copies, waits for them, and re-layouts, on_device(): jnp.zeros((quarter,) + received.shape[1:], received.dtype).at[local_lat]  19.4 us
    all_to_all x1, waiting for transfers between devices, on_device(): lax.all_to_all(rot, 'ma', split_axis=0, concat_axis=1, tiled=True)  14.3 us
    dot_general x1, matrix products, on_device(): jnp.einsum('sjl,jsx->slx', h_table, weighted, preferred_element_type=jnp....  9.98 us
    all_to_all x1, waiting for transfers between devices, on_device(): lax.all_to_all(div, 'ma', split_axis=0, concat_axis=1, tiled=True)  9.95 us
    dot_general x1, matrix products, on_device(): jnp.einsum('sjl,slx->jsx', p_table, potentials, preferred_element_type=jn...  9.13 us
    dot_general x1, matrix products, on_device(): jnp.einsum('sjl,slx->jsx', h_table, potentials, preferred_element_type=jn...  8.93 us
  transfers between devices with their start and end apart: 4, of which 4 were waited for; matrix products, arithmetic and copies ran while one was open for 5% of the time, Pallas kernels for 0%

commit v1 on v0

v1 whole, which is shorter than its diff:
```python
import functools

import jax
import jax.numpy as jnp
from jax import lax
from jax.experimental import pallas as pl
from jax.experimental.pallas import tpu as pltpu
from jax.sharding import PartitionSpec as P

LMAX = 2559
TILE = 128
GROUP = 3
PACK = 4
BF16 = jnp.bfloat16
F32 = jnp.float32
VMEM = 40 * 1024 * 1024


def dot(a, b, dims):
    return lax.dot_general(a, b, (dims, ((), ())), preferred_element_type=F32)


def pack_kernel(first_ref, second_ref, out_ref, wide_ref):
    rows, slots, lanes = first_ref.shape
    size = PACK * slots
    i = lax.broadcasted_iota(jnp.int32, (size, size), 0)
    j = lax.broadcasted_iota(jnp.int32, (size, size), 1)
    source = ((i >> 1) & (PACK - 1)) * slots + (i >> 3) * 2 + (i & 1)
    order = jnp.where(source == j, 1.0, 0.0).astype(BF16)
    for b in range(rows // PACK):
        for at, ref in enumerate((first_ref, second_ref)):
            block = ref[b * PACK:(b + 1) * PACK].reshape(size, lanes)
            moved = dot(order, block, ((1,), (0,)))
            wide_ref[:, 8 * b:8 * b + 8, at * lanes:(at + 1) * lanes] = moved.reshape(slots // 2, 8, lanes)
    out_ref[...] = wide_ref[...].astype(BF16)


def pack(wind, first, second):
    rows, slots, width = wind.shape
    lanes = width // 4
    return pl.pallas_call(
        pack_kernel,
        grid=(1,),
        out_shape=jax.ShapeDtypeStruct((slots // 2, rows * 2, 2 * lanes), BF16),
        in_specs=[
            pl.BlockSpec((rows, slots, lanes), lambda i: (0, 0, first)),
            pl.BlockSpec((rows, slots, lanes), lambda i: (0, 0, second)),
        ],
        out_specs=pl.BlockSpec((slots // 2, rows * 2, 2 * lanes), lambda i: (0, 0, 0)),
        scratch_shapes=[pltpu.VMEM((slots // 2, rows * 2, 2 * lanes), F32)],
        compiler_params=pltpu.CompilerParams(vmem_limit_bytes=VMEM),
        name="pack",
    )(wind, wind)


def unpack_kernel(rot_in, div_in, *refs):
    rot_out, div_out, wide_ref = refs[-3:]
    rows, slots, lanes = rot_out.shape
    size = PACK * slots
    i = lax.broadcasted_iota(jnp.int32, (size, size), 0)
    j = lax.broadcasted_iota(jnp.int32, (size, size), 1)
    slot = i & (slots - 1)
    source = (slot >> 1) * 8 + (i // slots) * 2 + (slot & 1)
    order = jnp.where(source == j, 1.0, 0.0).astype(BF16)
    for ref, out in ((rot_in, rot_out), (div_in, div_out)):
        wide_ref[...] = ref[...].astype(F32)
        for b in range(rows // PACK):
            block = wide_ref[:, 8 * b:8 * b + 8, :].reshape(size, lanes).astype(BF16)
            moved = dot(order, block, ((1,), (0,)))
            out[b * PACK:(b + 1) * PACK] = moved.reshape(PACK, slots, lanes).astype(BF16)


def unpack(payload, rows, base, stride, previous=()):
    pairs, both, width = payload.shape
    lanes = width // 4
    slots = pairs * 2
    shape = jax.ShapeDtypeStruct((rows, slots, width), BF16)
    out_spec = pl.BlockSpec((rows, slots, lanes), lambda i: (0, 0, base + stride * i))
    return pl.pallas_call(
        unpack_kernel,
        grid=(2,),
        out_shape=(shape, shape),
        in_specs=[
            pl.BlockSpec((pairs, both, lanes), lambda i: (0, 0, i)),
            pl.BlockSpec((pairs, both, lanes), lambda i: (0, 0, 2 + i)),
        ] + [pl.BlockSpec(memory_space=pl.ANY)] * len(previous),
        out_specs=(out_spec, out_spec),
        scratch_shapes=[pltpu.VMEM((pairs, both, lanes), F32)],
        input_output_aliases={2: 0, 3: 1} if previous else {},
        compiler_params=pltpu.CompilerParams(vmem_limit_bytes=VMEM),
        name="unpack",
    )(payload, payload, *previous)


def forward_kernel(meta, rate, recv, select, weight, *refs):
    p_refs, h_refs = refs[:GROUP], refs[GROUP:2 * GROUP]
    own, x1a, x1b, x2a, x2b, x3a, x3b, wind, spec = refs[2 * GROUP:]
    step = pl.program_id(0)
    quarter = wind.shape[2]
    levels = spec.shape[0] // 2

    @pl.when(step == 0)
    def _():
        by_lat = dot(recv[...], select[...], ((0,), (0,)))
        weighted = (by_lat * weight[...]).astype(BF16)
        wind[0] = weighted[:, :quarter]
        wind[1] = weighted[:, quarter:]

    base = step * GROUP
    first = meta[base]
    last = meta[base + GROUP - 1]

    def tile(slot, p, h):
        w = wind[slot]
        r = rate[slot]
        proj_p = dot(w, p, ((1,), (0,)))
        proj_h = dot(w, h, ((1,), (0,)))
        return (proj_h[:levels] - r * proj_p[levels:], r * proj_p[:levels] - proj_h[levels:])

    @pl.when(first == last)
    def _():
        psi, chi = tile(
            first,
            jnp.concatenate([ref[0] for ref in p_refs], axis=1),
            jnp.concatenate([ref[0] for ref in h_refs], axis=1),
        )
        spec[:levels] = psi
        spec[levels:] = chi

    @pl.when(first != last)
    def _():
        for k in range(GROUP):
            psi, chi = tile(meta[base + k], p_refs[k][0], h_refs[k][0])
            spec[:levels, k * TILE:(k + 1) * TILE] = psi
            spec[levels:, k * TILE:(k + 1) * TILE] = chi

    me = meta[meta.shape[0] - 1]
    chunk = own.shape[0]
    half = chunk // 2

    def part(k, at, size):
        start = lax.rem(me + k, 4) * chunk + at
        return spec[pl.ds(pl.multiple_of(start, half), size), :]

    own[...] = part(0, 0, chunk)
    x1a[...] = part(1, 0, half)
    x1b[...] = part(1, half, half).astype(BF16)
    x2a[...] = part(2, 0, half).astype(BF16)
    x2b[...] = part(2, half, half).astype(BF16)
    x3a[...] = part(3, 0, half).astype(BF16)
    x3b[...] = part(3, half, half)


def table_specs(quarter, n_tiles):
    def at(k):
        return lambda i, meta: (meta[i * GROUP + k], 0, meta[n_tiles + i * GROUP + k])

    return [pl.BlockSpec((1, quarter, TILE), at(k)) for k in range(GROUP)]


def forward(meta, rate, recv, select, weight, p_table, h_table, n_tiles):
    quarter = p_table.shape[1]
    both, width = recv.shape
    degrees = n_tiles * TILE
    chunk = width // 4
    half = chunk // 2
    shapes = [(chunk, F32), (half, F32), (half, BF16), (half, BF16), (half, BF16), (half, BF16), (half, F32)]
    once = pl.Buffered(1)
    return pl.pallas_call(
        forward_kernel,
        grid_spec=pltpu.PrefetchScalarGridSpec(
            num_scalar_prefetch=1,
            grid=(n_tiles // GROUP,),
            in_specs=[
                pl.BlockSpec(memory_space=pltpu.SMEM),
                pl.BlockSpec((both, width), lambda i, meta: (0, 0), pipeline_mode=once),
                pl.BlockSpec((both, both), lambda i, meta: (0, 0), pipeline_mode=once),
                pl.BlockSpec((1, both), lambda i, meta: (0, 0), pipeline_mode=once),
            ] + table_specs(quarter, n_tiles) * 2,
            out_specs=[pl.BlockSpec((n, GROUP * TILE), lambda i, meta: (0, i)) for n, _ in shapes],
            scratch_shapes=[
                pltpu.VMEM((2, width, quarter), BF16),
                pltpu.VMEM((width, GROUP * TILE), F32),
            ],
        ),
        out_shape=[jax.ShapeDtypeStruct((n, degrees), t) for n, t in shapes],
        compiler_params=pltpu.CompilerParams(vmem_limit_bytes=VMEM),
        cost_estimate=pl.CostEstimate(flops=6 * 10**9, bytes_accessed=16 * 10**6, transcendentals=0),
        name="forward",
    )(meta, rate, recv, select, weight, *([p_table] * GROUP), *([h_table] * GROUP))


def backward_kernel(meta, rate, select, *refs):
    parts, refs = refs[:8], refs[8:]
    p_refs, h_refs = refs[:GROUP], refs[GROUP:2 * GROUP]
    out, potential, sum_p, sum_h, winds = refs[2 * GROUP:]
    step = pl.program_id(0)
    quarter = sum_p.shape[1]
    levels = potential.shape[0] // 2
    me = meta[meta.shape[0] - 1]
    half = parts[0].shape[0]

    @pl.when(step == 0)
    def _():
        sum_p[...] = jnp.zeros_like(sum_p)
        sum_h[...] = jnp.zeros_like(sum_h)

    for n, ref in enumerate(parts):
        start = (lax.rem(me + n // 2, 4) * 2 + n % 2) * half
        potential[pl.ds(pl.multiple_of(start, half), half), :] = ref[...]

    base = step * GROUP
    first = meta[base]
    last = meta[base + GROUP - 1]

    @pl.when(first == last)
    def _():
        pot = potential[...]
        sum_p[first] += dot(jnp.concatenate([ref[0] for ref in p_refs], axis=1), pot, ((1,), (1,)))
        sum_h[first] += dot(jnp.concatenate([ref[0] for ref in h_refs], axis=1), pot, ((1,), (1,)))

    @pl.when(first != last)
    def _():
        for k in range(GROUP):
            pot = potential[:, k * TILE:(k + 1) * TILE]
            sum_p[meta[base + k]] += dot(p_refs[k][0], pot, ((1,), (1,)))
            sum_h[meta[base + k]] += dot(h_refs[k][0], pot, ((1,), (1,)))

    @pl.when(step == pl.num_programs(0) - 1)
    def _():
        for slot in range(2):
            r = rate[slot]
            rows = slice(slot * quarter, (slot + 1) * quarter)
            winds[rows, 0 * levels:1 * levels] = (-sum_h[slot, :, :levels]).astype(BF16)
            winds[rows, 1 * levels:2 * levels] = (r * sum_p[slot, :, :levels]).astype(BF16)
            winds[rows, 2 * levels:3 * levels] = (-r * sum_p[slot, :, levels:]).astype(BF16)
            winds[rows, 3 * levels:4 * levels] = sum_h[slot, :, levels:].astype(BF16)
        out[...] = dot(select[...], winds[...], ((1,), (0,))).astype(BF16)


def backward(meta, rate, select, parts, p_table, h_table, n_tiles):
    quarter = p_table.shape[1]
    half = parts[0].shape[0]
    width = half * 8
    both = select.shape[0]
    return pl.pallas_call(
        backward_kernel,
        grid_spec=pltpu.PrefetchScalarGridSpec(
            num_scalar_prefetch=1,
            grid=(n_tiles // GROUP,),
            in_specs=[
                pl.BlockSpec(memory_space=pltpu.SMEM),
                pl.BlockSpec((both, both), lambda i, meta: (0, 0), pipeline_mode=pl.Buffered(1)),
            ] + [pl.BlockSpec((half, GROUP * TILE), lambda i, meta: (0, i))] * 8
            + table_specs(quarter, n_tiles) * 2,
            out_specs=pl.BlockSpec((both, 2 * width), lambda i, meta: (0, 0)),
            scratch_shapes=[
                pltpu.VMEM((width, GROUP * TILE), BF16),
                pltpu.VMEM((2, quarter, width), F32),
                pltpu.VMEM((2, quarter, width), F32),
                pltpu.VMEM((both, 2 * width), BF16),
            ],
        ),
        out_shape=jax.ShapeDtypeStruct((both, 2 * width), BF16),
        compiler_params=pltpu.CompilerParams(vmem_limit_bytes=VMEM),
        cost_estimate=pl.CostEstimate(flops=6 * 10**9, bytes_accessed=16 * 10**6, transcendentals=0),
        name="backward",
    )(meta, rate, select, *parts, *([p_table] * GROUP), *([h_table] * GROUP))


def on_device(fourier_wind, quad_weight, p_table, h_table, wavenumbers, row_latitude):
    owners = lax.axis_size("ma")
    groups = lax.axis_size("oct")
    me = lax.axis_index("oct")
    rows = fourier_wind.shape[0]
    quarter = p_table.shape[1]
    degrees = p_table.shape[2]
    count = degrees // TILE
    n_tiles = count + 1
    up = [(i, (i + 1) % groups) for i in range(groups)]
    down = [(i, (i - 1) % groups) for i in range(groups)]

    sent = [pack(fourier_wind, 0, 3), pack(fourier_wind, 1, 2)]
    received = [lax.all_to_all(x, "ma", 0, 0, tiled=True) for x in sent]

    low = wavenumbers[0] // TILE
    n_first = count - low
    start = wavenumbers[1] // TILE
    t = jnp.arange(n_tiles)
    slot = (t >= n_first).astype(jnp.int32)
    tile_at = jnp.where(slot == 0, low + t, start + t - n_first)
    real = tile_at < count
    tile_at = jnp.minimum(tile_at, count - 1)
    meta = jnp.concatenate([slot, tile_at, me[None]]).astype(jnp.int32)
    rate = wavenumbers.astype(F32) / LMAX

    degree = (tile_at[:, None] * TILE + jnp.arange(TILE)[None, :]).astype(F32)
    limit = jnp.where(slot == 0, wavenumbers[0], wavenumbers[1]).astype(F32)[:, None]
    factor = jnp.where(
        (degree >= limit) & real[:, None],
        -(LMAX * LMAX * 1.0) / jnp.maximum(degree * (degree + 1.0), 1.0),
        0.0,
    ).reshape(1, n_tiles * TILE)

    local = lax.dynamic_index_in_dim(row_latitude.reshape(owners, groups, rows), me, 1, keepdims=False) - me * quarter
    target = (local[:, :, None] + quarter * jnp.arange(2)[None, None, :]).reshape(-1, 1)
    select = (target == jnp.arange(2 * quarter)[None, :]).astype(BF16)
    weight = jnp.concatenate([quad_weight, quad_weight]).reshape(1, -1)

    outs = []
    for n in range(2):
        sign = rate if n == 0 else -rate
        own, x1a, x1b, x2a, x2b, x3a, x3b = forward(
            meta, sign, received[n].reshape(2 * quarter, -1), select, weight, p_table, h_table, n_tiles)
        half = x1a.shape[0]
        a = lax.ppermute(x2a, "oct", up)
        b = lax.ppermute(x2b, "oct", down)
        c = lax.ppermute(x1b, "oct", up)
        d = lax.ppermute(x3a, "oct", down)
        a = lax.ppermute((a.astype(F32) + x1a).astype(BF16), "oct", up)
        b = lax.ppermute((b.astype(F32) + x3b).astype(BF16), "oct", down)
        pot_a = ((own[:half] + a.astype(F32) + d.astype(F32)) * factor).astype(BF16)
        pot_b = ((own[half:] + c.astype(F32) + b.astype(F32)) * factor).astype(BF16)
        below_a = lax.ppermute(pot_a, "oct", up)
        above_b = lax.ppermute(pot_b, "oct", down)
        below_b = lax.ppermute(pot_b, "oct", up)
        above_a = lax.ppermute(pot_a, "oct", down)
        far_a = lax.ppermute(below_a, "oct", up)
        far_b = lax.ppermute(above_b, "oct", down)
        parts = (pot_a, pot_b, above_a, above_b, far_a, far_b, below_a, below_b)
        payload = backward(meta, sign, select, parts, p_table, h_table, n_tiles)
        outs.append(lax.all_to_all(payload.reshape(owners, 2 * rows, -1), "ma", 0, 0, tiled=True))

    done = unpack(outs[0], rows, 0, 3)
    return tuple(unpack(outs[1], rows, 1, 1, done))


def solution(mesh):
    placed = (
        P(("ma", "oct"), None, None),
        P("oct"),
        P("ma", "oct", None),
        P("ma", "oct", None),
        P("ma"),
        P(),
    )
    return jax.shard_map(
        on_device,
        mesh=mesh,
        in_specs=placed,
        out_specs=(P(("ma", "oct"), None, None), P(("ma", "oct"), None, None)),
        check_vma=False,
    )
```

time: 374 us -> 193 us (0.52)
  waiting for transfers between devices: 236 us -> 43.7 us
  starting transfers between devices: 18.5 us -> 66.1 us
  Pallas kernels: 0 us -> 47.2 us
  local copies, waits for them, and re-layouts: 59.1 us -> 20.3 us
  matrix products: 34.8 us -> 0 us
  between operations: 14.3 us -> 5.68 us
    psum x1 -> x0, waiting for transfers between devices: 192 us -> none  [on_device(): total = lax.psum(spectra, 'oct')]
    pallas_call x0 -> x8, Pallas kernels: none -> 47.2 us  [the longest x2 20.9 us: backward(): pl.pallas_call(backward_kernel, grid_spec=pltpu.PrefetchScalarGridSpec(nu...]
    ppermute x0 -> x24, starting transfers between devices: none -> 37.6 us  [the longest x2 6.96 us: on_device(): far_b = lax.ppermute(above_b, 'oct', down)]
    dot_general x4 -> x0, matrix products: 34.8 us -> none  [the longest x1 9.98 us: on_device(): jnp.einsum('sjl,jsx->slx', h_table, weighted, preferred_element_type=jnp....]
    all_to_all x3 -> x4, waiting for transfers between devices: 44 us -> 20.2 us  [the longest x2 18.8 us: on_device(): lax.all_to_all(payload.reshape(owners, 2 * rows, -1), 'ma', 0, 0, tiled=T...]
    ppermute x0 -> x24, waiting for transfers between devices: none -> 23.5 us  [the longest x2 7.03 us: on_device(): far_a = lax.ppermute(below_a, 'oct', up)]
    gather x3 -> x0, local copies, waits for them, and re-layouts: 20 us -> none  [the longest x1 8.06 us: on_device(): rot.reshape(quarter, slots, 4 * levels).astype(jnp.bfloat16)[local_lat]]
    scatter x1 -> x0, local copies, waits for them, and re-layouts: 19.4 us -> none  [on_device(): jnp.zeros((quarter,) + received.shape[1:], received.dtype).at[local_lat]]
  transfers between devices with their start and end apart: 4 -> 28, of which waited for: 4 -> 13; matrix products, arithmetic and copies ran while one was open for 5% -> 4% of each run, Pallas kernels for 0% -> 17%
where the time goes in v1:
time: 193 us; the launch traced here: 191 us
  starting transfers between devices  66.1 us (34%)
  Pallas kernels  47.2 us (24%)
  waiting for transfers between devices  43.7 us (23%)
  local copies, waits for them, and re-layouts  20.3 us (11%)
  other arithmetic  8.36 us (4%)
  between operations  5.68 us (3%)
    pallas_call x2, Pallas kernels, backward(): pl.pallas_call(backward_kernel, grid_spec=pltpu.PrefetchScalarGridSpec(nu...  20.9 us
    pallas_call x2, Pallas kernels, forward(): pl.pallas_call(forward_kernel, grid_spec=pltpu.PrefetchScalarGridSpec(num...  19.6 us
    unnamed x44, local copies, waits for them, and re-layouts  19.4 us
    all_to_all x2, waiting for transfers between devices, on_device(): lax.all_to_all(payload.reshape(owners, 2 * rows, -1), 'ma', 0, 0, tiled=T...  18.8 us
    all_to_all x2, starting transfers between devices, on_device(): lax.all_to_all(payload.reshape(owners, 2 * rows, -1), 'ma', 0, 0, tiled=T...  14.9 us
    all_to_all x2, starting transfers between devices, on_device(): received = [lax.all_to_all(x, 'ma', 0, 0, tiled=True) for x in sent]  13.7 us
    ppermute x2, waiting for transfers between devices, on_device(): far_a = lax.ppermute(below_a, 'oct', up)  7.03 us
    ppermute x2, starting transfers between devices, on_device(): far_b = lax.ppermute(above_b, 'oct', down)  6.96 us
  transfers between devices with their start and end apart: 28, of which 13 were waited for; matrix products, arithmetic and copies ran while one was open for 4% of the time, Pallas kernels for 17%

profile of v1, /device:TPU:0, one launch (start us, length us, event | category | flops | bytes accessed | tf_op | source)
XLA Modules:
  0.0 191.4 jit_solution(3744931795443546537)
XLA Ops:
  3.3 7.5 %all-to-all-start.2 = ((bf16[32,40,256]{2,1,0:T(8,128)(2,1)}), bf16[32,40,256]{2,1,0:T(8,128)(2,1)S(1)}, u32[]{:S(2)}, u32[]{:S(2)}) async-start(bf16[32,40,256]{2,1,0:T(8,128)(2,1)} %pack.3), calls=%async_computation.2 | async-start | bytes 1310720 | tf_op jit(solution)/shard_map/all_to_all | solution.py:284
  24.1 6.1 %all-to-all-start = ((bf16[32,40,256]{2,1,0:T(8,128)(2,1)}), bf16[32,40,256]{2,1,0:T(8,128)(2,1)}, u32[]{:S(2)}, u32[]{:S(2)}) async-start(bf16[32,40,256]{2,1,0:T(8,128)(2,1)} %pack.2), calls=%async_computation | async-start | bytes 1310720 | tf_op jit(solution)/shard_map/all_to_all | solution.py:284
  30.3 2.9 %copy-done = bf16[2,640,2560]{2,1,0:T(8,128)(2,1)S(1)} copy-done((bf16[2,640,2560]{2,1,0:T(8,128)(2,1)S(1)}, bf16[2,640,2560]{2,1,0:T(8,128)(2,1)}, u32[]{:S(2)}) %copy-start) | copy-done | bytes 6553624
  35.1 9.8 %forward.3 = (f32[64,2688]{1,0:T(8,128)S(1)}, f32[32,2688]{1,0:T(8,128)S(1)}, bf16[32,2688]{1,0:T(8,128)(2,1)S(1)}, bf16[32,2688]{1,0:T(8,128)(2,1)}, bf16[32,26...) custom-call(s32[43]{0:T(128)S(1)} %pad_add_fusion.meta, f32[2]{0:T(128)S(1)} %get-tuple-element.42.rate, ...), custom_call_target="tpu_custom_call" | custom-call | flops 6000000000 | bytes 16000000 | tf_op jit(solution)/shard_map/forward/pallas_call | solution.py:169
  50.5 3.2 %collective-permute-start.16 = (bf16[32,2688]{1,0:T(8,128)(2,1)}, bf16[32,2688]{1,0:T(8,128)(2,1)}, u32[]{:S(2)}, u32[]{:S(2)}) collective-permute-start(bf16[32,2688]{1,0:T(8,128)(2,1)} %get-tuple-element.30), channel_id=1, source_target_pairs={{0,3},{1,0},{2,1},{3,2},{4,7},{5,4},{6,5},{7,6},{8,11},{9,8},{10,9... | collective-permute-start | bytes 516104 | tf_op jit(solution)/shard_map/ppermute | solution.py:317
  58.5 9.8 %forward.2 = (f32[64,2688]{1,0:T(8,128)S(1)}, f32[32,2688]{1,0:T(8,128)S(1)}, bf16[32,2688]{1,0:T(8,128)(2,1)S(1)}, bf16[32,2688]{1,0:T(8,128)(2,1)S(1)}, bf16[3...) custom-call(s32[43]{0:T(128)S(1)} %pad_add_fusion.meta, ...), custom_call_target="tpu_custom_call" | custom-call | flops 6000000000 | bytes 16000000 | tf_op jit(solution)/shard_map/forward/pallas_call | solution.py:169
  68.4 3.2 %collective-permute-start.2 = (bf16[32,2688]{1,0:T(8,128)(2,1)S(1)}, bf16[32,2688]{1,0:T(8,128)(2,1)S(1)}, u32[]{:S(2)}, u32[]{:S(2)}) collective-permute-start(bf16[32,2688]{1,0:T(8,128)(2,1)S(1)} %get-tuple-element.21), channel_id=1, source_target_pairs={{0,3},{1,0},{2,1},{3,2},{4,7},{5,4},{6,5},{7,6},{8,11},{9,8},{10,9... | collective-permute-start | bytes 516104 | tf_op jit(solution)/shard_map/ppermute | solution.py:319
  77.1 3.8 %collective-permute-done.4 = bf16[32,2688]{1,0:T(8,128)(2,1)S(1)} collective-permute-done((bf16[32,2688]{1,0:T(8,128)(2,1)S(1)}, bf16[32,2688]{1,0:T(8,128)(2,1)S(1)}, u32[]{:S(2)}, u32[]{:S(2)}) %collective-permute-start.4) | collective-permute-done | bytes 172064 | tf_op jit(solution)/shard_map/ppermute | solution.py:317
  81.0 3.3 %collective-permute-start.17 = (bf16[32,2688]{1,0:T(8,128)(2,1)S(1)}, bf16[32,2688]{1,0:T(8,128)(2,1)S(1)}, u32[]{:S(2)}, u32[]{:S(2)}) collective-permute-start(bf16[32,2688]{1,0:T(8,128)(2,1)S(1)} %add_convert_fusion), channel_id=1, source_target_pairs={{0,3},{1,0},{2,1},{3,2},{4,7},{5,4},{6,5},{7,6},{8,11},{9,8},{10,9... | collective-permute-start | bytes 516104 | tf_op jit(solution)/shard_map/ppermute | solution.py:321
  84.3 3.2 %collective-permute-start.5 = (bf16[32,2688]{1,0:T(8,128)(2,1)S(1)}, bf16[32,2688]{1,0:T(8,128)(2,1)S(1)}, u32[]{:S(2)}, u32[]{:S(2)}) collective-permute-start(bf16[32,2688]{1,0:T(8,128)(2,1)S(1)} %add_convert_fusion.2), channel_id=1, source_target_pairs={{0,3},{1,0},{2,1},{3,2},{4,7},{5,4},{6,5},{7,6},{8,11},{9,8},{10,9... | collective-permute-start | bytes 516104 | tf_op jit(solution)/shard_map/ppermute | solution.py:321
  92.3 3.3 %collective-permute-start.19 = (bf16[32,2688]{1,0:T(8,128)(2,1)S(1)}, bf16[32,2688]{1,0:T(8,128)(2,1)S(1)}, u32[]{:S(2)}, u32[]{:S(2)}) collective-permute-start(bf16[32,2688]{1,0:T(8,128)(2,1)S(1)} %get-tuple-element.36.refs_1_), channel_id=1, source_target_pairs={{0,3},{1,0},{2,1},{3,2},{4,7},{5,4},{6,5},{7,6},{8,11},{9,8},{10,9... | collective-permute-start | bytes 516104 | tf_op jit(solution)/shard_map/ppermute | solution.py:325
  95.6 3.3 %collective-permute-start.18 = (bf16[32,2688]{1,0:T(8,128)(2,1)S(1)}, bf16[32,2688]{1,0:T(8,128)(2,1)S(1)}, u32[]{:S(2)}, u32[]{:S(2)}) collective-permute-start(bf16[32,2688]{1,0:T(8,128)(2,1)S(1)} %get-tuple-element.37.refs_0_), channel_id=1, source_target_pairs={{0,3},{1,0},{2,1},{3,2},{4,7},{5,4},{6,5},{7,6},{8,11},{9,8},{10,9... | collective-permute-start | bytes 516104 | tf_op jit(solution)/shard_map/ppermute | solution.py:327
  100.3 3.7 %collective-permute-start.22 = (bf16[32,2688]{1,0:T(8,128)(2,1)S(1)}, bf16[32,2688]{1,0:T(8,128)(2,1)S(1)}, u32[]{:S(2)}, u32[]{:S(2)}) collective-permute-start(bf16[32,2688]{1,0:T(8,128)(2,1)S(1)} %collective-permute-done.19.refs_3_), channel_id=1, source_target_pairs={{0,3},{1,0},{2,1},{3,2},{4,7},{5,4},{6,5},{7,6},{8,11},{9,8},{10,9... | collective-permute-start | bytes 516104 | tf_op jit(solution)/shard_map/ppermute | solution.py:329
  106.9 3.7 %collective-permute-done.21.refs_4_ = bf16[32,2688]{1,0:T(8,128)(2,1)S(1)} collective-permute-done((bf16[32,2688]{1,0:T(8,128)(2,1)S(1)}, bf16[32,2688]{1,0:T(8,128)(2,1)S(1)}, u32[]{:S(2)}, u32[]{:S(2)}) %collective-permute-start.21) | collective-permute-done | bytes 172064 | tf_op jit(solution)/shard_map/ppermute | solution.py:328
  110.6 10.5 %backward.3 = bf16[1280,512]{1,0:T(8,128)(2,1)S(1)} custom-call(s32[43]{0:T(128)S(1)} %pad_add_fusion.meta, f32[2]{0:T(128)S(1)} %get-tuple-element.42.rate, bf16[1280,1280]{1,0:T(8,128)(2,1)S(1)} %copy-done.5, bf16[32,2688]{1,0:T(8,128)(2,1)S(1)} %get-tuple-element.37.refs_0_, bf16[32,2688]{1,0:T(8,128)(2,1)S(1)} %get-tuple-element.36.refs_1_, ...), custom_call_target="tpu_custom_call" | custom-call | flops 6000000000 | bytes 16000000 | tf_op jit(solution)/shard_map/backward/pallas_call | solution.py:246
  122.2 7.5 %all-to-all-start.3 = ((bf16[32,40,512]{2,1,0:T(8,128)(2,1)}), bf16[32,40,512]{2,1,0:T(8,128)(2,1)S(1)}, u32[]{:S(2)}, u32[]{:S(2)}) async-start(bf16[32,40,512]{2,1,0:T(8,128)(2,1)} %bitcast.25), calls=%async_computation.3 | async-start | bytes 2621440 | tf_op jit(solution)/shard_map/all_to_all | solution.py:332
  129.7 3.2 %collective-permute-start.7 = (bf16[32,2688]{1,0:T(8,128)(2,1)S(1)}, bf16[32,2688]{1,0:T(8,128)(2,1)S(1)}, u32[]{:S(2)}, u32[]{:S(2)}) collective-permute-start(bf16[32,2688]{1,0:T(8,128)(2,1)S(1)} %get-tuple-element.41.refs_1_), channel_id=1, source_target_pairs={{0,3},{1,0},{2,1},{3,2},{4,7},{5,4},{6,5},{7,6},{8,11},{9,8},{10,9... | collective-permute-start | bytes 516104 | tf_op jit(solution)/shard_map/ppermute | solution.py:325
  135.0 3.1 %collective-permute-done.8.refs_6_ = bf16[32,2688]{1,0:T(8,128)(2,1)S(1)} collective-permute-done((bf16[32,2688]{1,0:T(8,128)(2,1)S(1)}, bf16[32,2688]{1,0:T(8,128)(2,1)S(1)}, u32[]{:S(2)}, u32[]{:S(2)}) %collective-permute-start.8) | collective-permute-done | bytes 172064 | tf_op jit(solution)/shard_map/ppermute | solution.py:324
  138.1 3.3 %collective-permute-start.10 = (bf16[32,2688]{1,0:T(8,128)(2,1)S(1)}, bf16[32,2688]{1,0:T(8,128)(2,1)S(1)}, u32[]{:S(2)}, u32[]{:S(2)}) collective-permute-start(bf16[32,2688]{1,0:T(8,128)(2,1)S(1)} %collective-permute-done.7.refs_3_), channel_id=1, source_target_pairs={{0,3},{1,0},{2,1},{3,2},{4,7},{5,4},{6,5},{7,6},{8,11},{9,8},{10,9... | collective-permute-start | bytes 516104 | tf_op jit(solution)/shard_map/ppermute | solution.py:329
  141.5 3.3 %collective-permute-done.9.refs_4_ = bf16[32,2688]{1,0:T(8,128)(2,1)S(1)} collective-permute-done((bf16[32,2688]{1,0:T(8,128)(2,1)S(1)}, bf16[32,2688]{1,0:T(8,128)(2,1)S(1)}, u32[]{:S(2)}, u32[]{:S(2)}) %collective-permute-start.9) | collective-permute-done | bytes 172064 | tf_op jit(solution)/shard_map/ppermute | solution.py:328
  144.8 2.9 %copy-done.2 = bf16[2,640,2560]{2,1,0:T(8,128)(2,1)S(1)} copy-done((bf16[2,640,2560]{2,1,0:T(8,128)(2,1)S(1)}, bf16[2,640,2560]{2,1,0:T(8,128)(2,1)}, u32[]{:S(2)}) %copy-start.2) | copy-done | bytes 6553624
  149.6 10.5 %backward.2 = bf16[1280,512]{1,0:T(8,128)(2,1)S(1)} custom-call(s32[43]{0:T(128)S(1)} %pad_add_fusion.meta, f32[2]{0:T(128)S(1)} %get-tuple-element.43.rate, bf16[1280,1280]{1,0:T(8,128)(2,1)S(1)} %copy-done.6, bf16[32,2688]{1,0:T(8,128)(2,1)S(1)} %get-tuple-element.40.refs_0_, bf16[32,2688]{1,0:T(8,128)(2,1)S(1)} %get-tuple-element.41.refs_1_, ...), custom_call_target="tpu_custom_call" | custom-call | flops 6000000000 | bytes 16000000 | tf_op jit(solution)/shard_map/backward/pallas_call | solution.py:246
  161.2 7.4 %all-to-all-start.1 = ((bf16[32,40,512]{2,1,0:T(8,128)(2,1)}), bf16[32,40,512]{2,1,0:T(8,128)(2,1)S(1)}, u32[]{:S(2)}, u32[]{:S(2)}) async-start(bf16[32,40,512]{2,1,0:T(8,128)(2,1)} %bitcast.26), calls=%async_computation.1 | async-start | bytes 2621440 | tf_op jit(solution)/shard_map/all_to_all | solution.py:332
  170.6 18.8 %all-to-all-done.1.rot_in.div_in = bf16[32,40,512]{2,1,0:T(8,128)(2,1)S(1)} async-done(((bf16[32,40,512]{2,1,0:T(8,128)(2,1)}), bf16[32,40,512]{2,1,0:T(8,128)(2,1)S(1)}, u32[]{:S(2)}, u32[]{:S(2)}) %all-to-all-start.1) | async-done | bytes 1310752 | tf_op jit(solution)/shard_map/all_to_all | solution.py:332
  (106 shorter events, 48.4 us)
Async XLA Ops:
  3.3 20.8 %all-to-all-start.2 = ((bf16[32,40,256]{2,1,0:T(8,128)(2,1)}), bf16[32,40,256]{2,1,0:T(8,128)(2,1)S(1)}, u32[]{:S(2)}, u32[]{:S(2)}) async-start(bf16[32,40,256]{2,1,0:T(8,128)(2,1)} %pack.3), calls=%async_computation.2 | async-start | bytes 1310720 | tf_op jit(solution)/shard_map/all_to_all | solution.py:284
  24.1 29.7 %all-to-all-start = ((bf16[32,40,256]{2,1,0:T(8,128)(2,1)}), bf16[32,40,256]{2,1,0:T(8,128)(2,1)}, u32[]{:S(2)}, u32[]{:S(2)}) async-start(bf16[32,40,256]{2,1,0:T(8,128)(2,1)} %pack.2), calls=%async_computation | async-start | bytes 1310720 | tf_op jit(solution)/shard_map/all_to_all | solution.py:284
  46.4 22.0 %collective-permute-start.12 = (bf16[32,2688]{1,0:T(8,128)(2,1)}, bf16[32,2688]{1,0:T(8,128)(2,1)}, u32[]{:S(2)}, u32[]{:S(2)}) collective-permute-start(bf16[32,2688]{1,0:T(8,128)(2,1)} %get-tuple-element.26), channel_id=1, source_target_pairs={{0,1},{1,2},{2,3},{3,0},{4,5},{5,6},{6,7},{7,4},{8,9},{9,10},{10,1... | collective-permute-start | bytes 516104 | tf_op jit(solution)/shard_map/ppermute | solution.py:316
  48.4 32.6 %collective-permute-start.14 = (bf16[32,2688]{1,0:T(8,128)(2,1)}, bf16[32,2688]{1,0:T(8,128)(2,1)}, u32[]{:S(2)}, u32[]{:S(2)}) collective-permute-start(bf16[32,2688]{1,0:T(8,128)(2,1)} %get-tuple-element.28), channel_id=1, source_target_pairs={{0,3},{1,0},{2,1},{3,2},{4,7},{5,4},{6,5},{7,6},{8,11},{9,8},{10,9... | collective-permute-start | bytes 516104 | tf_op jit(solution)/shard_map/ppermute | solution.py:319
  50.5 33.8 %collective-permute-start.15 = (bf16[32,2688]{1,0:T(8,128)(2,1)S(1)}, bf16[32,2688]{1,0:T(8,128)(2,1)}, u32[]{:S(2)}, u32[]{:S(2)}) collective-permute-start(bf16[32,2688]{1,0:T(8,128)(2,1)S(1)} %get-tuple-element.29), channel_id=1, source_target_pairs={{0,1},{1,2},{2,3},{3,0},{4,5},{5,6},{6,7},{7,4},{8,9},{9,10},{10,1... | collective-permute-start | bytes 516104 | tf_op jit(solution)/shard_map/ppermute | solution.py:318
  50.5 22.2 %collective-permute-start.16 = (bf16[32,2688]{1,0:T(8,128)(2,1)}, bf16[32,2688]{1,0:T(8,128)(2,1)}, u32[]{:S(2)}, u32[]{:S(2)}) collective-permute-start(bf16[32,2688]{1,0:T(8,128)(2,1)} %get-tuple-element.30), channel_id=1, source_target_pairs={{0,3},{1,0},{2,1},{3,2},{4,7},{5,4},{6,5},{7,6},{8,11},{9,8},{10,9... | collective-permute-start | bytes 516104 | tf_op jit(solution)/shard_map/ppermute | solution.py:317
  68.3 7.2 %collective-permute-start = (bf16[32,2688]{1,0:T(8,128)(2,1)S(1)}, bf16[32,2688]{1,0:T(8,128)(2,1)S(1)}, u32[]{:S(2)}, u32[]{:S(2)}) collective-permute-start(bf16[32,2688]{1,0:T(8,128)(2,1)S(1)} %get-tuple-element.19), channel_id=1, source_target_pairs={{0,1},{1,2},{2,3},{3,0},{4,5},{5,6},{6,7},{7,4},{8,9},{9,10},{10,1... | collective-permute-start | bytes 516104 | tf_op jit(solution)/shard_map/ppermute | solution.py:316
  68.4 15.8 %collective-permute-start.2 = (bf16[32,2688]{1,0:T(8,128)(2,1)S(1)}, bf16[32,2688]{1,0:T(8,128)(2,1)S(1)}, u32[]{:S(2)}, u32[]{:S(2)}) collective-permute-start(bf16[32,2688]{1,0:T(8,128)(2,1)S(1)} %get-tuple-element.21), channel_id=1, source_target_pairs={{0,3},{1,0},{2,1},{3,2},{4,7},{5,4},{6,5},{7,6},{8,11},{9,8},{10,9... | collective-permute-start | bytes 516104 | tf_op jit(solution)/shard_map/ppermute | solution.py:319
  72.7 14.9 %collective-permute-start.3 = (bf16[32,2688]{1,0:T(8,128)(2,1)S(1)}, bf16[32,2688]{1,0:T(8,128)(2,1)S(1)}, u32[]{:S(2)}, u32[]{:S(2)}) collective-permute-start(bf16[32,2688]{1,0:T(8,128)(2,1)S(1)} %get-tuple-element.22), channel_id=1, source_target_pairs={{0,1},{1,2},{2,3},{3,0},{4,5},{5,6},{6,7},{7,4},{8,9},{9,10},{10,1... | collective-permute-start | bytes 516104 | tf_op jit(solution)/shard_map/ppermute | solution.py:318
  80.9 8.1 %collective-permute-start.13 = (bf16[32,2688]{1,0:T(8,128)(2,1)S(1)}, bf16[32,2688]{1,0:T(8,128)(2,1)S(1)}, u32[]{:S(2)}, u32[]{:S(2)}) collective-permute-start(bf16[32,2688]{1,0:T(8,128)(2,1)S(1)} %add_convert_fusion.1), channel_id=1, source_target_pairs={{0,1},{1,2},{2,3},{3,0},{4,5},{5,6},{6,7},{7,4},{8,9},{9,10},{10,1... | collective-permute-start | bytes 516104 | tf_op jit(solution)/shard_map/ppermute | solution.py:320
  81.0 8.1 %collective-permute-start.17 = (bf16[32,2688]{1,0:T(8,128)(2,1)S(1)}, bf16[32,2688]{1,0:T(8,128)(2,1)S(1)}, u32[]{:S(2)}, u32[]{:S(2)}) collective-permute-start(bf16[32,2688]{1,0:T(8,128)(2,1)S(1)} %add_convert_fusion), channel_id=1, source_target_pairs={{0,3},{1,0},{2,1},{3,2},{4,7},{5,4},{6,5},{7,6},{8,11},{9,8},{10,9... | collective-permute-start | bytes 516104 | tf_op jit(solution)/shard_map/ppermute | solution.py:321
  84.3 6.6 %collective-permute-start.1 = (bf16[32,2688]{1,0:T(8,128)(2,1)S(1)}, bf16[32,2688]{1,0:T(8,128)(2,1)S(1)}, u32[]{:S(2)}, u32[]{:S(2)}) collective-permute-start(bf16[32,2688]{1,0:T(8,128)(2,1)S(1)} %add_convert_fusion.3), channel_id=1, source_target_pairs={{0,1},{1,2},{2,3},{3,0},{4,5},{5,6},{6,7},{7,4},{8,9},{9,10},{10,1... | collective-permute-start | bytes 516104 | tf_op jit(solution)/shard_map/ppermute | solution.py:320
  92.3 8.0 %collective-permute-start.19 = (bf16[32,2688]{1,0:T(8,128)(2,1)S(1)}, bf16[32,2688]{1,0:T(8,128)(2,1)S(1)}, u32[]{:S(2)}, u32[]{:S(2)}) collective-permute-start(bf16[32,2688]{1,0:T(8,128)(2,1)S(1)} %get-tuple-element.36.refs_1_), channel_id=1, source_target_pairs={{0,3},{1,0},{2,1},{3,2},{4,7},{5,4},{6,5},{7,6},{8,11},{9,8},{10,9... | collective-permute-start | bytes 516104 | tf_op jit(solution)/shard_map/ppermute | solution.py:325
  95.6 8.4 %collective-permute-start.20 = (bf16[32,2688]{1,0:T(8,128)(2,1)S(1)}, bf16[32,2688]{1,0:T(8,128)(2,1)S(1)}, u32[]{:S(2)}, u32[]{:S(2)}) collective-permute-start(bf16[32,2688]{1,0:T(8,128)(2,1)S(1)} %get-tuple-element.37.refs_0_), channel_id=1, source_target_pairs={{0,1},{1,2},{2,3},{3,0},{4,5},{5,6},{6,7},{7,4},{8,9},{9,10},{10,1... | collective-permute-start | bytes 516104 | tf_op jit(solution)/shard_map/ppermute | solution.py:324
  95.6 10.3 %collective-permute-start.23 = (bf16[32,2688]{1,0:T(8,128)(2,1)S(1)}, bf16[32,2688]{1,0:T(8,128)(2,1)S(1)}, u32[]{:S(2)}, u32[]{:S(2)}) collective-permute-start(bf16[32,2688]{1,0:T(8,128)(2,1)S(1)} %get-tuple-element.36.refs_1_), channel_id=1, source_target_pairs={{0,1},{1,2},{2,3},{3,0},{4,5},{5,6},{6,7},{7,4},{8,9},{9,10},{10,1... | collective-permute-start | bytes 516104 | tf_op jit(solution)/shard_map/ppermute | solution.py:326
  95.6 10.3 %collective-permute-start.18 = (bf16[32,2688]{1,0:T(8,128)(2,1)S(1)}, bf16[32,2688]{1,0:T(8,128)(2,1)S(1)}, u32[]{:S(2)}, u32[]{:S(2)}) collective-permute-start(bf16[32,2688]{1,0:T(8,128)(2,1)S(1)} %get-tuple-element.37.refs_0_), channel_id=1, source_target_pairs={{0,3},{1,0},{2,1},{3,2},{4,7},{5,4},{6,5},{7,6},{8,11},{9,8},{10,9... | collective-permute-start | bytes 516104 | tf_op jit(solution)/shard_map/ppermute | solution.py:327
  122.2 39.0 %all-to-all-start.3 = ((bf16[32,40,512]{2,1,0:T(8,128)(2,1)}), bf16[32,40,512]{2,1,0:T(8,128)(2,1)S(1)}, u32[]{:S(2)}, u32[]{:S(2)}) async-start(bf16[32,40,512]{2,1,0:T(8,128)(2,1)} %bitcast.25), calls=%async_computation.3 | async-start | bytes 2621440 | tf_op jit(solution)/shard_map/all_to_all | solution.py:332
  129.6 8.5 %collective-permute-start.8 = (bf16[32,2688]{1,0:T(8,128)(2,1)S(1)}, bf16[32,2688]{1,0:T(8,128)(2,1)S(1)}, u32[]{:S(2)}, u32[]{:S(2)}) collective-permute-start(bf16[32,2688]{1,0:T(8,128)(2,1)S(1)} %get-tuple-element.40.refs_0_), channel_id=1, source_target_pairs={{0,1},{1,2},{2,3},{3,0},{4,5},{5,6},{6,7},{7,4},{8,9},{9,10},{10,1... | collective-permute-start | bytes 516104 | tf_op jit(solution)/shard_map/ppermute | solution.py:324
  129.7 8.4 %collective-permute-start.7 = (bf16[32,2688]{1,0:T(8,128)(2,1)S(1)}, bf16[32,2688]{1,0:T(8,128)(2,1)S(1)}, u32[]{:S(2)}, u32[]{:S(2)}) collective-permute-start(bf16[32,2688]{1,0:T(8,128)(2,1)S(1)} %get-tuple-element.41.refs_1_), channel_id=1, source_target_pairs={{0,3},{1,0},{2,1},{3,2},{4,7},{5,4},{6,5},{7,6},{8,11},{9,8},{10,9... | collective-permute-start | bytes 516104 | tf_op jit(solution)/shard_map/ppermute | solution.py:325
  132.9 8.5 %collective-permute-start.6 = (bf16[32,2688]{1,0:T(8,128)(2,1)S(1)}, bf16[32,2688]{1,0:T(8,128)(2,1)S(1)}, u32[]{:S(2)}, u32[]{:S(2)}) collective-permute-start(bf16[32,2688]{1,0:T(8,128)(2,1)S(1)} %get-tuple-element.40.refs_0_), channel_id=1, source_target_pairs={{0,3},{1,0},{2,1},{3,2},{4,7},{5,4},{6,5},{7,6},{8,11},{9,8},{10,9... | collective-permute-start | bytes 516104 | tf_op jit(solution)/shard_map/ppermute | solution.py:327
  133.0 8.5 %collective-permute-start.11 = (bf16[32,2688]{1,0:T(8,128)(2,1)S(1)}, bf16[32,2688]{1,0:T(8,128)(2,1)S(1)}, u32[]{:S(2)}, u32[]{:S(2)}) collective-permute-start(bf16[32,2688]{1,0:T(8,128)(2,1)S(1)} %get-tuple-element.41.refs_1_), channel_id=1, source_target_pairs={{0,1},{1,2},{2,3},{3,0},{4,5},{5,6},{6,7},{7,4},{8,9},{9,10},{10,1... | collective-permute-start | bytes 516104 | tf_op jit(solution)/shard_map/ppermute | solution.py:326
  138.1 6.7 %collective-permute-start.9 = (bf16[32,2688]{1,0:T(8,128)(2,1)S(1)}, bf16[32,2688]{1,0:T(8,128)(2,1)S(1)}, u32[]{:S(2)}, u32[]{:S(2)}) collective-permute-start(bf16[32,2688]{1,0:T(8,128)(2,1)S(1)} %collective-permute-done.8.refs_6_), channel_id=1, source_target_pairs={{0,1},{1,2},{2,3},{3,0},{4,5},{5,6},{6,7},{7,4},{8,9},{9,10},{10,1... | collective-permute-start | bytes 516104 | tf_op jit(solution)/shard_map/ppermute | solution.py:328
  138.1 6.7 %collective-permute-start.10 = (bf16[32,2688]{1,0:T(8,128)(2,1)S(1)}, bf16[32,2688]{1,0:T(8,128)(2,1)S(1)}, u32[]{:S(2)}, u32[]{:S(2)}) collective-permute-start(bf16[32,2688]{1,0:T(8,128)(2,1)S(1)} %collective-permute-done.7.refs_3_), channel_id=1, source_target_pairs={{0,3},{1,0},{2,1},{3,2},{4,7},{5,4},{6,5},{7,6},{8,11},{9,8},{10,9... | collective-permute-start | bytes 516104 | tf_op jit(solution)/shard_map/ppermute | solution.py:329
  161.2 28.2 %all-to-all-start.1 = ((bf16[32,40,512]{2,1,0:T(8,128)(2,1)}), bf16[32,40,512]{2,1,0:T(8,128)(2,1)S(1)}, u32[]{:S(2)}, u32[]{:S(2)}) async-start(bf16[32,40,512]{2,1,0:T(8,128)(2,1)} %bitcast.26), calls=%async_computation.1 | async-start | bytes 2621440 | tf_op jit(solution)/shard_map/all_to_all | solution.py:332
  (26 other events, 282.7 us)

commit v2 on v0

v2 whole, which is shorter than its diff:
```python
import functools

import jax
import jax.numpy as jnp
from jax import lax
from jax.experimental import pallas as pl
from jax.experimental.pallas import tpu as pltpu
from jax.sharding import PartitionSpec as P

LMAX = 2559
TILE = 128
SURE = (11, 5)
SHARED = 5
KEPT = SURE[0] + SHARED + SURE[1]
BLOCK = 512
BF16 = jnp.bfloat16
F32 = jnp.float32
LIMIT = 32 * 1024 * 1024
IN_VMEM = pl.BlockSpec(memory_space=pltpu.VMEM)
IN_SMEM = pl.BlockSpec(memory_space=pltpu.SMEM)
IN_PLACE = pl.BlockSpec(memory_space=pl.ANY)
NN = ((1,), (0,))
TN = ((0,), (0,))
NT = ((1,), (1,))


def dot(a, b, dims):
    return lax.dot_general(a, b, (dims, ((), ())), preferred_element_type=F32)


def call(kernel, name, **kwargs):
    return pl.pallas_call(
        kernel, name=name, compiler_params=pltpu.CompilerParams(vmem_limit_bytes=LIMIT), **kwargs)


def one_hot(index):
    size = index.shape[0]
    return jnp.where(index == lax.broadcasted_iota(jnp.int32, (size, size), 1), 1.0, 0.0).astype(BF16)


def pack_kernel(wind_ref, out_ref, wide_ref, order8, order4):
    rows, slots, lanes = wind_ref.shape

    @pl.when(pl.program_id(0) == 0)
    def _():
        for count, order in ((8, order8), (4, order4)):
            i = lax.broadcasted_iota(jnp.int32, order.shape, 0)
            order[...] = one_hot((i % count) * slots + (i // (2 * count)) * 2 + (i // count) % 2)

    for start in (0, 8, 16):
        count, order = (8, order8) if start < 16 else (4, order4)
        block = wind_ref[start:start + count].reshape(count * slots, lanes)
        moved = dot(order[...], block, NN).reshape(slots // 2, 2 * count, lanes)
        if start < 16:
            wide_ref[:, start:start + 8] = moved[:, :8]
            wide_ref[:, 16 + start:24 + start] = moved[:, 8:]
        else:
            wide_ref[:, 32:] = moved
    out_ref[...] = wide_ref[...].astype(BF16)


def pack(wind):
    rows, slots, width = wind.shape
    lanes = width // 2
    block = (slots // 2, rows * 2, lanes)
    return call(
        pack_kernel,
        "pack",
        grid=(2,),
        out_shape=pltpu.HBM((slots // 2, rows * 2, width), BF16),
        in_specs=[pl.BlockSpec((rows, slots, lanes), lambda i: (0, 0, i))],
        out_specs=pl.BlockSpec(block, lambda i: (0, 0, i)),
        scratch_shapes=[
            pltpu.VMEM(block, F32),
            pltpu.VMEM((8 * slots, 8 * slots), BF16),
            pltpu.VMEM((4 * slots, 4 * slots), BF16),
        ],
    )(*in_hbm(wind))


def unpack_kernel(rot_in, div_in, rot_out, div_out, wide_ref, order8, order4):
    rows, slots, lanes = rot_out.shape

    @pl.when(pl.program_id(0) == 0)
    def _():
        for count, order in ((8, order8), (4, order4)):
            i = lax.broadcasted_iota(jnp.int32, order.shape, 0)
            slot = i % slots
            order[...] = one_hot((slot // 2) * (2 * count) + (slot % 2) * count + i // slots)

    for ref, out in ((rot_in, rot_out), (div_in, div_out)):
        wide_ref[...] = ref[...].astype(F32)
        for start in (0, 8, 16):
            if start < 16:
                block = jnp.concatenate([wide_ref[:, start:start + 8], wide_ref[:, 16 + start:24 + start]], axis=1)
                count, order = 8, order8
            else:
                block = wide_ref[:, 32:]
                count, order = 4, order4
            moved = dot(order[...], block.reshape(count * slots, lanes).astype(BF16), NN)
            out[start:start + count] = moved.reshape(count, slots, lanes).astype(BF16)


def unpack(payload, rows):
    pairs, both, width = payload.shape
    lanes = width // 8
    slots = pairs * 2
    shape = jax.ShapeDtypeStruct((rows, slots, width // 2), BF16)

    def column(i):
        return jnp.where(i == 0, 0, jnp.where(i == 3, 1, i + 3))

    out_spec = pl.BlockSpec((rows, slots, lanes), lambda i: (0, 0, i))
    return call(
        unpack_kernel,
        "unpack",
        grid=(4,),
        out_shape=(shape, shape),
        in_specs=[
            pl.BlockSpec((pairs, both, lanes), lambda i: (0, 0, column(i))),
            pl.BlockSpec((pairs, both, lanes), lambda i: (0, 0, column(i) + 2)),
        ],
        out_specs=(out_spec, out_spec),
        scratch_shapes=[
            pltpu.VMEM((pairs, both, lanes), F32),
            pltpu.VMEM((8 * slots, 8 * slots), BF16),
            pltpu.VMEM((4 * slots, 4 * slots), BF16),
        ],
    )(payload, payload)


def in_hbm(*arrays):
    return [pltpu.with_memory_space_constraint(x, pltpu.HBM) for x in arrays]


def keep_kernel(meta, p_ref, h_ref, out_ref, sems):
    quarter, degrees = p_ref.shape[1:]
    pieces = [(0, degrees - SURE[0] * TILE, SURE[0], 0)]
    for k in range(SHARED):
        pieces.append((meta[k], pl.multiple_of(meta[SHARED + k] * TILE, TILE), 1, SURE[0] + k))
    pieces.append((1, degrees - SURE[1] * TILE, SURE[1], SURE[0] + SHARED))
    copies = []
    for slot, source, count, target in pieces:
        for at, ref in enumerate((p_ref, h_ref)):
            copies.append(pltpu.make_async_copy(
                ref.at[slot, :, pl.ds(source, count * TILE)],
                out_ref.at[pl.ds(at * quarter, quarter), pl.ds(target * TILE, count * TILE)],
                sems.at[len(copies)],
            ))
            copies[-1].start()
    for copy in copies:
        copy.wait()


def keep(meta, p_table, h_table):
    shape = (2 * p_table.shape[1], KEPT * TILE)
    return call(
        keep_kernel,
        "keep",
        out_shape=pltpu.VMEM(shape, BF16),
        in_specs=[IN_SMEM] + [IN_PLACE] * 2,
        out_specs=IN_VMEM,
        scratch_shapes=[pltpu.SemaphoreType.DMA((2 * (2 + SHARED),))],
    )(meta, *in_hbm(p_table, h_table))


def forward_kernel(part, meta, rate, mask, weight, recv, select, table, keep, send, wide, wind, spec):
    owners, both, width = wide.shape
    quarter = select.shape[2]
    levels = width // 2
    main = owners * 16
    for n, at in enumerate((part, 3 - part)):
        wide[:, :, n * levels:(n + 1) * levels] = recv[:, :, at * levels:(at + 1) * levels].astype(F32)
    mixed = wide[:, 32:].reshape(owners * 8, width).astype(BF16)
    for slot in range(2):
        rows = wide[:, 16 * slot:16 * slot + 16].reshape(main, width).astype(BF16)
        by_lat = dot(rows, select[slot, :main], TN) + dot(mixed, select[slot, main:], TN)
        wind[slot] = (by_lat * weight[...]).astype(BF16)
    split = (SURE[0] + SHARED) * TILE
    for slot in range(2):
        low, high = (0, split) if slot == 0 else (SURE[0] * TILE, KEPT * TILE)
        r = rate[slot]
        w = wind[slot]
        for start in range(low, high, BLOCK):
            cols = slice(start, min(start + BLOCK, high))
            proj_p = dot(w, table[:quarter, cols], NN)
            proj_h = dot(w, table[quarter:, cols], NN)
            psi = proj_h[:levels] - r * proj_p[levels:]
            chi = r * proj_p[:levels] - proj_h[levels:]
            if slot == 1 and start < split:
                first = mask[:, cols] > 0.5
                psi = jnp.where(first, spec[:levels, cols], psi)
                chi = jnp.where(first, spec[levels:, cols], chi)
            spec[:levels, cols] = psi
            spec[levels:, cols] = chi
    mine = meta[2 * SHARED] * levels
    keep[...] = spec[pl.ds(pl.multiple_of(mine, levels), levels), :]
    send[...] = spec[pl.ds(pl.multiple_of(levels - mine, levels), levels), :].astype(BF16)


def forward(part, meta, rate, mask, weight, recv, select, table):
    owners, both, width = recv.shape
    levels = width // 4
    quarter = select.shape[2]
    degrees = table.shape[1]
    return call(
        functools.partial(forward_kernel, part),
        "forward",
        in_specs=[IN_SMEM] * 2 + [IN_VMEM] * 5,
        out_specs=[IN_VMEM] * 2,
        out_shape=[jax.ShapeDtypeStruct((levels, degrees), F32), jax.ShapeDtypeStruct((levels, degrees), BF16)],
        scratch_shapes=[
            pltpu.VMEM((owners, both, 2 * levels), F32),
            pltpu.VMEM((2, 2 * levels, quarter), BF16),
            pltpu.VMEM((2 * levels, degrees), F32),
        ],
    )(meta, rate, mask, weight, recv, select, table)


def backward_kernel(part, meta, rate, mask, mine, theirs, select, table, *refs):
    out_ref, every, masked, winds, wide, out, sem = refs[-7:]
    levels = mine.shape[0]
    quarter = select.shape[2]
    owners, both, width = out.shape
    main = owners * 16
    split = (SURE[0] + SHARED) * TILE
    degrees = KEPT * TILE
    at = meta[2 * SHARED] * levels
    every[pl.ds(pl.multiple_of(at, levels), levels), :] = mine[...]
    every[pl.ds(pl.multiple_of(levels - at, levels), levels), :] = theirs[...]
    shared = slice(SURE[0] * TILE, split)
    first = mask[:, shared] > 0.5
    both_slots = every[:, shared].astype(F32)
    masked[0, :, :shared.start] = every[:, :shared.start]
    masked[0, :, shared] = jnp.where(first, both_slots, 0.0).astype(BF16)
    masked[1, :, :split - shared.start] = jnp.where(first, 0.0, both_slots).astype(BF16)
    masked[1, :, split - shared.start:degrees - shared.start] = every[:, split:]
    for slot in range(2):
        low, high = (0, split) if slot == 0 else (shared.start, degrees)
        pot = masked[slot, :, :high - low]
        sums = [dot(table[n * quarter:(n + 1) * quarter, low:high], pot, NT) for n in range(2)]
        r = rate[slot]
        winds[slot, :, :levels] = (-sums[1][:, :levels]).astype(BF16)
        winds[slot, :, levels:2 * levels] = (r * sums[0][:, :levels]).astype(BF16)
        winds[slot, :, 2 * levels:3 * levels] = (-r * sums[0][:, levels:]).astype(BF16)
        winds[slot, :, 3 * levels:] = sums[1][:, levels:].astype(BF16)
    for slot in range(2):
        moved = dot(select[slot, :main], winds[slot], NN)
        wide[:, 16 * slot:16 * slot + 16] = moved.reshape(owners, 16, width)
    mixed = dot(select[0, main:], winds[0], NN) + dot(select[1, main:], winds[1], NN)
    wide[:, 32:] = mixed.reshape(owners, 8, width)
    out[...] = wide[...].astype(BF16)
    copy = pltpu.make_async_copy(out, out_ref.at[:, :, pl.ds(part * width, width)], sem)
    copy.start()
    copy.wait()


def backward(part, meta, rate, mask, mine, theirs, select, table, payload, filled=()):
    quarter = select.shape[2]
    levels, degrees = mine.shape
    owners, both, width = payload
    piece = (owners, both, width // 2)
    return call(
        functools.partial(backward_kernel, part),
        "backward",
        in_specs=[IN_SMEM] * 2 + [IN_VMEM] * 5 + [IN_PLACE] * len(filled),
        out_specs=IN_PLACE,
        out_shape=pltpu.HBM(payload, BF16),
        input_output_aliases={7: 0} if filled else {},
        scratch_shapes=[
            pltpu.VMEM((2 * levels, degrees), BF16),
            pltpu.VMEM((2, 2 * levels, (SURE[0] + SHARED) * TILE), BF16),
            pltpu.VMEM((2, quarter, width // 2), BF16),
            pltpu.VMEM(piece, F32),
            pltpu.VMEM(piece, BF16),
            pltpu.SemaphoreType.DMA,
        ],
    )(meta, rate, mask, mine, theirs, select, table, *filled)


def add_kernel(kept, got, total, sent):
    total[...] = kept[...] + got[...].astype(F32)
    sent[...] = total[...].astype(BF16)


def add(kept, got):
    return call(
        add_kernel,
        "add",
        in_specs=[IN_VMEM] * 2,
        out_specs=[IN_VMEM] * 2,
        out_shape=[jax.ShapeDtypeStruct(kept.shape, F32), jax.ShapeDtypeStruct(kept.shape, BF16)],
    )(kept, got)


def scale_kernel(kept, got, factor, mine):
    mine[...] = ((kept[...] + got[...].astype(F32)) * factor[...]).astype(BF16)


def scale(kept, got, factor):
    return call(
        scale_kernel,
        "scale",
        in_specs=[IN_VMEM] * 3,
        out_specs=IN_VMEM,
        out_shape=jax.ShapeDtypeStruct(kept.shape, BF16),
    )(kept, got, factor)


def on_device(fourier_wind, quad_weight, p_table, h_table, wavenumbers, row_latitude):
    owners = lax.axis_size("ma")
    groups = lax.axis_size("oct")
    me = lax.axis_index("oct")
    rows = fourier_wind.shape[0]
    quarter = p_table.shape[1]
    count = p_table.shape[2] // TILE
    flip, turn = [z ^ 1 for z in range(groups)], [groups - 1 - z for z in range(groups)]
    first = [
        (d * groups + z, d * groups + (flip, turn)[d % 2][z]) for d in range(owners) for z in range(groups)]
    second = [
        (d * groups + z, d * groups + (turn, flip)[d % 2][z]) for d in range(owners) for z in range(groups)]
    half = jnp.where(lax.axis_index("ma") % 2 == 0, ((me + 1) // 2) % 2, me // 2)

    def swap(x, pairs):
        return lax.ppermute(x, ("ma", "oct"), pairs)

    received = lax.all_to_all(pack(fourier_wind), "ma", 0, 0, tiled=True)

    n_first = count - wavenumbers[0] // TILE - SURE[0]
    k = jnp.arange(SHARED)
    shared_slot = (k >= n_first).astype(jnp.int32)
    shared_tile = jnp.where(k < n_first, count - SURE[0] - 1 - k, count - SURE[1] - 1 - (k - n_first))
    meta = jnp.concatenate([shared_slot, shared_tile, half[None]]).astype(jnp.int32)
    slot = jnp.concatenate([jnp.zeros(SURE[0], jnp.int32), shared_slot, jnp.ones(SURE[1], jnp.int32)])
    tile = jnp.concatenate([jnp.arange(count - SURE[0], count), shared_tile, jnp.arange(count - SURE[1], count)])
    mask = jnp.repeat(1.0 - slot.astype(F32), TILE)[None, :]
    degree = (tile[:, None] * TILE + jnp.arange(TILE)[None, :]).astype(F32)
    limit = jnp.where(slot == 0, wavenumbers[0], wavenumbers[1]).astype(F32)[:, None]
    factor = jnp.where(
        degree >= limit, -(LMAX * LMAX * 1.0) / jnp.maximum(degree * (degree + 1.0), 1.0), 0.0).reshape(1, -1)
    rate = wavenumbers.astype(F32) / LMAX

    local = lax.dynamic_index_in_dim(row_latitude.reshape(owners, groups, rows), me, 1, keepdims=False) - me * quarter
    none = jnp.full((owners, 4), -1, jnp.int32)
    main, last = local[:, :16].reshape(-1), local[:, 16:]
    target = jnp.stack([
        jnp.concatenate([main, jnp.concatenate([last, none], axis=1).reshape(-1)]),
        jnp.concatenate([main, jnp.concatenate([none, last], axis=1).reshape(-1)]),
    ])
    select = (target[:, :, None] == jnp.arange(quarter)[None, None, :]).astype(BF16)
    weight = quad_weight.reshape(1, -1)

    table = pltpu.with_memory_space_constraint(keep(meta, p_table, h_table), pltpu.VMEM)
    owners, both, width = received.shape
    payload = (owners, both, 2 * width)
    signs = (rate, -rate)
    mines, theirs = [], []
    for n in range(2):
        kept, sent = forward(n, meta, signs[n], mask, weight, received, select, table)
        kept, sent = add(kept, swap(sent, first))
        mines.append(scale(kept, swap(sent, second), factor))
        theirs.append(swap(mines[n], first))
    filled = ()
    for n in range(2):
        filled = (backward(n, meta, signs[n], mask, mines[n], theirs[n], select, table, payload, filled),)
    return tuple(unpack(lax.all_to_all(filled[0], "ma", 0, 0, tiled=True), rows))


def solution(mesh):
    placed = (
        P(("ma", "oct"), None, None),
        P("oct"),
        P("ma", "oct", None),
        P("ma", "oct", None),
        P("ma"),
        P(),
    )
    return jax.shard_map(
        on_device,
        mesh=mesh,
        in_specs=placed,
        out_specs=(P(("ma", "oct"), None, None), P(("ma", "oct"), None, None)),
        check_vma=False,
    )
```

time: 374 us -> 145 us (0.39)
  waiting for transfers between devices: 236 us -> 41.3 us
  local copies, waits for them, and re-layouts: 59.1 us -> 7.16 us
  blocking collectives: 0 us -> 38.3 us
  matrix products: 34.8 us -> 0 us
  Pallas kernels: 0 us -> 31.9 us
  between operations: 14.3 us -> 3.38 us
  other arithmetic: 10.6 us -> 2.17 us
    psum x1 -> x0, waiting for transfers between devices: 192 us -> none  [on_device(): total = lax.psum(spectra, 'oct')]
    all_to_all x0 -> x1, blocking collectives: none -> 38.3 us  [on_device(): lax.all_to_all(filled[0], 'ma', 0, 0, tiled=True)]
    dot_general x4 -> x0, matrix products: 34.8 us -> none  [the longest x1 9.98 us: on_device(): jnp.einsum('sjl,jsx->slx', h_table, weighted, preferred_element_type=jnp....]
    all_to_all x3 -> x1, waiting for transfers between devices: 44 us -> 9.73 us  [on_device(): received = lax.all_to_all(pack(fourier_wind), 'ma', 0, 0, tiled=True)]
    pallas_call x0 -> x11, Pallas kernels: none -> 31.9 us  [the longest x2 11 us: backward(): call(functools.partial(backward_kernel, part), 'backward', in_specs=[IN_S...]
    ppermute x0 -> x6, waiting for transfers between devices: none -> 31.6 us  [swap(): return lax.ppermute(x, ('ma', 'oct'), pairs)]
    gather x3 -> x0, local copies, waits for them, and re-layouts: 20 us -> none  [the longest x1 8.06 us: on_device(): rot.reshape(quarter, slots, 4 * levels).astype(jnp.bfloat16)[local_lat]]
    scatter x1 -> x0, local copies, waits for them, and re-layouts: 19.4 us -> none  [on_device(): jnp.zeros((quarter,) + received.shape[1:], received.dtype).at[local_lat]]
  transfers between devices with their start and end apart: 4 -> 7, of which waited for: 4 -> 5; matrix products, arithmetic and copies ran while one was open for 5% -> 2% of each run, Pallas kernels for 0% -> 10%
where the time goes in v2:
time: 145 us; the launch traced here: 144 us
  waiting for transfers between devices  41.3 us (28%)
  blocking collectives  38.3 us (26%)
  Pallas kernels  31.9 us (22%)
  starting transfers between devices  19.4 us (13%)
  local copies, waits for them, and re-layouts  7.16 us (5%)
  between operations  3.38 us (2%)
  other arithmetic  2.17 us (1%)
    all_to_all x1, blocking collectives, on_device(): lax.all_to_all(filled[0], 'ma', 0, 0, tiled=True)  38.3 us
    ppermute x6, waiting for transfers between devices, swap(): return lax.ppermute(x, ('ma', 'oct'), pairs)  31.6 us
    ppermute x6, starting transfers between devices, swap(): return lax.ppermute(x, ('ma', 'oct'), pairs)  11.8 us
    pallas_call x2, Pallas kernels, backward(): call(functools.partial(backward_kernel, part), 'backward', in_specs=[IN_S...  11 us
    all_to_all x1, waiting for transfers between devices, on_device(): received = lax.all_to_all(pack(fourier_wind), 'ma', 0, 0, tiled=True)  9.73 us
    pallas_call x2, Pallas kernels, forward(): call(functools.partial(forward_kernel, part), 'forward', in_specs=[IN_SME...  8.37 us
    all_to_all x1, starting transfers between devices, on_device(): received = lax.all_to_all(pack(fourier_wind), 'ma', 0, 0, tiled=True)  7.54 us
    unnamed x17, local copies, waits for them, and re-layouts  5.97 us
  transfers between devices with their start and end apart: 7, of which 5 were waited for; matrix products, arithmetic and copies ran while one was open for 2% of the time, Pallas kernels for 10%

profile of v2, /device:TPU:0, one launch (start us, length us, event | category | flops | bytes accessed | tf_op | source)
XLA Modules:
  0.0 143.5 jit_solution(3369178259501625324)
XLA Ops:
  0.6 3.2 %pack.1 = bf16[32,40,512]{2,1,0:T(8,128)(2,1)} custom-call(bf16[20,64,512]{2,1,0:T(8,128)(2,1)} %wind_ref.1), custom_call_target="tpu_custom_call" | custom-call | tf_op jit(solution)/shard_map/pack/pallas_call | solution.py:66
  3.8 7.5 %all-to-all-start = ((bf16[32,40,512]{2,1,0:T(8,128)(2,1)}), bf16[32,40,512]{2,1,0:T(8,128)(2,1)S(1)}, u32[]{:S(2)}, u32[]{:S(2)}) async-start(bf16[32,40,512]{2,1,0:T(8,128)(2,1)} %pack.1), calls=%async_computation | async-start | bytes 2621440 | tf_op jit(solution)/shard_map/all_to_all | solution.py:327
  11.4 0.7 fusion.5
  15.4 3.7 %keep.1.table = bf16[1280,2688]{1,0:T(8,128)(2,1)S(1)} custom-call(s32[11]{0:T(128)S(1)} %pad_add_fusion.3.meta, bf16[2,640,2560]{2,1,0:T(8,128)(2,1)} %p_ref.1, bf16[2,640,2560]{2,1,0:T(8,128)(2,1)} %h_ref.1), custom_call_target="tpu_custom_call" | custom-call | tf_op jit(solution)/shard_map/keep/pallas_call | solution.py:157
  19.1 2.8 %copy-done = bf16[1280,2688]{1,0:T(8,128)(2,1)} copy-done((bf16[1280,2688]{1,0:T(8,128)(2,1)}, bf16[1280,2688]{1,0:T(8,128)(2,1)S(1)}, u32[]{:S(2)}) %copy-start) | copy-done | bytes 6881304
  22.0 0.4 fusion.select
  22.4 9.7 %all-to-all-done.recv = bf16[32,40,512]{2,1,0:T(8,128)(2,1)S(1)} async-done(((bf16[32,40,512]{2,1,0:T(8,128)(2,1)}), bf16[32,40,512]{2,1,0:T(8,128)(2,1)S(1)}, u32[]{:S(2)}, u32[]{:S(2)}) %all-to-all-start) | async-done | bytes 1310752 | tf_op jit(solution)/shard_map/all_to_all | solution.py:327
  32.1 3.0 %copy-done.1 = bf16[1280,2688]{1,0:T(8,128)(2,1)S(1)} copy-done((bf16[1280,2688]{1,0:T(8,128)(2,1)S(1)}, bf16[1280,2688]{1,0:T(8,128)(2,1)}, u32[]{:S(2)}) %copy-start.1) | copy-done | bytes 6881304
  35.1 4.2 %forward.3 = (f32[128,2688]{1,0:T(8,128)S(1)}, bf16[128,2688]{1,0:T(8,128)(2,1)S(1)}) custom-call(s32[11]{0:T(128)S(1)} %pad_add_fusion.3.meta, f32[2]{0:T(128)S(1)} %get-tuple-element.22.rate, f32[1,2688]{1,0:T(1,128)S(1)} %bitcast.23, f32[1,640]{1,0:T(1,128)S(1)} %reshape.113.weight, bf16[32,40,512]{2,1,0:T(8,128)(2,1)S(1)} %all-to-all-done.recv, ...), custom_call_target="tpu_custom_call" | custom-call | tf_op jit(solution)/shard_map/forward/pallas_call | solution.py:206
  39.3 2.0 %collective-permute-start.3 = (bf16[128,2688]{1,0:T(8,128)(2,1)S(1)}, bf16[128,2688]{1,0:T(8,128)(2,1)S(1)}, u32[]{:S(2)}, u32[]{:S(2)}) collective-permute-start(bf16[128,2688]{1,0:T(8,128)(2,1)S(1)} %get-tuple-element.15), channel_id=1, source_target_pairs={{0,1},{1,0},{2,3},{3,2},{4,7},{5,6},{6,5},{7,4},{8,9},{9,8},{10,11... | collective-permute-start | bytes 2064392 | tf_op jit(solution)/shard_map/ppermute | solution.py:325
  41.3 4.2 %forward.2 = (f32[128,2688]{1,0:T(8,128)S(1)}, bf16[128,2688]{1,0:T(8,128)(2,1)S(1)}) custom-call(s32[11]{0:T(128)S(1)} %pad_add_fusion.3.meta, f32[2]{0:T(128)S(1)} %get-tuple-element.23.rate, f32[1,2688]{1,0:T(1,128)S(1)} %bitcast.24, f32[1,640]{1,0:T(1,128)S(1)} %reshape.113.weight, bf16[32,40,512]{2,1,0:T(8,128)(2,1)S(1)} %all-to-all-done.recv, ...), custom_call_target="tpu_custom_call" | custom-call | tf_op jit(solution)/shard_map/forward/pallas_call | solution.py:206
  45.7 1.4 fusion.2
  47.2 3.1 %collective-permute-done.3.got = bf16[128,2688]{1,0:T(8,128)(2,1)S(1)} collective-permute-done((bf16[128,2688]{1,0:T(8,128)(2,1)S(1)}, bf16[128,2688]{1,0:T(8,128)(2,1)S(1)}, u32[]{:S(2)}, u32[]{:S(2)}) %collective-permute-start.3) | collective-permute-done | bytes 688160 | tf_op jit(solution)/shard_map/ppermute | solution.py:325
  50.3 0.2 add.113
  50.5 4.1 %collective-permute-start.4 = (bf16[128,2688]{1,0:T(8,128)(2,1)S(1)}, bf16[128,2688]{1,0:T(8,128)(2,1)S(1)}, u32[]{:S(2)}, u32[]{:S(2)}) collective-permute-start(bf16[128,2688]{1,0:T(8,128)(2,1)S(1)} %get-tuple-element.17), channel_id=1, source_target_pairs={{0,3},{1,2},{2,1},{3,0},{4,5},{5,4},{6,7},{7,6},{8,11},{9,10},{10,... | collective-permute-start | bytes 2064392 | tf_op jit(solution)/shard_map/ppermute | solution.py:325
  54.7 8.8 %collective-permute-done.got = bf16[128,2688]{1,0:T(8,128)(2,1)S(1)} collective-permute-done((bf16[128,2688]{1,0:T(8,128)(2,1)S(1)}, bf16[128,2688]{1,0:T(8,128)(2,1)S(1)}, u32[]{:S(2)}, u32[]{:S(2)}) %collective-permute-start) | collective-permute-done | bytes 688160 | tf_op jit(solution)/shard_map/ppermute | solution.py:325
  63.7 4.2 %collective-permute-start.1 = (bf16[128,2688]{1,0:T(8,128)(2,1)S(1)}, bf16[128,2688]{1,0:T(8,128)(2,1)S(1)}, u32[]{:S(2)}, u32[]{:S(2)}) collective-permute-start(bf16[128,2688]{1,0:T(8,128)(2,1)S(1)} %get-tuple-element.13), channel_id=1, source_target_pairs={{0,3},{1,2},{2,1},{3,0},{4,5},{5,4},{6,7},{7,6},{8,11},{9,10},{10,... | collective-permute-start | bytes 2064392 | tf_op jit(solution)/shard_map/ppermute | solution.py:325
  68.2 15.3 %collective-permute-done.1.got = bf16[128,2688]{1,0:T(8,128)(2,1)S(1)} collective-permute-done((bf16[128,2688]{1,0:T(8,128)(2,1)S(1)}, bf16[128,2688]{1,0:T(8,128)(2,1)S(1)}, u32[]{:S(2)}, u32[]{:S(2)}) %collective-permute-start.1) | collective-permute-done | bytes 688160 | tf_op jit(solution)/shard_map/ppermute | solution.py:325
  83.7 1.3 collective-permute-start.2
  85.0 5.5 %backward.2.refs_0_ = bf16[32,40,1024]{2,1,0:T(8,128)(2,1)} custom-call(s32[11]{0:T(128)S(1)} %pad_add_fusion.3.meta, f32[2]{0:T(128)S(1)} %get-tuple-element.22.rate, f32[1,2688]{1,0:T(1,128)S(1)} %bitcast.25, bf16[128,2688]{1,0:T(8,128)(2,1)S(1)} %scale.3.mine, bf16[128,2688]{1,0:T(8,128)(2,1)S(1)} %collective-permute-done.5.theirs, ...), custom_call_target="tpu_custom_call" | custom-call | tf_op jit(solution)/shard_map/backward/pallas_call | solution.py:263
  90.5 4.4 %collective-permute-done.2.theirs = bf16[128,2688]{1,0:T(8,128)(2,1)S(1)} collective-permute-done((bf16[128,2688]{1,0:T(8,128)(2,1)S(1)}, bf16[128,2688]{1,0:T(8,128)(2,1)S(1)}, u32[]{:S(2)}, u32[]{:S(2)}) %collective-permute-start.2) | collective-permute-done | bytes 688160 | tf_op jit(solution)/shard_map/ppermute | solution.py:325
  94.9 5.5 %backward.3 = bf16[32,40,1024]{2,1,0:T(8,128)(2,1)} custom-call(s32[11]{0:T(128)S(1)} %pad_add_fusion.3.meta, f32[2]{0:T(128)S(1)} %get-tuple-element.23.rate, f32[1,2688]{1,0:T(1,128)S(1)} %bitcast.26, bf16[128,2688]{1,0:T(8,128)(2,1)S(1)} %scale.2.mine, bf16[128,2688]{1,0:T(8,128)(2,1)S(1)} %collective-permute-done.2.theirs, ...), custom_call_target="tpu_custom_call", output_to_operand_aliasing={{}: (7, {})} | custom-call | tf_op jit(solution)/shard_map/backward/pallas_call | solution.py:263
  100.4 38.3 %all_to_all.10.rot_in.div_in = bf16[32,40,1024]{2,1,0:T(8,128)(2,1)S(1)} all-to-all(bf16[32,40,1024]{2,1,0:T(8,128)(2,1)} %backward.3), channel_id=1, replica_groups=mesh['ma'=32,'oct'=4] {'ma'}, dimensions={0} | all-to-all | bytes 5242880 | tf_op jit(solution)/shard_map/all_to_all | solution.py:366
  138.7 4.9 %unpack.1 = (bf16[20,64,512]{2,1,0:T(8,128)(2,1)}, bf16[20,64,512]{2,1,0:T(8,128)(2,1)}) custom-call(bf16[32,40,1024]{2,1,0:T(8,128)(2,1)S(1)} %all_to_all.10.rot_in.div_in, bf16[32,40,1024]{2,1,0:T(8,128)(2,1)S(1)} %all_to_all.10.rot_in.div_in), custom_call_target="tpu_custom_call" | custom-call | tf_op jit(solution)/shard_map/unpack/pallas_call | solution.py:114
  (47 shorter events, 2.0 us)
Async XLA Ops:
  3.8 7.6 %copy-start.4 = (s32[2]{0:T(128)S(1)}, s32[2]{0:T(128)}, u32[]{:S(2)}) copy-start(s32[2]{0:T(128)} %param.10) | copy-start | bytes 28
  3.8 10.9 %copy-start.3 = (f32[640]{0:T(1024)S(1)}, f32[640]{0:T(1024)}, u32[]{:S(2)}) copy-start(f32[640]{0:T(1024)} %param.7) | copy-start | bytes 7684
  3.8 10.9 %copy-start.2 = (s32[2560]{0:T(1024)S(1)}, s32[2560]{0:T(1024)}, u32[]{:S(2)}) copy-start(s32[2560]{0:T(1024)} %param.11) | copy-start | bytes 30724
  3.8 28.3 %all-to-all-start = ((bf16[32,40,512]{2,1,0:T(8,128)(2,1)}), bf16[32,40,512]{2,1,0:T(8,128)(2,1)S(1)}, u32[]{:S(2)}, u32[]{:S(2)}) async-start(bf16[32,40,512]{2,1,0:T(8,128)(2,1)} %pack.1), calls=%async_computation | async-start | bytes 2621440 | tf_op jit(solution)/shard_map/all_to_all | solution.py:327
  19.1 2.8 %copy-start = (bf16[1280,2688]{1,0:T(8,128)(2,1)}, bf16[1280,2688]{1,0:T(8,128)(2,1)S(1)}, u32[]{:S(2)}) copy-start(bf16[1280,2688]{1,0:T(8,128)(2,1)S(1)} %keep.1.table) | copy-start | bytes 20643844
  32.1 3.0 %copy-start.1 = (bf16[1280,2688]{1,0:T(8,128)(2,1)S(1)}, bf16[1280,2688]{1,0:T(8,128)(2,1)}, u32[]{:S(2)}) copy-start(bf16[1280,2688]{1,0:T(8,128)(2,1)} %copy-done) | copy-start | bytes 20643844
  35.1 49.9 %slice-start = ((s8[6881280]{0:T(1024)(128)(4,1)}), s8[4194304]{0:T(1024)(128)(4,1)S(1)}, s32[]{:S(2)}) async-start(s8[6881280]{0:T(1024)(128)(4,1)} %bitcast.21), calls=%async_computation.2 | async-start | bytes 8388608
  39.3 11.0 %collective-permute-start.3 = (bf16[128,2688]{1,0:T(8,128)(2,1)S(1)}, bf16[128,2688]{1,0:T(8,128)(2,1)S(1)}, u32[]{:S(2)}, u32[]{:S(2)}) collective-permute-start(bf16[128,2688]{1,0:T(8,128)(2,1)S(1)} %get-tuple-element.15), channel_id=1, source_target_pairs={{0,1},{1,0},{2,3},{3,2},{4,7},{5,6},{6,5},{7,4},{8,9},{9,8},{10,11... | collective-permute-start | bytes 2064392 | tf_op jit(solution)/shard_map/ppermute | solution.py:325
  41.3 43.7 %slice-start.1 = ((s8[6881280]{0:T(1024)(128)(4,1)}), s8[2686976]{0:T(1024)(128)(4,1)S(1)}, s32[]{:S(2)}) async-start(s8[6881280]{0:T(1024)(128)(4,1)} %bitcast.21), calls=%async_computation.3 | async-start | bytes 5373952
  45.5 17.9 %collective-permute-start = (bf16[128,2688]{1,0:T(8,128)(2,1)S(1)}, bf16[128,2688]{1,0:T(8,128)(2,1)S(1)}, u32[]{:S(2)}, u32[]{:S(2)}) collective-permute-start(bf16[128,2688]{1,0:T(8,128)(2,1)S(1)} %get-tuple-element.11), channel_id=1, source_target_pairs={{0,1},{1,0},{2,3},{3,2},{4,7},{5,6},{6,5},{7,4},{8,9},{9,8},{10,11... | collective-permute-start | bytes 2064392 | tf_op jit(solution)/shard_map/ppermute | solution.py:325
  50.5 17.4 %collective-permute-start.4 = (bf16[128,2688]{1,0:T(8,128)(2,1)S(1)}, bf16[128,2688]{1,0:T(8,128)(2,1)S(1)}, u32[]{:S(2)}, u32[]{:S(2)}) collective-permute-start(bf16[128,2688]{1,0:T(8,128)(2,1)S(1)} %get-tuple-element.17), channel_id=1, source_target_pairs={{0,3},{1,2},{2,1},{3,0},{4,5},{5,4},{6,7},{7,6},{8,11},{9,10},{10,... | collective-permute-start | bytes 2064392 | tf_op jit(solution)/shard_map/ppermute | solution.py:325
  63.7 19.8 %collective-permute-start.1 = (bf16[128,2688]{1,0:T(8,128)(2,1)S(1)}, bf16[128,2688]{1,0:T(8,128)(2,1)S(1)}, u32[]{:S(2)}, u32[]{:S(2)}) collective-permute-start(bf16[128,2688]{1,0:T(8,128)(2,1)S(1)} %get-tuple-element.13), channel_id=1, source_target_pairs={{0,3},{1,2},{2,1},{3,0},{4,5},{5,4},{6,7},{7,6},{8,11},{9,10},{10,... | collective-permute-start | bytes 2064392 | tf_op jit(solution)/shard_map/ppermute | solution.py:325
  68.1 16.8 %collective-permute-start.5 = (bf16[128,2688]{1,0:T(8,128)(2,1)S(1)}, bf16[128,2688]{1,0:T(8,128)(2,1)S(1)}, u32[]{:S(2)}, u32[]{:S(2)}) collective-permute-start(bf16[128,2688]{1,0:T(8,128)(2,1)S(1)} %scale.3.mine), channel_id=1, source_target_pairs={{0,1},{1,0},{2,3},{3,2},{4,7},{5,6},{6,5},{7,4},{8,9},{9,8},{10,11... | collective-permute-start | bytes 2064392 | tf_op jit(solution)/shard_map/ppermute | solution.py:325
  83.7 11.2 %collective-permute-start.2 = (bf16[128,2688]{1,0:T(8,128)(2,1)S(1)}, bf16[128,2688]{1,0:T(8,128)(2,1)S(1)}, u32[]{:S(2)}, u32[]{:S(2)}) collective-permute-start(bf16[128,2688]{1,0:T(8,128)(2,1)S(1)} %scale.2.mine), channel_id=1, source_target_pairs={{0,1},{1,0},{2,3},{3,2},{4,7},{5,6},{6,5},{7,4},{8,9},{9,8},{10,11... | collective-permute-start | bytes 2064392 | tf_op jit(solution)/shard_map/ppermute | solution.py:325

commit v3 on v2

--- a/solution.py
+++ b/solution.py
@@ -33,122 +33,134 @@
         kernel, name=name, compiler_params=pltpu.CompilerParams(vmem_limit_bytes=LIMIT), **kwargs)
 
 
-def one_hot(index):
-    size = index.shape[0]
-    return jnp.where(index == lax.broadcasted_iota(jnp.int32, (size, size), 1), 1.0, 0.0).astype(BF16)
-
-
-def pack_kernel(wind_ref, out_ref, wide_ref, order8, order4):
+def fill_order(order, source):
+    size = order.shape[0]
+    index = source(lax.broadcasted_iota(jnp.int32, (size, 1), 0))
+    hit = index == lax.broadcasted_iota(jnp.int32, (size, size), 1)
+    order[...] = jnp.where(hit, 1.0, 0.0).astype(BF16)
+
+
+def log2(n):
+    return n.bit_length() - 1
+
+
+def pack_kernel(wind_ref, out_ref, order8, order4):
     rows, slots, lanes = wind_ref.shape
 
     @pl.when(pl.program_id(0) == 0)
     def _():
         for count, order in ((8, order8), (4, order4)):
-            i = lax.broadcasted_iota(jnp.int32, order.shape, 0)
-            order[...] = one_hot((i % count) * slots + (i // (2 * count)) * 2 + (i // count) % 2)
-
+            c = log2(count)
+            fill_order(order, lambda i: (i & (count - 1)) * slots + ((i >> (c + 1)) << 1) + ((i >> c) & 1))
+
+    eights = []
     for start in (0, 8, 16):
         count, order = (8, order8) if start < 16 else (4, order4)
         block = wind_ref[start:start + count].reshape(count * slots, lanes)
-        moved = dot(order[...], block, NN).reshape(slots // 2, 2 * count, lanes)
-        if start < 16:
-            wide_ref[:, start:start + 8] = moved[:, :8]
-            wide_ref[:, 16 + start:24 + start] = moved[:, 8:]
-        else:
-            wide_ref[:, 32:] = moved
-    out_ref[...] = wide_ref[...].astype(BF16)
+        eights.append(dot(order[...], block, NN).reshape(slots // 2, 2 * count, lanes))
+    for slot in range(2):
+        rows_of = [x[:, 8 * slot:8 * slot + 8] for x in eights[:2]]
+        out_ref[:, 16 * slot:16 * slot + 16] = jnp.concatenate(rows_of, axis=1).astype(BF16)
+    out_ref[:, 32:] = eights[2].astype(BF16)
 
 
 def pack(wind):
     rows, slots, width = wind.shape
     lanes = width // 2
-    block = (slots // 2, rows * 2, lanes)
     return call(
         pack_kernel,
         "pack",
         grid=(2,),
         out_shape=pltpu.HBM((slots // 2, rows * 2, width), BF16),
         in_specs=[pl.BlockSpec((rows, slots, lanes), lambda i: (0, 0, i))],
-        out_specs=pl.BlockSpec(block, lambda i: (0, 0, i)),
+        out_specs=pl.BlockSpec((slots // 2, rows * 2, lanes), lambda i: (0, 0, i)),
         scratch_shapes=[
-            pltpu.VMEM(block, F32),
             pltpu.VMEM((8 * slots, 8 * slots), BF16),
             pltpu.VMEM((4 * slots, 4 * slots), BF16),
         ],
     )(*in_hbm(wind))
 
 
-def unpack_kernel(rot_in, div_in, rot_out, div_out, wide_ref, order8, order4):
-    rows, slots, lanes = rot_out.shape
-
-    @pl.when(pl.program_id(0) == 0)
-    def _():
-        for count, order in ((8, order8), (4, order4)):
-            i = lax.broadcasted_iota(jnp.int32, order.shape, 0)
-            slot = i % slots
-            order[...] = one_hot((slot // 2) * (2 * count) + (slot % 2) * count + i // slots)
-
-    for ref, out in ((rot_in, rot_out), (div_in, div_out)):
-        wide_ref[...] = ref[...].astype(F32)
+def unpack_kernel(payload, rot_ref, div_ref, outs, order8, order4, sems):
+    _, rows, slots, width = outs.shape
+    lanes = width // 4
+    for count, order in ((8, order8), (4, order4)):
+        c = log2(count)
+
+        def source(i):
+            slot = i & (slots - 1)
+            return ((slot >> 1) << (c + 1)) + ((slot & 1) << c) + (i >> log2(slots))
+
+        fill_order(order, source)
+    copies = []
+    for n, component in enumerate((0, 3, 1, 2)):
+        cols = slice(2 * n * lanes, 2 * (n + 1) * lanes)
+        mains = [payload[:, 16 * slot:16 * slot + 16, cols].astype(F32) for slot in range(2)]
         for start in (0, 8, 16):
             if start < 16:
-                block = jnp.concatenate([wide_ref[:, start:start + 8], wide_ref[:, 16 + start:24 + start]], axis=1)
+                block = jnp.concatenate([x[:, start:start + 8] for x in mains], axis=1)
                 count, order = 8, order8
             else:
-                block = wide_ref[:, 32:]
+                block = payload[:, 32:, cols].astype(F32)
                 count, order = 4, order4
-            moved = dot(order[...], block.reshape(count * slots, lanes).astype(BF16), NN)
-            out[start:start + count] = moved.reshape(count, slots, lanes).astype(BF16)
+            moved = dot(order[...], block.reshape(count * slots, 2 * lanes).astype(BF16), NN)
+            moved = moved.reshape(count, slots, 2 * lanes).astype(BF16)
+            for k, ref in enumerate((rot_ref, div_ref)):
+                outs[k, start:start + count, :, component * lanes:(component + 1) * lanes] = (
+                    moved[:, :, k * lanes:(k + 1) * lanes])
+                at = (pl.ds(start, count), slice(None), pl.ds(component * lanes, lanes))
+                copies.append(pltpu.make_async_copy(outs.at[(k, *at)], ref.at[at], sems.at[len(copies)]))
+                copies[-1].start()
+    for copy in copies:
+        copy.wait()
 
 
 def unpack(payload, rows):
     pairs, both, width = payload.shape
-    lanes = width // 8
     slots = pairs * 2
-    shape = jax.ShapeDtypeStruct((rows, slots, width // 2), BF16)
-
-    def column(i):
-        return jnp.where(i == 0, 0, jnp.where(i == 3, 1, i + 3))
-
-    out_spec = pl.BlockSpec((rows, slots, lanes), lambda i: (0, 0, i))
+    shape = (rows, slots, width // 2)
     return call(
         unpack_kernel,
         "unpack",
-        grid=(4,),
-        out_shape=(shape, shape),
-        in_specs=[
-            pl.BlockSpec((pairs, both, lanes), lambda i: (0, 0, column(i))),
-            pl.BlockSpec((pairs, both, lanes), lambda i: (0, 0, column(i) + 2)),
-        ],
-        out_specs=(out_spec, out_spec),
+        out_shape=(pltpu.HBM(shape, BF16), pltpu.HBM(shape, BF16)),
+        in_specs=[IN_VMEM],
+        out_specs=(IN_PLACE, IN_PLACE),
         scratch_shapes=[
-            pltpu.VMEM((pairs, both, lanes), F32),
+            pltpu.VMEM((2, *shape), BF16),
             pltpu.VMEM((8 * slots, 8 * slots), BF16),
             pltpu.VMEM((4 * slots, 4 * slots), BF16),
+            pltpu.SemaphoreType.DMA((24,)),
         ],
-    )(payload, payload)
+    )(payload)
 
 
 def in_hbm(*arrays):
     return [pltpu.with_memory_space_constraint(x, pltpu.HBM) for x in arrays]
 
 
-def keep_kernel(meta, p_ref, h_ref, out_ref, sems):
+def keep_kernel(meta, p_ref, h_ref, out_ref, kept, sems, out_sems):
     quarter, degrees = p_ref.shape[1:]
     pieces = [(0, degrees - SURE[0] * TILE, SURE[0], 0)]
     for k in range(SHARED):
         pieces.append((meta[k], pl.multiple_of(meta[SHARED + k] * TILE, TILE), 1, SURE[0] + k))
     pieces.append((1, degrees - SURE[1] * TILE, SURE[1], SURE[0] + SHARED))
     copies = []
-    for slot, source, count, target in pieces:
-        for at, ref in enumerate((p_ref, h_ref)):
+    for at, ref in enumerate((p_ref, h_ref)):
+        for slot, source, count, target in pieces:
             copies.append(pltpu.make_async_copy(
                 ref.at[slot, :, pl.ds(source, count * TILE)],
-                out_ref.at[pl.ds(at * quarter, quarter), pl.ds(target * TILE, count * TILE)],
+                kept.at[pl.ds(at * quarter, quarter), pl.ds(target * TILE, count * TILE)],
                 sems.at[len(copies)],
             ))
             copies[-1].start()
-    for copy in copies:
+    sent = []
+    for at in range(2):
+        for copy in copies[at * len(pieces):(at + 1) * len(pieces)]:
+            copy.wait()
+        rows = pl.ds(at * quarter, quarter)
+        sent.append(pltpu.make_async_copy(kept.at[rows], out_ref.at[rows], out_sems.at[at]))
+        sent[at].start()
+    for copy in sent:
         copy.wait()
 
 
@@ -157,24 +169,39 @@
     return call(
         keep_kernel,
         "keep",
-        out_shape=pltpu.VMEM(shape, BF16),
+        out_shape=pltpu.HBM(shape, BF16),
         in_specs=[IN_SMEM] + [IN_PLACE] * 2,
-        out_specs=IN_VMEM,
-        scratch_shapes=[pltpu.SemaphoreType.DMA((2 * (2 + SHARED),))],
+        out_specs=IN_PLACE,
+        scratch_shapes=[
+            pltpu.VMEM(shape, BF16),
+            pltpu.SemaphoreType.DMA((2 * (2 + SHARED),)),
+            pltpu.SemaphoreType.DMA((2,)),
+        ],
     )(meta, *in_hbm(p_table, h_table))
 
 
-def forward_kernel(part, meta, rate, mask, weight, recv, select, table, keep, send, wide, wind, spec):
-    owners, both, width = wide.shape
+STREAM = 512
+N_BLOCKS = -(-KEPT * TILE // STREAM)
+
+
+def forward_kernel(part, meta, rate, mask, weight, recv, select, table, keep, send, *refs):
+    owners, both, width = recv.shape
+    source, (table, wind, spec, sems) = table, refs
+    copies = []
+    for n in range(N_BLOCKS):
+        cols = pl.ds(n * STREAM, min(STREAM, KEPT * TILE - n * STREAM))
+        copies.append(pltpu.make_async_copy(source.at[:, cols], table.at[:, cols], sems.at[n]))
+        copies[n].start()
+    waited = 0
     quarter = select.shape[2]
-    levels = width // 2
+    levels = width // 4
     main = owners * 16
-    for n, at in enumerate((part, 3 - part)):
-        wide[:, :, n * levels:(n + 1) * levels] = recv[:, :, at * levels:(at + 1) * levels].astype(F32)
-    mixed = wide[:, 32:].reshape(owners * 8, width).astype(BF16)
+    columns = [slice(at * levels, (at + 1) * levels) for at in (part, 3 - part)]
+    mixed = [recv[:, 32:, cols].astype(F32).reshape(owners * 8, levels).astype(BF16) for cols in columns]
     for slot in range(2):
-        rows = wide[:, 16 * slot:16 * slot + 16].reshape(main, width).astype(BF16)
-        by_lat = dot(rows, select[slot, :main], TN) + dot(mixed, select[slot, main:], TN)
+        rows = [recv[:, 16 * slot:16 * slot + 16, cols].reshape(main, levels) for cols in columns]
+        by_lat = dot(jnp.concatenate(rows, axis=1), select[slot, :main], TN)
+        by_lat = by_lat + dot(jnp.concatenate(mixed, axis=1), select[slot, main:], TN)
         wind[slot] = (by_lat * weight[...]).astype(BF16)
     split = (SURE[0] + SHARED) * TILE
     for slot in range(2):
@@ -183,6 +210,9 @@
         w = wind[slot]
         for start in range(low, high, BLOCK):
             cols = slice(start, min(start + BLOCK, high))
+            while waited < len(copies) and waited * STREAM < cols.stop:
+                copies[waited].wait()
+                waited += 1
             proj_p = dot(w, table[:quarter, cols], NN)
             proj_h = dot(w, table[quarter:, cols], NN)
             psi = proj_h[:levels] - r * proj_p[levels:]
@@ -203,22 +233,26 @@
     levels = width // 4
     quarter = select.shape[2]
     degrees = table.shape[1]
+    out_shape = [jax.ShapeDtypeStruct((levels, degrees), F32), jax.ShapeDtypeStruct((levels, degrees), BF16)]
+    scratch = [
+        pltpu.VMEM((2, 2 * levels, quarter), BF16),
+        pltpu.VMEM((2 * levels, degrees), F32),
+        pltpu.SemaphoreType.DMA((N_BLOCKS,)),
+    ]
+    (scratch, out_shape)[part].insert((0, 2)[part], pltpu.VMEM(table.shape, BF16))
     return call(
         functools.partial(forward_kernel, part),
         "forward",
-        in_specs=[IN_SMEM] * 2 + [IN_VMEM] * 5,
-        out_specs=[IN_VMEM] * 2,
-        out_shape=[jax.ShapeDtypeStruct((levels, degrees), F32), jax.ShapeDtypeStruct((levels, degrees), BF16)],
-        scratch_shapes=[
-            pltpu.VMEM((owners, both, 2 * levels), F32),
-            pltpu.VMEM((2, 2 * levels, quarter), BF16),
-            pltpu.VMEM((2 * levels, degrees), F32),
-        ],
-    )(meta, rate, mask, weight, recv, select, table)
+        in_specs=[IN_SMEM] * 2 + [IN_VMEM] * 4 + [IN_PLACE],
+        out_specs=[IN_VMEM] * len(out_shape),
+        out_shape=out_shape,
+        scratch_shapes=scratch,
+        cost_estimate=pl.CostEstimate(flops=5 * 10**9, bytes_accessed=10**7, transcendentals=0),
+    )(meta, rate, mask, weight, recv, select, *in_hbm(table))
 
 
 def backward_kernel(part, meta, rate, mask, mine, theirs, select, table, *refs):
-    out_ref, every, masked, winds, wide, out, sem = refs[-7:]
+    out_ref, every, masked, winds, out, sems = refs[-6:]
     levels = mine.shape[0]
     quarter = select.shape[2]
     owners, both, width = out.shape
@@ -241,18 +275,25 @@
         sums = [dot(table[n * quarter:(n + 1) * quarter, low:high], pot, NT) for n in range(2)]
         r = rate[slot]
         winds[slot, :, :levels] = (-sums[1][:, :levels]).astype(BF16)
-        winds[slot, :, levels:2 * levels] = (r * sums[0][:, :levels]).astype(BF16)
-        winds[slot, :, 2 * levels:3 * levels] = (-r * sums[0][:, levels:]).astype(BF16)
+        winds[slot, :, levels:2 * levels] = (-r * sums[0][:, levels:]).astype(BF16)
+        winds[slot, :, 2 * levels:3 * levels] = (r * sums[0][:, :levels]).astype(BF16)
         winds[slot, :, 3 * levels:] = sums[1][:, levels:].astype(BF16)
-    for slot in range(2):
-        moved = dot(select[slot, :main], winds[slot], NN)
-        wide[:, 16 * slot:16 * slot + 16] = moved.reshape(owners, 16, width)
-    mixed = dot(select[0, main:], winds[0], NN) + dot(select[1, main:], winds[1], NN)
-    wide[:, 32:] = mixed.reshape(owners, 8, width)
-    out[...] = wide[...].astype(BF16)
-    copy = pltpu.make_async_copy(out, out_ref.at[:, :, pl.ds(part * width, width)], sem)
-    copy.start()
-    copy.wait()
+    copies = []
+    for n in range(2):
+        cols = slice(n * width // 2, (n + 1) * width // 2)
+        for slot in range(2):
+            moved = dot(select[slot, :main], winds[slot, :, cols], NN)
+            out[:, 16 * slot:16 * slot + 16, cols] = moved.astype(BF16).reshape(owners, 16, width // 2)
+        mixed = dot(select[0, main:], winds[0, :, cols], NN) + dot(select[1, main:], winds[1, :, cols], NN)
+        out[:, 32:, cols] = mixed.reshape(owners, 8, width // 2).astype(BF16)
+        copies.append(pltpu.make_async_copy(
+            out.at[:, :, pl.ds(n * width // 2, width // 2)],
+            out_ref.at[:, :, pl.ds(part * width + n * width // 2, width // 2)],
+            sems.at[n],
+        ))
+        copies[n].start()
+    for copy in copies:
+        copy.wait()
 
 
 def backward(part, meta, rate, mask, mine, theirs, select, table, payload, filled=()):
@@ -271,9 +312,8 @@
             pltpu.VMEM((2 * levels, degrees), BF16),
             pltpu.VMEM((2, 2 * levels, (SURE[0] + SHARED) * TILE), BF16),
             pltpu.VMEM((2, quarter, width // 2), BF16),
-            pltpu.VMEM(piece, F32),
             pltpu.VMEM(piece, BF16),
-            pltpu.SemaphoreType.DMA,
+            pltpu.SemaphoreType.DMA((2,)),
         ],
     )(meta, rate, mask, mine, theirs, select, table, *filled)
 
@@ -350,20 +390,20 @@
     select = (target[:, :, None] == jnp.arange(quarter)[None, None, :]).astype(BF16)
     weight = quad_weight.reshape(1, -1)
 
-    table = pltpu.with_memory_space_constraint(keep(meta, p_table, h_table), pltpu.VMEM)
+    table = keep(meta, p_table, h_table)
     owners, both, width = received.shape
     payload = (owners, both, 2 * width)
     signs = (rate, -rate)
-    mines, theirs = [], []
-    for n in range(2):
-        kept, sent = forward(n, meta, signs[n], mask, weight, received, select, table)
-        kept, sent = add(kept, swap(sent, first))
-        mines.append(scale(kept, swap(sent, second), factor))
-        theirs.append(swap(mines[n], first))
-    filled = ()
-    for n in range(2):
-        filled = (backward(n, meta, signs[n], mask, mines[n], theirs[n], select, table, payload, filled),)
-    return tuple(unpack(lax.all_to_all(filled[0], "ma", 0, 0, tiled=True), rows))
+    kept_a, sent_a = forward(0, meta, signs[0], mask, weight, received, select, table)
+    kept_b, sent_b, table = forward(1, meta, signs[1], mask, weight, received, select, table)
+    table = pltpu.with_memory_space_constraint(table, pltpu.VMEM)
+    kept_a, sent_a = add(kept_a, swap(sent_a, first))
+    kept_b, sent_b = add(kept_b, swap(sent_b, first))
+    mine_a = scale(kept_a, swap(sent_a, second), factor)
+    mine_b = scale(kept_b, swap(sent_b, second), factor)
+    out = backward(0, meta, signs[0], mask, mine_a, swap(mine_a, first), select, table, payload)
+    out = backward(1, meta, signs[1], mask, mine_b, swap(mine_b, first), select, table, payload, (out,))
+    return tuple(unpack(lax.all_to_all(out, "ma", 0, 0, tiled=True), rows))
 
 
 def solution(mesh):

time: 145 us -> 142 us (0.979)
  local copies, waits for them, and re-layouts: 7.16 us -> 1.35 us
  Pallas kernels: 31.9 us -> 35.1 us
    unnamed x17 -> x9, local copies, waits for them, and re-layouts: 5.97 us -> 0.17 us
    pallas_call x2, Pallas kernels: 8.37 us -> 12 us  [forward(): call(functools.partial(forward_kernel, part), 'forward', in_specs=[IN_SME...]
    ppermute x6, waiting for transfers between devices: 31.6 us -> 30.1 us  [swap(): return lax.ppermute(x, ('ma', 'oct'), pairs)]
  transfers between devices with their start and end apart: 7 -> 7, of which waited for: 5 -> 5; matrix products, arithmetic and copies ran while one was open for 2% -> 2% of each run, Pallas kernels for 10% -> 13%
where the time goes in v3:
time: 142 us; the launch traced here: 140 us
  waiting for transfers between devices  40.8 us (29%)
  blocking collectives  38.3 us (27%)
  Pallas kernels  35.1 us (25%)
  starting transfers between devices  19.4 us (14%)
  between operations  3.25 us (2%)
  other arithmetic  2.11 us (1%)
    all_to_all x1, blocking collectives, on_device(): return tuple(unpack(lax.all_to_all(out, 'ma', 0, 0, tiled=True), rows))  38.3 us
    ppermute x6, waiting for transfers between devices, swap(): return lax.ppermute(x, ('ma', 'oct'), pairs)  30.1 us
    pallas_call x2, Pallas kernels, forward(): call(functools.partial(forward_kernel, part), 'forward', in_specs=[IN_SME...  12 us
    ppermute x6, starting transfers between devices, swap(): return lax.ppermute(x, ('ma', 'oct'), pairs)  11.9 us
    pallas_call x2, Pallas kernels, backward(): call(functools.partial(backward_kernel, part), 'backward', in_specs=[IN_S...  10.8 us
    all_to_all x1, waiting for transfers between devices, on_device(): received = lax.all_to_all(pack(fourier_wind), 'ma', 0, 0, tiled=True)  10.7 us
    all_to_all x1, starting transfers between devices, on_device(): received = lax.all_to_all(pack(fourier_wind), 'ma', 0, 0, tiled=True)  7.54 us
    pallas_call x1, Pallas kernels, keep(): call(keep_kernel, 'keep', out_shape=pltpu.HBM(shape, BF16), in_specs=[IN_...  5.78 us
  transfers between devices with their start and end apart: 7, of which 5 were waited for; matrix products, arithmetic and copies ran while one was open for 2% of the time, Pallas kernels for 13%

profile of v3, /device:TPU:0, one launch (start us, length us, event | category | flops | bytes accessed | tf_op | source)
XLA Modules:
  0.0 140.4 jit_solution(9624274332655857094)
XLA Ops:
  0.6 3.1 %pack.1 = bf16[32,40,512]{2,1,0:T(8,128)(2,1)} custom-call(bf16[20,64,512]{2,1,0:T(8,128)(2,1)} %wind_ref.1), custom_call_target="tpu_custom_call" | custom-call | tf_op jit(solution)/shard_map/pack/pallas_call | solution.py:70
  3.8 7.5 %all-to-all-start = ((bf16[32,40,512]{2,1,0:T(8,128)(2,1)}), bf16[32,40,512]{2,1,0:T(8,128)(2,1)S(1)}, u32[]{:S(2)}, u32[]{:S(2)}) async-start(bf16[32,40,512]{2,1,0:T(8,128)(2,1)} %pack.1), calls=%async_computation | async-start | bytes 2621440 | tf_op jit(solution)/shard_map/all_to_all | solution.py:367
  11.3 0.6 fusion.5
  15.2 5.8 %keep.1.table = bf16[1280,2688]{1,0:T(8,128)(2,1)} custom-call(s32[11]{0:T(128)S(1)} %pad_add_fusion.3.meta, bf16[2,640,2560]{2,1,0:T(8,128)(2,1)} %p_ref.1, bf16[2,640,2560]{2,1,0:T(8,128)(2,1)} %h_ref.1), custom_call_target="tpu_custom_call" | custom-call | tf_op jit(solution)/shard_map/keep/pallas_call | solution.py:169
  21.0 0.4 fusion.select
  21.4 10.7 %all-to-all-done.recv = bf16[32,40,512]{2,1,0:T(8,128)(2,1)S(1)} async-done(((bf16[32,40,512]{2,1,0:T(8,128)(2,1)}), bf16[32,40,512]{2,1,0:T(8,128)(2,1)S(1)}, u32[]{:S(2)}, u32[]{:S(2)}) %all-to-all-start) | async-done | bytes 1310752 | tf_op jit(solution)/shard_map/all_to_all | solution.py:367
  32.1 6.2 %forward.3 = (f32[128,2688]{1,0:T(8,128)S(1)}, bf16[128,2688]{1,0:T(8,128)(2,1)S(1)}) custom-call(s32[11]{0:T(128)S(1)} %pad_add_fusion.3.meta, f32[2]{0:T(128)S(1)} %get-tuple-element.24.rate, f32[1,2688]{1,0:T(1,128)S(1)} %bitcast.21, f32[1,640]{1,0:T(1,128)S(1)} %reshape.113.weight, bf16[32,40,512]{2,1,0:T(8,128)(2,1)S(1)} %all-to-all-done.recv, ...), custom_call_target="tpu_custom_call" | custom-call | flops 5000000000 | bytes 10000000 | tf_op jit(solution)/shard_map/forward/pallas_call | solution.py:243
  38.4 2.0 %collective-permute-start.3 = (bf16[128,2688]{1,0:T(8,128)(2,1)S(1)}, bf16[128,2688]{1,0:T(8,128)(2,1)S(1)}, u32[]{:S(2)}, u32[]{:S(2)}) collective-permute-start(bf16[128,2688]{1,0:T(8,128)(2,1)S(1)} %get-tuple-element.17), channel_id=1, source_target_pairs={{0,1},{1,0},{2,3},{3,2},{4,7},{5,6},{6,5},{7,4},{8,9},{9,8},{10,11... | collective-permute-start | bytes 2064392 | tf_op jit(solution)/shard_map/ppermute | solution.py:365
  40.4 5.8 %forward.2 = (f32[128,2688]{1,0:T(8,128)S(1)}, bf16[128,2688]{1,0:T(8,128)(2,1)S(1)}, bf16[1280,2688]{1,0:T(8,128)(2,1)S(1)}) custom-call(s32[11]{0:T(128)S(1)} %pad_add_fusion.3.meta, f32[2]{0:T(128)S(1)} %get-tuple-element.25.rate, f32[1,2688]{1,0:T(1,128)S(1)} %bitcast.22, f32[1,640]{1,0:T(1,128)S(1)} %reshape.113.weight, ...), custom_call_target="tpu_custom_call" | custom-call | flops 5000000000 | bytes 10000000 | tf_op jit(solution)/shard_map/forward/pallas_call | solution.py:243
  46.3 1.3 fusion.2
  47.8 1.6 %collective-permute-done.3.got = bf16[128,2688]{1,0:T(8,128)(2,1)S(1)} collective-permute-done((bf16[128,2688]{1,0:T(8,128)(2,1)S(1)}, bf16[128,2688]{1,0:T(8,128)(2,1)S(1)}, u32[]{:S(2)}, u32[]{:S(2)}) %collective-permute-start.3) | collective-permute-done | bytes 688160 | tf_op jit(solution)/shard_map/ppermute | solution.py:365
  49.4 0.2 add.113
  49.6 4.1 %collective-permute-start.4 = (bf16[128,2688]{1,0:T(8,128)(2,1)S(1)}, bf16[128,2688]{1,0:T(8,128)(2,1)S(1)}, u32[]{:S(2)}, u32[]{:S(2)}) collective-permute-start(bf16[128,2688]{1,0:T(8,128)(2,1)S(1)} %get-tuple-element.19), channel_id=1, source_target_pairs={{0,3},{1,2},{2,1},{3,0},{4,5},{5,4},{6,7},{7,6},{8,11},{9,10},{10,... | collective-permute-start | bytes 2064392 | tf_op jit(solution)/shard_map/ppermute | solution.py:365
  53.7 8.8 %collective-permute-done.got = bf16[128,2688]{1,0:T(8,128)(2,1)S(1)} collective-permute-done((bf16[128,2688]{1,0:T(8,128)(2,1)S(1)}, bf16[128,2688]{1,0:T(8,128)(2,1)S(1)}, u32[]{:S(2)}, u32[]{:S(2)}) %collective-permute-start) | collective-permute-done | bytes 688160 | tf_op jit(solution)/shard_map/ppermute | solution.py:365
  62.5 0.2 add.112
  62.8 4.1 %collective-permute-start.1 = (bf16[128,2688]{1,0:T(8,128)(2,1)S(1)}, bf16[128,2688]{1,0:T(8,128)(2,1)S(1)}, u32[]{:S(2)}, u32[]{:S(2)}) collective-permute-start(bf16[128,2688]{1,0:T(8,128)(2,1)S(1)} %get-tuple-element.14), channel_id=1, source_target_pairs={{0,3},{1,2},{2,1},{3,0},{4,5},{5,4},{6,7},{7,6},{8,11},{9,10},{10,... | collective-permute-start | bytes 2064392 | tf_op jit(solution)/shard_map/ppermute | solution.py:365
  67.2 0.2 collective-permute-start.5
  67.4 15.2 %collective-permute-done.1.got = bf16[128,2688]{1,0:T(8,128)(2,1)S(1)} collective-permute-done((bf16[128,2688]{1,0:T(8,128)(2,1)S(1)}, bf16[128,2688]{1,0:T(8,128)(2,1)S(1)}, u32[]{:S(2)}, u32[]{:S(2)}) %collective-permute-start.1) | collective-permute-done | bytes 688160 | tf_op jit(solution)/shard_map/ppermute | solution.py:365
  82.7 1.2 collective-permute-start.2
  83.9 5.4 %backward.2.refs_0_ = bf16[32,40,1024]{2,1,0:T(8,128)(2,1)} custom-call(s32[11]{0:T(128)S(1)} %pad_add_fusion.3.meta, f32[2]{0:T(128)S(1)} %get-tuple-element.24.rate, f32[1,2688]{1,0:T(1,128)S(1)} %bitcast.23, bf16[128,2688]{1,0:T(8,128)(2,1)S(1)} %scale.3.mine, bf16[128,2688]{1,0:T(8,128)(2,1)S(1)} %collective-permute-done.5.theirs, ...), custom_call_target="tpu_custom_call" | custom-call | tf_op jit(solution)/shard_map/backward/pallas_call | solution.py:304
  89.4 4.5 %collective-permute-done.2.theirs = bf16[128,2688]{1,0:T(8,128)(2,1)S(1)} collective-permute-done((bf16[128,2688]{1,0:T(8,128)(2,1)S(1)}, bf16[128,2688]{1,0:T(8,128)(2,1)S(1)}, u32[]{:S(2)}, u32[]{:S(2)}) %collective-permute-start.2) | collective-permute-done | bytes 688160 | tf_op jit(solution)/shard_map/ppermute | solution.py:365
  93.9 5.4 %backward.3 = bf16[32,40,1024]{2,1,0:T(8,128)(2,1)} custom-call(s32[11]{0:T(128)S(1)} %pad_add_fusion.3.meta, f32[2]{0:T(128)S(1)} %get-tuple-element.25.rate, f32[1,2688]{1,0:T(1,128)S(1)} %bitcast.24, bf16[128,2688]{1,0:T(8,128)(2,1)S(1)} %scale.2.mine, bf16[128,2688]{1,0:T(8,128)(2,1)S(1)} %collective-permute-done.2.theirs, ...), custom_call_target="tpu_custom_call", output_to_operand_aliasing={{}: (7, {})} | custom-call | tf_op jit(solution)/shard_map/backward/pallas_call | solution.py:304
  99.3 38.3 %all_to_all.10.payload = bf16[32,40,1024]{2,1,0:T(8,128)(2,1)S(1)} all-to-all(bf16[32,40,1024]{2,1,0:T(8,128)(2,1)} %backward.3), channel_id=1, replica_groups=mesh['ma'=32,'oct'=4] {'ma'}, dimensions={0} | all-to-all | bytes 5242880 | tf_op jit(solution)/shard_map/all_to_all | solution.py:406
  137.6 2.6 %unpack.1 = (bf16[20,64,512]{2,1,0:T(8,128)(2,1)}, bf16[20,64,512]{2,1,0:T(8,128)(2,1)}) custom-call(bf16[32,40,1024]{2,1,0:T(8,128)(2,1)S(1)} %all_to_all.10.payload), custom_call_target="tpu_custom_call" | custom-call | tf_op jit(solution)/shard_map/unpack/pallas_call | solution.py:122
  (38 shorter events, 1.6 us)
Async XLA Ops:
  3.8 7.6 %copy-start.2 = (s32[2]{0:T(128)S(1)}, s32[2]{0:T(128)}, u32[]{:S(2)}) copy-start(s32[2]{0:T(128)} %param.10) | copy-start | bytes 28
  3.8 10.6 %copy-start.1 = (f32[640]{0:T(1024)S(1)}, f32[640]{0:T(1024)}, u32[]{:S(2)}) copy-start(f32[640]{0:T(1024)} %param.7) | copy-start | bytes 7684
  3.8 10.6 %copy-start = (s32[2560]{0:T(1024)S(1)}, s32[2560]{0:T(1024)}, u32[]{:S(2)}) copy-start(s32[2560]{0:T(1024)} %param.11) | copy-start | bytes 30724
  3.8 28.3 %all-to-all-start = ((bf16[32,40,512]{2,1,0:T(8,128)(2,1)}), bf16[32,40,512]{2,1,0:T(8,128)(2,1)S(1)}, u32[]{:S(2)}, u32[]{:S(2)}) async-start(bf16[32,40,512]{2,1,0:T(8,128)(2,1)} %pack.1), calls=%async_computation | async-start | bytes 2621440 | tf_op jit(solution)/shard_map/all_to_all | solution.py:367
  38.4 11.0 %collective-permute-start.3 = (bf16[128,2688]{1,0:T(8,128)(2,1)S(1)}, bf16[128,2688]{1,0:T(8,128)(2,1)S(1)}, u32[]{:S(2)}, u32[]{:S(2)}) collective-permute-start(bf16[128,2688]{1,0:T(8,128)(2,1)S(1)} %get-tuple-element.17), channel_id=1, source_target_pairs={{0,1},{1,0},{2,3},{3,2},{4,7},{5,6},{6,5},{7,4},{8,9},{9,8},{10,11... | collective-permute-start | bytes 2064392 | tf_op jit(solution)/shard_map/ppermute | solution.py:365
  46.1 16.4 %collective-permute-start = (bf16[128,2688]{1,0:T(8,128)(2,1)S(1)}, bf16[128,2688]{1,0:T(8,128)(2,1)S(1)}, u32[]{:S(2)}, u32[]{:S(2)}) collective-permute-start(bf16[128,2688]{1,0:T(8,128)(2,1)S(1)} %get-tuple-element.12), channel_id=1, source_target_pairs={{0,1},{1,0},{2,3},{3,2},{4,7},{5,6},{6,5},{7,4},{8,9},{9,8},{10,11... | collective-permute-start | bytes 2064392 | tf_op jit(solution)/shard_map/ppermute | solution.py:365
  49.6 17.4 %collective-permute-start.4 = (bf16[128,2688]{1,0:T(8,128)(2,1)S(1)}, bf16[128,2688]{1,0:T(8,128)(2,1)S(1)}, u32[]{:S(2)}, u32[]{:S(2)}) collective-permute-start(bf16[128,2688]{1,0:T(8,128)(2,1)S(1)} %get-tuple-element.19), channel_id=1, source_target_pairs={{0,3},{1,2},{2,1},{3,0},{4,5},{5,4},{6,7},{7,6},{8,11},{9,10},{10,... | collective-permute-start | bytes 2064392 | tf_op jit(solution)/shard_map/ppermute | solution.py:365
  62.8 19.8 %collective-permute-start.1 = (bf16[128,2688]{1,0:T(8,128)(2,1)S(1)}, bf16[128,2688]{1,0:T(8,128)(2,1)S(1)}, u32[]{:S(2)}, u32[]{:S(2)}) collective-permute-start(bf16[128,2688]{1,0:T(8,128)(2,1)S(1)} %get-tuple-element.14), channel_id=1, source_target_pairs={{0,3},{1,2},{2,1},{3,0},{4,5},{5,4},{6,7},{7,6},{8,11},{9,10},{10,... | collective-permute-start | bytes 2064392 | tf_op jit(solution)/shard_map/ppermute | solution.py:365
  67.2 16.8 %collective-permute-start.5 = (bf16[128,2688]{1,0:T(8,128)(2,1)S(1)}, bf16[128,2688]{1,0:T(8,128)(2,1)S(1)}, u32[]{:S(2)}, u32[]{:S(2)}) collective-permute-start(bf16[128,2688]{1,0:T(8,128)(2,1)S(1)} %scale.3.mine), channel_id=1, source_target_pairs={{0,1},{1,0},{2,3},{3,2},{4,7},{5,6},{6,5},{7,4},{8,9},{9,8},{10,11... | collective-permute-start | bytes 2064392 | tf_op jit(solution)/shard_map/ppermute | solution.py:365
  82.7 11.2 %collective-permute-start.2 = (bf16[128,2688]{1,0:T(8,128)(2,1)S(1)}, bf16[128,2688]{1,0:T(8,128)(2,1)S(1)}, u32[]{:S(2)}, u32[]{:S(2)}) collective-permute-start(bf16[128,2688]{1,0:T(8,128)(2,1)S(1)} %scale.2.mine), channel_id=1, source_target_pairs={{0,1},{1,0},{2,3},{3,2},{4,7},{5,6},{6,5},{7,4},{8,9},{9,8},{10,11... | collective-permute-start | bytes 2064392 | tf_op jit(solution)/shard_map/ppermute | solution.py:365

commit v4 on v3

--- a/solution.py
+++ b/solution.py
@@ -12,6 +12,9 @@
 SURE = (11, 5)
 SHARED = 5
 KEPT = SURE[0] + SHARED + SURE[1]
+CUT = (SURE[0] + SHARED - 1) * TILE
+SENT = (KEPT - 1) * TILE
+HALF, ALL_FIRST, LANE, AT, AT_SENT = range(2 * SHARED, 2 * SHARED + 5)
 BLOCK = 512
 BF16 = jnp.bfloat16
 F32 = jnp.float32
@@ -184,7 +187,8 @@
 N_BLOCKS = -(-KEPT * TILE // STREAM)
 
 
-def forward_kernel(part, meta, rate, mask, weight, recv, select, table, keep, send, *refs):
+def forward_kernel(part, meta, rate, mask, weight, recv, select, table, factor, keep, send, *refs):
+    del factor
     owners, both, width = recv.shape
     source, (table, wind, spec, sems) = table, refs
     copies = []
@@ -223,32 +227,39 @@
                 chi = jnp.where(first, spec[levels:, cols], chi)
             spec[:levels, cols] = psi
             spec[levels:, cols] = chi
-    mine = meta[2 * SHARED] * levels
-    keep[...] = spec[pl.ds(pl.multiple_of(mine, levels), levels), :]
-    send[...] = spec[pl.ds(pl.multiple_of(levels - mine, levels), levels), :].astype(BF16)
-
-
-def forward(part, meta, rate, mask, weight, recv, select, table):
+    lane = lax.broadcasted_iota(jnp.int32, (2 * levels, TILE), 1)
+    at = pl.ds(pl.multiple_of(meta[AT] * TILE, TILE), TILE)
+    last, other = spec[:, CUT:CUT + TILE], spec[:, at]
+    all_first = meta[ALL_FIRST] == 1
+    low_first, low_second = jnp.where(all_first, last, other), jnp.where(all_first, other, last)
+    spec[:, at] = jnp.where(lane >= meta[LANE], low_first, pltpu.roll(low_second, meta[LANE], 1))
+    mine = pl.multiple_of(meta[HALF] * levels, levels)
+    for ref, start in ((keep, mine), (send, levels - mine)):
+        rows = pl.ds(pl.multiple_of(start, levels), levels)
+        ref[:, :CUT] = spec[rows, :CUT].astype(ref.dtype)
+        ref[:, CUT:] = spec[rows, CUT + TILE:].astype(ref.dtype)
+
+
+def forward(part, meta, rate, mask, weight, recv, select, table, factor):
     owners, both, width = recv.shape
     levels = width // 4
     quarter = select.shape[2]
-    degrees = table.shape[1]
-    out_shape = [jax.ShapeDtypeStruct((levels, degrees), F32), jax.ShapeDtypeStruct((levels, degrees), BF16)]
+    out_shape = [jax.ShapeDtypeStruct((levels, SENT), F32), jax.ShapeDtypeStruct((levels, SENT), BF16)]
     scratch = [
         pltpu.VMEM((2, 2 * levels, quarter), BF16),
-        pltpu.VMEM((2 * levels, degrees), F32),
+        pltpu.VMEM((2 * levels, KEPT * TILE), F32),
         pltpu.SemaphoreType.DMA((N_BLOCKS,)),
     ]
     (scratch, out_shape)[part].insert((0, 2)[part], pltpu.VMEM(table.shape, BF16))
     return call(
         functools.partial(forward_kernel, part),
         "forward",
-        in_specs=[IN_SMEM] * 2 + [IN_VMEM] * 4 + [IN_PLACE],
+        in_specs=[IN_SMEM] * 2 + [IN_VMEM] * 4 + [IN_PLACE] * 2,
         out_specs=[IN_VMEM] * len(out_shape),
         out_shape=out_shape,
         scratch_shapes=scratch,
         cost_estimate=pl.CostEstimate(flops=5 * 10**9, bytes_accessed=10**7, transcendentals=0),
-    )(meta, rate, mask, weight, recv, select, *in_hbm(table))
+    )(meta, rate, mask, weight, recv, select, *in_hbm(table), factor)
 
 
 def backward_kernel(part, meta, rate, mask, mine, theirs, select, table, *refs):
@@ -259,16 +270,35 @@
     main = owners * 16
     split = (SURE[0] + SHARED) * TILE
     degrees = KEPT * TILE
-    at = meta[2 * SHARED] * levels
+    at = meta[HALF] * levels
     every[pl.ds(pl.multiple_of(at, levels), levels), :] = mine[...]
     every[pl.ds(pl.multiple_of(levels - at, levels), levels), :] = theirs[...]
     shared = slice(SURE[0] * TILE, split)
-    first = mask[:, shared] > 0.5
-    both_slots = every[:, shared].astype(F32)
+    cut = CUT - shared.start
+    first = mask[:, shared.start:CUT] > 0.5
+    both_slots = every[:, shared.start:CUT].astype(F32)
+    lane = lax.broadcasted_iota(jnp.int32, (2 * levels, TILE), 1)
+    joint = every[:, pl.ds(pl.multiple_of(meta[AT_SENT] * TILE, TILE), TILE)].astype(F32)
+    back = TILE - meta[LANE]
+    low_first = jnp.where(lane >= meta[LANE], joint, 0.0).astype(BF16)
+    low_second = jnp.where(lane >= back, pltpu.roll(joint, back & (TILE - 1), 1), 0.0).astype(BF16)
     masked[0, :, :shared.start] = every[:, :shared.start]
-    masked[0, :, shared] = jnp.where(first, both_slots, 0.0).astype(BF16)
-    masked[1, :, :split - shared.start] = jnp.where(first, 0.0, both_slots).astype(BF16)
-    masked[1, :, split - shared.start:degrees - shared.start] = every[:, split:]
+    masked[0, :, shared.start:CUT] = jnp.where(first, both_slots, 0.0).astype(BF16)
+    masked[1, :, :cut] = jnp.where(first, 0.0, both_slots).astype(BF16)
+    masked[1, :, cut + TILE:degrees - shared.start] = every[:, CUT:]
+
+    @pl.when(meta[ALL_FIRST] == 1)
+    def _():
+        masked[0, :, CUT:split] = low_first
+        masked[1, :, cut:cut + TILE] = jnp.zeros_like(low_second)
+        masked[1, :, cut + TILE:cut + 2 * TILE] = low_second
+
+    @pl.when(meta[ALL_FIRST] != 1)
+    def _():
+        masked[0, :, CUT:split] = jnp.zeros_like(low_first)
+        masked[0, :, pl.ds(pl.multiple_of(meta[AT] * TILE, TILE), TILE)] = low_first
+        masked[1, :, cut:cut + TILE] = low_second
+
     for slot in range(2):
         low, high = (0, split) if slot == 0 else (shared.start, degrees)
         pot = masked[slot, :, :high - low]
@@ -298,7 +328,7 @@
 
 def backward(part, meta, rate, mask, mine, theirs, select, table, payload, filled=()):
     quarter = select.shape[2]
-    levels, degrees = mine.shape
+    levels = mine.shape[0]
     owners, both, width = payload
     piece = (owners, both, width // 2)
     return call(
@@ -309,7 +339,7 @@
         out_shape=pltpu.HBM(payload, BF16),
         input_output_aliases={7: 0} if filled else {},
         scratch_shapes=[
-            pltpu.VMEM((2 * levels, degrees), BF16),
+            pltpu.VMEM((2 * levels, SENT), BF16),
             pltpu.VMEM((2, 2 * levels, (SURE[0] + SHARED) * TILE), BF16),
             pltpu.VMEM((2, quarter, width // 2), BF16),
             pltpu.VMEM(piece, BF16),
@@ -345,6 +375,30 @@
         out_specs=IN_VMEM,
         out_shape=jax.ShapeDtypeStruct(kept.shape, BF16),
     )(kept, got, factor)
+
+
+def layout(wavenumbers, count, half):
+    low_first, low_second = wavenumbers[0] // TILE, wavenumbers[1] // TILE
+    n_first = count - low_first - SURE[0]
+    k = jnp.arange(SHARED)
+    shared_slot = (k >= n_first).astype(jnp.int32)
+    shared_tile = jnp.where(k < n_first, count - SURE[0] - 1 - k, count - SURE[1] - 1 - (k - n_first))
+    slot = jnp.concatenate([jnp.zeros(SURE[0], jnp.int32), shared_slot, jnp.ones(SURE[1], jnp.int32)])
+    mask = jnp.repeat(1.0 - slot.astype(F32), TILE)[None, :]
+    all_first = n_first == SHARED
+    at = jnp.where(n_first == 0, 0, SURE[0] - 1 + n_first)
+    at, at_sent = jnp.where(all_first, SURE[0] + SHARED, at), jnp.where(all_first, SURE[0] + SHARED - 1, at)
+    lane_first = wavenumbers[0] % TILE
+    scalars = jnp.stack([half, all_first.astype(jnp.int32), lane_first, at, at_sent])
+    meta = jnp.concatenate([shared_slot, shared_tile, scalars]).astype(jnp.int32)
+    tile = jnp.concatenate([jnp.arange(count - SURE[0], count), shared_tile[:-1], jnp.arange(count - SURE[1], count)])
+    joint = jnp.arange(tile.shape[0]) == at_sent
+    lane = jnp.arange(TILE)
+    degree = jnp.where(joint, low_first, tile)[:, None] * TILE + lane[None, :]
+    degree_second = low_second * TILE + TILE + lane - lane_first
+    degree = jnp.where(joint[:, None] & (lane < lane_first)[None, :], degree_second[None, :], degree).astype(F32)
+    factor = (-(LMAX * LMAX * 1.0) / jnp.maximum(degree * (degree + 1.0), 1.0)).reshape(1, -1)
+    return meta, mask, factor
 
 
 def on_device(fourier_wind, quad_weight, p_table, h_table, wavenumbers, row_latitude):
@@ -366,18 +420,7 @@
 
     received = lax.all_to_all(pack(fourier_wind), "ma", 0, 0, tiled=True)
 
-    n_first = count - wavenumbers[0] // TILE - SURE[0]
-    k = jnp.arange(SHARED)
-    shared_slot = (k >= n_first).astype(jnp.int32)
-    shared_tile = jnp.where(k < n_first, count - SURE[0] - 1 - k, count - SURE[1] - 1 - (k - n_first))
-    meta = jnp.concatenate([shared_slot, shared_tile, half[None]]).astype(jnp.int32)
-    slot = jnp.concatenate([jnp.zeros(SURE[0], jnp.int32), shared_slot, jnp.ones(SURE[1], jnp.int32)])
-    tile = jnp.concatenate([jnp.arange(count - SURE[0], count), shared_tile, jnp.arange(count - SURE[1], count)])
-    mask = jnp.repeat(1.0 - slot.astype(F32), TILE)[None, :]
-    degree = (tile[:, None] * TILE + jnp.arange(TILE)[None, :]).astype(F32)
-    limit = jnp.where(slot == 0, wavenumbers[0], wavenumbers[1]).astype(F32)[:, None]
-    factor = jnp.where(
-        degree >= limit, -(LMAX * LMAX * 1.0) / jnp.maximum(degree * (degree + 1.0), 1.0), 0.0).reshape(1, -1)
+    meta, mask, factor = layout(wavenumbers, count, half)
     rate = wavenumbers.astype(F32) / LMAX
 
     local = lax.dynamic_index_in_dim(row_latitude.reshape(owners, groups, rows), me, 1, keepdims=False) - me * quarter
@@ -394,8 +437,8 @@
     owners, both, width = received.shape
     payload = (owners, both, 2 * width)
     signs = (rate, -rate)
-    kept_a, sent_a = forward(0, meta, signs[0], mask, weight, received, select, table)
-    kept_b, sent_b, table = forward(1, meta, signs[1], mask, weight, received, select, table)
+    kept_a, sent_a = forward(0, meta, signs[0], mask, weight, received, select, table, factor)
+    kept_b, sent_b, table = forward(1, meta, signs[1], mask, weight, received, select, table, factor)
     table = pltpu.with_memory_space_constraint(table, pltpu.VMEM)
     kept_a, sent_a = add(kept_a, swap(sent_a, first))
     kept_b, sent_b = add(kept_b, swap(sent_b, first))

time: 142 us -> 140 us (0.986)
  waiting for transfers between devices: 40.8 us -> 35.1 us
  between operations: 3.25 us -> 6.52 us
    all_to_all x1, waiting for transfers between devices: 10.7 us -> 7.29 us  [on_device(): received = lax.all_to_all(pack(fourier_wind), 'ma', 0, 0, tiled=True)]
    ppermute x6, waiting for transfers between devices: 30.1 us -> 27.8 us  [swap(): return lax.ppermute(x, ('ma', 'oct'), pairs)]
  transfers between devices with their start and end apart: 7 -> 7, of which waited for: 5 -> 5; matrix products, arithmetic and copies ran while one was open for 2% -> 1% of each run, Pallas kernels for 13% -> 13%
where the time goes in v4:
time: 140 us; the launch traced here: 138 us
  blocking collectives  38.3 us (27%)
  Pallas kernels  35.7 us (26%)
  waiting for transfers between devices  35.1 us (25%)
  starting transfers between devices  20.5 us (15%)
  between operations  6.52 us (5%)
    all_to_all x1, blocking collectives, on_device(): return tuple(unpack(lax.all_to_all(out, 'ma', 0, 0, tiled=True), rows))  38.3 us
    ppermute x6, waiting for transfers between devices, swap(): return lax.ppermute(x, ('ma', 'oct'), pairs)  27.8 us
    ppermute x6, starting transfers between devices, swap(): return lax.ppermute(x, ('ma', 'oct'), pairs)  12.9 us
    pallas_call x2, Pallas kernels, forward(): call(functools.partial(forward_kernel, part), 'forward', in_specs=[IN_SME...  12.2 us
    pallas_call x2, Pallas kernels, backward(): call(functools.partial(backward_kernel, part), 'backward', in_specs=[IN_S...  11.2 us
    all_to_all x1, starting transfers between devices, on_device(): received = lax.all_to_all(pack(fourier_wind), 'ma', 0, 0, tiled=True)  7.54 us
    all_to_all x1, waiting for transfers between devices, on_device(): received = lax.all_to_all(pack(fourier_wind), 'ma', 0, 0, tiled=True)  7.29 us
    pallas_call x1, Pallas kernels, keep(): call(keep_kernel, 'keep', out_shape=pltpu.HBM(shape, BF16), in_specs=[IN_...  5.78 us
  transfers between devices with their start and end apart: 7, of which 5 were waited for; matrix products, arithmetic and copies ran while one was open for 1% of the time, Pallas kernels for 13%

profile of v4, /device:TPU:0, one launch (start us, length us, event | category | flops | bytes accessed | tf_op | source)
XLA Modules:
  0.0 138.1 jit_solution(10336776906775276063)
XLA Ops:
  0.6 3.1 %pack.1 = bf16[32,40,512]{2,1,0:T(8,128)(2,1)} custom-call(bf16[20,64,512]{2,1,0:T(8,128)(2,1)} %wind_ref.1), custom_call_target="tpu_custom_call" | custom-call | tf_op jit(solution)/shard_map/pack/pallas_call | solution.py:73
  3.8 7.5 %all-to-all-start = ((bf16[32,40,512]{2,1,0:T(8,128)(2,1)}), bf16[32,40,512]{2,1,0:T(8,128)(2,1)S(1)}, u32[]{:S(2)}, u32[]{:S(2)}) async-start(bf16[32,40,512]{2,1,0:T(8,128)(2,1)} %pack.1), calls=%async_computation | async-start | bytes 2621440 | tf_op jit(solution)/shard_map/all_to_all | solution.py:421
  11.4 0.6 fusion.7
  18.4 5.8 %keep.1.table = bf16[1280,2688]{1,0:T(8,128)(2,1)} custom-call(s32[15]{0:T(128)S(1)} %concatenate.25.meta, bf16[2,640,2560]{2,1,0:T(8,128)(2,1)} %p_ref.1, bf16[2,640,2560]{2,1,0:T(8,128)(2,1)} %h_ref.1), custom_call_target="tpu_custom_call" | custom-call | tf_op jit(solution)/shard_map/keep/pallas_call | solution.py:172
  24.4 0.4 fusion.select
  24.8 7.3 %all-to-all-done.recv = bf16[32,40,512]{2,1,0:T(8,128)(2,1)S(1)} async-done(((bf16[32,40,512]{2,1,0:T(8,128)(2,1)}), bf16[32,40,512]{2,1,0:T(8,128)(2,1)S(1)}, u32[]{:S(2)}, u32[]{:S(2)}) %all-to-all-start) | async-done | bytes 1310752 | tf_op jit(solution)/shard_map/all_to_all | solution.py:421
  32.1 6.3 %forward.3 = (f32[128,2560]{1,0:T(8,128)S(1)}, bf16[128,2560]{1,0:T(8,128)(2,1)S(1)}) custom-call(s32[15]{0:T(128)S(1)} %concatenate.25.meta, f32[2]{0:T(128)S(1)} %get-tuple-element.24.rate, f32[1,2688]{1,0:T(1,128)S(1)} %bitcast.21, f32[1,640]{1,0:T(1,128)S(1)} %reshape.133.weight, bf16[32,40,512]{2,1,0:T(8,128)(2,1)S(1)} %all-to-all-done.recv, ...), custom_call_target="tpu_custom_call" | custom-call | flops 5000000000 | bytes 10000000 | tf_op jit(solution)/shard_map/forward/pallas_call | solution.py:254
  38.4 2.0 %collective-permute-start.3 = (bf16[128,2560]{1,0:T(8,128)(2,1)S(1)}, bf16[128,2560]{1,0:T(8,128)(2,1)S(1)}, u32[]{:S(2)}, u32[]{:S(2)}) collective-permute-start(bf16[128,2560]{1,0:T(8,128)(2,1)S(1)} %get-tuple-element.17), channel_id=1, source_target_pairs={{0,1},{1,0},{2,3},{3,2},{4,7},{5,6},{6,5},{7,4},{8,9},{9,8},{10,11... | collective-permute-start | bytes 1966088 | tf_op jit(solution)/shard_map/ppermute | solution.py:419
  40.4 5.9 %forward.2 = (f32[128,2560]{1,0:T(8,128)S(1)}, bf16[128,2560]{1,0:T(8,128)(2,1)S(1)}, bf16[1280,2688]{1,0:T(8,128)(2,1)S(1)}) custom-call(s32[15]{0:T(128)S(1)} %concatenate.25.meta, f32[2]{0:T(128)S(1)} %get-tuple-element.25.rate, f32[1,2688]{1,0:T(1,128)S(1)} %bitcast.22, f32[1,640]{1,0:T(1,128)S(1)} %reshape.133.weight, ...), custom_call_target="tpu_custom_call" | custom-call | flops 5000000000 | bytes 10000000 | tf_op jit(solution)/shard_map/forward/pallas_call | solution.py:254
  46.3 0.2 collective-permute-start
  46.5 2.6 %collective-permute-done.3.got = bf16[128,2560]{1,0:T(8,128)(2,1)S(1)} collective-permute-done((bf16[128,2560]{1,0:T(8,128)(2,1)S(1)}, bf16[128,2560]{1,0:T(8,128)(2,1)S(1)}, u32[]{:S(2)}, u32[]{:S(2)}) %collective-permute-start.3) | collective-permute-done | bytes 655392 | tf_op jit(solution)/shard_map/ppermute | solution.py:419
  49.1 0.2 add.129
  49.3 4.1 %collective-permute-start.4 = (bf16[128,2560]{1,0:T(8,128)(2,1)S(1)}, bf16[128,2560]{1,0:T(8,128)(2,1)S(1)}, u32[]{:S(2)}, u32[]{:S(2)}) collective-permute-start(bf16[128,2560]{1,0:T(8,128)(2,1)S(1)} %get-tuple-element.19), channel_id=1, source_target_pairs={{0,3},{1,2},{2,1},{3,0},{4,5},{5,4},{6,7},{7,6},{8,11},{9,10},{10,... | collective-permute-start | bytes 1966088 | tf_op jit(solution)/shard_map/ppermute | solution.py:419
  53.4 8.7 %collective-permute-done.got = bf16[128,2560]{1,0:T(8,128)(2,1)S(1)} collective-permute-done((bf16[128,2560]{1,0:T(8,128)(2,1)S(1)}, bf16[128,2560]{1,0:T(8,128)(2,1)S(1)}, u32[]{:S(2)}, u32[]{:S(2)}) %collective-permute-start) | collective-permute-done | bytes 655392 | tf_op jit(solution)/shard_map/ppermute | solution.py:419
  62.1 0.2 add.128
  62.4 3.5 %collective-permute-start.1 = (bf16[128,2560]{1,0:T(8,128)(2,1)S(1)}, bf16[128,2560]{1,0:T(8,128)(2,1)S(1)}, u32[]{:S(2)}, u32[]{:S(2)}) collective-permute-start(bf16[128,2560]{1,0:T(8,128)(2,1)S(1)} %get-tuple-element.14), channel_id=1, source_target_pairs={{0,3},{1,2},{2,1},{3,0},{4,5},{5,4},{6,7},{7,6},{8,11},{9,10},{10,... | collective-permute-start | bytes 1966088 | tf_op jit(solution)/shard_map/ppermute | solution.py:419
  66.1 1.2 collective-permute-start.5
  67.3 13.4 %collective-permute-done.1.got = bf16[128,2560]{1,0:T(8,128)(2,1)S(1)} collective-permute-done((bf16[128,2560]{1,0:T(8,128)(2,1)S(1)}, bf16[128,2560]{1,0:T(8,128)(2,1)S(1)}, u32[]{:S(2)}, u32[]{:S(2)}) %collective-permute-start.1) | collective-permute-done | bytes 655392 | tf_op jit(solution)/shard_map/ppermute | solution.py:419
  80.9 1.9 %collective-permute-start.2 = (bf16[128,2560]{1,0:T(8,128)(2,1)S(1)}, bf16[128,2560]{1,0:T(8,128)(2,1)S(1)}, u32[]{:S(2)}, u32[]{:S(2)}) collective-permute-start(bf16[128,2560]{1,0:T(8,128)(2,1)S(1)} %scale.2.mine), channel_id=1, source_target_pairs={{0,1},{1,0},{2,3},{3,2},{4,7},{5,6},{6,5},{7,4},{8,9},{9,8},{10,11... | collective-permute-start | bytes 1966088 | tf_op jit(solution)/shard_map/ppermute | solution.py:419
  82.8 5.7 %backward.2.refs_0_ = bf16[32,40,1024]{2,1,0:T(8,128)(2,1)} custom-call(s32[15]{0:T(128)S(1)} %concatenate.25.meta, f32[2]{0:T(128)S(1)} %get-tuple-element.24.rate, f32[1,2688]{1,0:T(1,128)S(1)} %bitcast.23, bf16[128,2560]{1,0:T(8,128)(2,1)S(1)} %scale.3.mine, bf16[128,2560]{1,0:T(8,128)(2,1)S(1)} %collective-permute-done.5.theirs, ...), custom_call_target="tpu_custom_call" | custom-call | tf_op jit(solution)/shard_map/backward/pallas_call | solution.py:334
  88.5 3.0 %collective-permute-done.2.theirs = bf16[128,2560]{1,0:T(8,128)(2,1)S(1)} collective-permute-done((bf16[128,2560]{1,0:T(8,128)(2,1)S(1)}, bf16[128,2560]{1,0:T(8,128)(2,1)S(1)}, u32[]{:S(2)}, u32[]{:S(2)}) %collective-permute-start.2) | collective-permute-done | bytes 655392 | tf_op jit(solution)/shard_map/ppermute | solution.py:419
  91.6 5.5 %backward.3 = bf16[32,40,1024]{2,1,0:T(8,128)(2,1)} custom-call(s32[15]{0:T(128)S(1)} %concatenate.25.meta, f32[2]{0:T(128)S(1)} %get-tuple-element.25.rate, f32[1,2688]{1,0:T(1,128)S(1)} %bitcast.24, bf16[128,2560]{1,0:T(8,128)(2,1)S(1)} %scale.2.mine, bf16[128,2560]{1,0:T(8,128)(2,1)S(1)} %collective-permute-done.2.theirs, ...), custom_call_target="tpu_custom_call", output_to_operand_aliasing={{}: (7, {})} | custom-call | tf_op jit(solution)/shard_map/backward/pallas_call | solution.py:334
  97.1 38.3 %all_to_all.10.payload = bf16[32,40,1024]{2,1,0:T(8,128)(2,1)S(1)} all-to-all(bf16[32,40,1024]{2,1,0:T(8,128)(2,1)} %backward.3), channel_id=1, replica_groups=mesh['ma'=32,'oct'=4] {'ma'}, dimensions={0} | all-to-all | bytes 5242880 | tf_op jit(solution)/shard_map/all_to_all | solution.py:449
  135.4 2.6 %unpack.1 = (bf16[20,64,512]{2,1,0:T(8,128)(2,1)}, bf16[20,64,512]{2,1,0:T(8,128)(2,1)}) custom-call(bf16[32,40,1024]{2,1,0:T(8,128)(2,1)S(1)} %all_to_all.10.payload), custom_call_target="tpu_custom_call" | custom-call | tf_op jit(solution)/shard_map/unpack/pallas_call | solution.py:125
  (39 shorter events, 1.4 us)
Async XLA Ops:
  3.8 7.6 %copy-start.2 = (s32[2]{0:T(128)S(1)}, s32[2]{0:T(128)}, u32[]{:S(2)}) copy-start(s32[2]{0:T(128)} %param.10) | copy-start | bytes 28
  3.8 13.6 %copy-start = (s32[2560]{0:T(1024)S(1)}, s32[2560]{0:T(1024)}, u32[]{:S(2)}) copy-start(s32[2560]{0:T(1024)} %param.11) | copy-start | bytes 30724
  3.8 14.5 %copy-start.1 = (f32[640]{0:T(1024)S(1)}, f32[640]{0:T(1024)}, u32[]{:S(2)}) copy-start(f32[640]{0:T(1024)} %param.7) | copy-start | bytes 7684
  3.8 28.3 %all-to-all-start = ((bf16[32,40,512]{2,1,0:T(8,128)(2,1)}), bf16[32,40,512]{2,1,0:T(8,128)(2,1)S(1)}, u32[]{:S(2)}, u32[]{:S(2)}) async-start(bf16[32,40,512]{2,1,0:T(8,128)(2,1)} %pack.1), calls=%async_computation | async-start | bytes 2621440 | tf_op jit(solution)/shard_map/all_to_all | solution.py:421
  38.4 10.7 %collective-permute-start.3 = (bf16[128,2560]{1,0:T(8,128)(2,1)S(1)}, bf16[128,2560]{1,0:T(8,128)(2,1)S(1)}, u32[]{:S(2)}, u32[]{:S(2)}) collective-permute-start(bf16[128,2560]{1,0:T(8,128)(2,1)S(1)} %get-tuple-element.17), channel_id=1, source_target_pairs={{0,1},{1,0},{2,3},{3,2},{4,7},{5,6},{6,5},{7,4},{8,9},{9,8},{10,11... | collective-permute-start | bytes 1966088 | tf_op jit(solution)/shard_map/ppermute | solution.py:419
  46.3 15.8 %collective-permute-start = (bf16[128,2560]{1,0:T(8,128)(2,1)S(1)}, bf16[128,2560]{1,0:T(8,128)(2,1)S(1)}, u32[]{:S(2)}, u32[]{:S(2)}) collective-permute-start(bf16[128,2560]{1,0:T(8,128)(2,1)S(1)} %get-tuple-element.12), channel_id=1, source_target_pairs={{0,1},{1,0},{2,3},{3,2},{4,7},{5,6},{6,5},{7,4},{8,9},{9,8},{10,11... | collective-permute-start | bytes 1966088 | tf_op jit(solution)/shard_map/ppermute | solution.py:419
  49.3 16.5 %collective-permute-start.4 = (bf16[128,2560]{1,0:T(8,128)(2,1)S(1)}, bf16[128,2560]{1,0:T(8,128)(2,1)S(1)}, u32[]{:S(2)}, u32[]{:S(2)}) collective-permute-start(bf16[128,2560]{1,0:T(8,128)(2,1)S(1)} %get-tuple-element.19), channel_id=1, source_target_pairs={{0,3},{1,2},{2,1},{3,0},{4,5},{5,4},{6,7},{7,6},{8,11},{9,10},{10,... | collective-permute-start | bytes 1966088 | tf_op jit(solution)/shard_map/ppermute | solution.py:419
  62.4 18.4 %collective-permute-start.1 = (bf16[128,2560]{1,0:T(8,128)(2,1)S(1)}, bf16[128,2560]{1,0:T(8,128)(2,1)S(1)}, u32[]{:S(2)}, u32[]{:S(2)}) collective-permute-start(bf16[128,2560]{1,0:T(8,128)(2,1)S(1)} %get-tuple-element.14), channel_id=1, source_target_pairs={{0,3},{1,2},{2,1},{3,0},{4,5},{5,4},{6,7},{7,6},{8,11},{9,10},{10,... | collective-permute-start | bytes 1966088 | tf_op jit(solution)/shard_map/ppermute | solution.py:419
  66.1 16.7 %collective-permute-start.5 = (bf16[128,2560]{1,0:T(8,128)(2,1)S(1)}, bf16[128,2560]{1,0:T(8,128)(2,1)S(1)}, u32[]{:S(2)}, u32[]{:S(2)}) collective-permute-start(bf16[128,2560]{1,0:T(8,128)(2,1)S(1)} %scale.3.mine), channel_id=1, source_target_pairs={{0,1},{1,0},{2,3},{3,2},{4,7},{5,6},{6,5},{7,4},{8,9},{9,8},{10,11... | collective-permute-start | bytes 1966088 | tf_op jit(solution)/shard_map/ppermute | solution.py:419
  80.9 10.7 %collective-permute-start.2 = (bf16[128,2560]{1,0:T(8,128)(2,1)S(1)}, bf16[128,2560]{1,0:T(8,128)(2,1)S(1)}, u32[]{:S(2)}, u32[]{:S(2)}) collective-permute-start(bf16[128,2560]{1,0:T(8,128)(2,1)S(1)} %scale.2.mine), channel_id=1, source_target_pairs={{0,1},{1,0},{2,3},{3,2},{4,7},{5,6},{6,5},{7,4},{8,9},{9,8},{10,11... | collective-permute-start | bytes 1966088 | tf_op jit(solution)/shard_map/ppermute | solution.py:419

commit v5 on v4

--- a/solution.py
+++ b/solution.py
@@ -16,6 +16,8 @@
 SENT = (KEPT - 1) * TILE
 HALF, ALL_FIRST, LANE, AT, AT_SENT = range(2 * SHARED, 2 * SHARED + 5)
 BLOCK = 512
+STREAM = 512
+N_BLOCKS = -(-KEPT * TILE // STREAM)
 BF16 = jnp.bfloat16
 F32 = jnp.float32
 LIMIT = 32 * 1024 * 1024
@@ -141,7 +143,7 @@
     return [pltpu.with_memory_space_constraint(x, pltpu.HBM) for x in arrays]
 
 
-def keep_kernel(meta, p_ref, h_ref, out_ref, kept, sems, out_sems):
+def keep_kernel(meta, select, p_ref, h_ref, out_ref, kept, moved, sems, out_sems):
     quarter, degrees = p_ref.shape[1:]
     pieces = [(0, degrees - SURE[0] * TILE, SURE[0], 0)]
     for k in range(SHARED):
@@ -160,34 +162,42 @@
     for at in range(2):
         for copy in copies[at * len(pieces):(at + 1) * len(pieces)]:
             copy.wait()
-        rows = pl.ds(at * quarter, quarter)
-        sent.append(pltpu.make_async_copy(kept.at[rows], out_ref.at[rows], out_sems.at[at]))
-        sent[at].start()
+        rows = slice(at * quarter, (at + 1) * quarter)
+        for n in range(N_BLOCKS):
+            start, size = n * STREAM, min(STREAM, KEPT * TILE - n * STREAM)
+            cols = slice(start, start + size)
+            moved[rows, cols] = dot(select[...], kept[rows, cols], NN).astype(BF16)
+            block = (pl.ds(at * quarter, quarter), pl.ds(start, size))
+            sent.append(pltpu.make_async_copy(moved.at[block], out_ref.at[block], out_sems.at[len(sent)]))
+            sent[-1].start()
     for copy in sent:
         copy.wait()
 
 
-def keep(meta, p_table, h_table):
+def keep(meta, select, p_table, h_table):
     shape = (2 * p_table.shape[1], KEPT * TILE)
     return call(
         keep_kernel,
         "keep",
         out_shape=pltpu.HBM(shape, BF16),
-        in_specs=[IN_SMEM] + [IN_PLACE] * 2,
+        in_specs=[IN_SMEM, IN_VMEM] + [IN_PLACE] * 2,
         out_specs=IN_PLACE,
         scratch_shapes=[
             pltpu.VMEM(shape, BF16),
+            pltpu.VMEM(shape, BF16),
             pltpu.SemaphoreType.DMA((2 * (2 + SHARED),)),
-            pltpu.SemaphoreType.DMA((2,)),
+            pltpu.SemaphoreType.DMA((2 * N_BLOCKS,)),
         ],
-    )(meta, *in_hbm(p_table, h_table))
-
-
-STREAM = 512
-N_BLOCKS = -(-KEPT * TILE // STREAM)
-
-
-def forward_kernel(part, meta, rate, mask, weight, recv, select, table, factor, keep, send, *refs):
+    )(meta, select, *in_hbm(p_table, h_table))
+
+
+def last_rows(slot, owners):
+    i = lax.broadcasted_iota(jnp.int32, (4 * owners, 1), 0)
+    hit = ((i >> 2) << 3) + (i & 3) + 4 * slot == lax.broadcasted_iota(jnp.int32, (4 * owners, 8 * owners), 1)
+    return jnp.where(hit, 1.0, 0.0).astype(BF16)
+
+
+def forward_kernel(part, meta, rate, mask, weight, recv, table, factor, keep, send, *refs):
     del factor
     owners, both, width = recv.shape
     source, (table, wind, spec, sems) = table, refs
@@ -197,16 +207,17 @@
         copies.append(pltpu.make_async_copy(source.at[:, cols], table.at[:, cols], sems.at[n]))
         copies[n].start()
     waited = 0
-    quarter = select.shape[2]
+    quarter = weight.shape[0]
     levels = width // 4
     main = owners * 16
     columns = [slice(at * levels, (at + 1) * levels) for at in (part, 3 - part)]
     mixed = [recv[:, 32:, cols].astype(F32).reshape(owners * 8, levels).astype(BF16) for cols in columns]
+    mixed = jnp.concatenate(mixed, axis=1)
     for slot in range(2):
-        rows = [recv[:, 16 * slot:16 * slot + 16, cols].reshape(main, levels) for cols in columns]
-        by_lat = dot(jnp.concatenate(rows, axis=1), select[slot, :main], TN)
-        by_lat = by_lat + dot(jnp.concatenate(mixed, axis=1), select[slot, main:], TN)
-        wind[slot] = (by_lat * weight[...]).astype(BF16)
+        rows = [recv[:, 16 * slot:16 * slot + 16, cols].reshape(main, levels).astype(F32) for cols in columns]
+        rows = [jnp.concatenate(rows, axis=1), dot(last_rows(slot, owners), mixed, NN)]
+        weighted = jnp.concatenate(rows, axis=0) * weight[...]
+        wind[slot] = weighted.T.astype(BF16)
     split = (SURE[0] + SHARED) * TILE
     for slot in range(2):
         low, high = (0, split) if slot == 0 else (SURE[0] * TILE, KEPT * TILE)
@@ -240,10 +251,10 @@
         ref[:, CUT:] = spec[rows, CUT + TILE:].astype(ref.dtype)
 
 
-def forward(part, meta, rate, mask, weight, recv, select, table, factor):
+def forward(part, meta, rate, mask, weight, recv, table, factor):
     owners, both, width = recv.shape
     levels = width // 4
-    quarter = select.shape[2]
+    quarter = weight.shape[0]
     out_shape = [jax.ShapeDtypeStruct((levels, SENT), F32), jax.ShapeDtypeStruct((levels, SENT), BF16)]
     scratch = [
         pltpu.VMEM((2, 2 * levels, quarter), BF16),
@@ -254,18 +265,18 @@
     return call(
         functools.partial(forward_kernel, part),
         "forward",
-        in_specs=[IN_SMEM] * 2 + [IN_VMEM] * 4 + [IN_PLACE] * 2,
+        in_specs=[IN_SMEM] * 2 + [IN_VMEM] * 3 + [IN_PLACE] * 2,
         out_specs=[IN_VMEM] * len(out_shape),
         out_shape=out_shape,
         scratch_shapes=scratch,
         cost_estimate=pl.CostEstimate(flops=5 * 10**9, bytes_accessed=10**7, transcendentals=0),
-    )(meta, rate, mask, weight, recv, select, *in_hbm(table), factor)
-
-
-def backward_kernel(part, meta, rate, mask, mine, theirs, select, table, *refs):
-    out_ref, every, masked, winds, out, sems = refs[-6:]
+    )(meta, rate, mask, weight, recv, *in_hbm(table), factor)
+
+
+def backward_kernel(part, meta, rate, mask, mine, theirs, table, *refs):
+    out_ref, every, masked, last, out, sems = refs[-6:]
     levels = mine.shape[0]
-    quarter = select.shape[2]
+    quarter = table.shape[0] // 2
     owners, both, width = out.shape
     main = owners * 16
     split = (SURE[0] + SHARED) * TILE
@@ -304,48 +315,46 @@
         pot = masked[slot, :, :high - low]
         sums = [dot(table[n * quarter:(n + 1) * quarter, low:high], pot, NT) for n in range(2)]
         r = rate[slot]
-        winds[slot, :, :levels] = (-sums[1][:, :levels]).astype(BF16)
-        winds[slot, :, levels:2 * levels] = (-r * sums[0][:, levels:]).astype(BF16)
-        winds[slot, :, 2 * levels:3 * levels] = (r * sums[0][:, :levels]).astype(BF16)
-        winds[slot, :, 3 * levels:] = sums[1][:, levels:].astype(BF16)
-    copies = []
-    for n in range(2):
-        cols = slice(n * width // 2, (n + 1) * width // 2)
-        for slot in range(2):
-            moved = dot(select[slot, :main], winds[slot, :, cols], NN)
-            out[:, 16 * slot:16 * slot + 16, cols] = moved.astype(BF16).reshape(owners, 16, width // 2)
-        mixed = dot(select[0, main:], winds[0, :, cols], NN) + dot(select[1, main:], winds[1, :, cols], NN)
-        out[:, 32:, cols] = mixed.reshape(owners, 8, width // 2).astype(BF16)
-        copies.append(pltpu.make_async_copy(
-            out.at[:, :, pl.ds(n * width // 2, width // 2)],
-            out_ref.at[:, :, pl.ds(part * width + n * width // 2, width // 2)],
+        fields = (-sums[1][:, :levels], -r * sums[0][:, levels:], r * sums[0][:, :levels], sums[1][:, levels:])
+        for n, field in enumerate(fields):
+            field = field.astype(BF16)
+            cols = slice(n * levels, (n + 1) * levels)
+            out[:, 16 * slot:16 * slot + 16, cols] = field[:main].reshape(owners, 16, levels)
+            last[slot, :, cols] = field[main:]
+    mixed = dot(last_rows(0, owners), last[0], TN) + dot(last_rows(1, owners), last[1], TN)
+    out[:, 32:] = mixed.reshape(owners, 8, width).astype(BF16)
+    sent = []
+    for n in range(4):
+        some = owners // 4
+        sent.append(pltpu.make_async_copy(
+            out.at[pl.ds(n * some, some)],
+            out_ref.at[pl.ds(n * some, some), :, pl.ds(part * width, width)],
             sems.at[n],
         ))
-        copies[n].start()
-    for copy in copies:
+        sent[n].start()
+    for copy in sent:
         copy.wait()
 
 
-def backward(part, meta, rate, mask, mine, theirs, select, table, payload, filled=()):
-    quarter = select.shape[2]
+def backward(part, meta, rate, mask, mine, theirs, table, payload, filled=()):
     levels = mine.shape[0]
     owners, both, width = payload
     piece = (owners, both, width // 2)
     return call(
         functools.partial(backward_kernel, part),
         "backward",
-        in_specs=[IN_SMEM] * 2 + [IN_VMEM] * 5 + [IN_PLACE] * len(filled),
+        in_specs=[IN_SMEM] * 2 + [IN_VMEM] * 4 + [IN_PLACE] * len(filled),
         out_specs=IN_PLACE,
         out_shape=pltpu.HBM(payload, BF16),
-        input_output_aliases={7: 0} if filled else {},
+        input_output_aliases={6: 0} if filled else {},
         scratch_shapes=[
             pltpu.VMEM((2 * levels, SENT), BF16),
             pltpu.VMEM((2, 2 * levels, (SURE[0] + SHARED) * TILE), BF16),
-            pltpu.VMEM((2, quarter, width // 2), BF16),
+            pltpu.VMEM((2, owners * 4, width // 2), BF16),
             pltpu.VMEM(piece, BF16),
-            pltpu.SemaphoreType.DMA((2,)),
+            pltpu.SemaphoreType.DMA((4,)),
         ],
-    )(meta, rate, mask, mine, theirs, select, table, *filled)
+    )(meta, rate, mask, mine, theirs, table, *filled)
 
 
 def add_kernel(kept, got, total, sent):
@@ -424,28 +433,22 @@
     rate = wavenumbers.astype(F32) / LMAX
 
     local = lax.dynamic_index_in_dim(row_latitude.reshape(owners, groups, rows), me, 1, keepdims=False) - me * quarter
-    none = jnp.full((owners, 4), -1, jnp.int32)
-    main, last = local[:, :16].reshape(-1), local[:, 16:]
-    target = jnp.stack([
-        jnp.concatenate([main, jnp.concatenate([last, none], axis=1).reshape(-1)]),
-        jnp.concatenate([main, jnp.concatenate([none, last], axis=1).reshape(-1)]),
-    ])
-    select = (target[:, :, None] == jnp.arange(quarter)[None, None, :]).astype(BF16)
-    weight = quad_weight.reshape(1, -1)
-
-    table = keep(meta, p_table, h_table)
+    target = jnp.concatenate([local[:, :16].reshape(-1), local[:, 16:].reshape(-1)])[:, None]
+    hit = target == jnp.arange(quarter)[None, :]
+    weight = jnp.sum(jnp.where(hit, quad_weight[None, :], 0.0), axis=1, keepdims=True)
+    table = keep(meta, hit.astype(BF16), p_table, h_table)
     owners, both, width = received.shape
     payload = (owners, both, 2 * width)
     signs = (rate, -rate)
-    kept_a, sent_a = forward(0, meta, signs[0], mask, weight, received, select, table, factor)
-    kept_b, sent_b, table = forward(1, meta, signs[1], mask, weight, received, select, table, factor)
+    kept_a, sent_a = forward(0, meta, signs[0], mask, weight, received, table, factor)
+    kept_b, sent_b, table = forward(1, meta, signs[1], mask, weight, received, table, factor)
     table = pltpu.with_memory_space_constraint(table, pltpu.VMEM)
     kept_a, sent_a = add(kept_a, swap(sent_a, first))
     kept_b, sent_b = add(kept_b, swap(sent_b, first))
     mine_a = scale(kept_a, swap(sent_a, second), factor)
     mine_b = scale(kept_b, swap(sent_b, second), factor)
-    out = backward(0, meta, signs[0], mask, mine_a, swap(mine_a, first), select, table, payload)
-    out = backward(1, meta, signs[1], mask, mine_b, swap(mine_b, first), select, table, payload, (out,))
+    out = backward(0, meta, signs[0], mask, mine_a, swap(mine_a, first), table, payload)
+    out = backward(1, meta, signs[1], mask, mine_b, swap(mine_b, first), table, payload, (out,))
     return tuple(unpack(lax.all_to_all(out, "ma", 0, 0, tiled=True), rows))
 
 

time: 140 us -> 139 us (level)
  waiting for transfers between devices: 35.1 us -> 32.2 us
  Pallas kernels: 35.7 us -> 37.4 us
    pallas_call x1, Pallas kernels: 5.78 us -> 9.53 us  [keep(): call(keep_kernel, 'keep', out_shape=pltpu.HBM(shape, BF16), in_specs=[IN_...]
    all_to_all x1, waiting for transfers between devices: 7.29 us -> 3.69 us  [on_device(): received = lax.all_to_all(pack(fourier_wind), 'ma', 0, 0, tiled=True)]
    pallas_call x2, Pallas kernels: 11.2 us -> 9.49 us  [backward(): call(functools.partial(backward_kernel, part), 'backward', in_specs=[IN_S...]
  transfers between devices with their start and end apart: 7 -> 7, of which waited for: 5 -> 5; matrix products, arithmetic and copies ran while one was open for 1% -> 2% of each run, Pallas kernels for 13% -> 15%
where the time goes in v5:
time: 139 us; the launch traced here: 137 us
  blocking collectives  38.3 us (28%)
  Pallas kernels  37.4 us (27%)
  waiting for transfers between devices  32.2 us (23%)
  starting transfers between devices  20.9 us (15%)
  between operations  6.25 us (4%)
    all_to_all x1, blocking collectives, on_device(): return tuple(unpack(lax.all_to_all(out, 'ma', 0, 0, tiled=True), rows))  38.3 us
    ppermute x6, waiting for transfers between devices, swap(): return lax.ppermute(x, ('ma', 'oct'), pairs)  28.6 us
    ppermute x6, starting transfers between devices, swap(): return lax.ppermute(x, ('ma', 'oct'), pairs)  13.3 us
    pallas_call x2, Pallas kernels, forward(): call(functools.partial(forward_kernel, part), 'forward', in_specs=[IN_SME...  11.9 us
    pallas_call x1, Pallas kernels, keep(): call(keep_kernel, 'keep', out_shape=pltpu.HBM(shape, BF16), in_specs=[IN_...  9.53 us
    pallas_call x2, Pallas kernels, backward(): call(functools.partial(backward_kernel, part), 'backward', in_specs=[IN_S...  9.49 us
    all_to_all x1, starting transfers between devices, on_device(): received = lax.all_to_all(pack(fourier_wind), 'ma', 0, 0, tiled=True)  7.54 us
    all_to_all x1, waiting for transfers between devices, on_device(): received = lax.all_to_all(pack(fourier_wind), 'ma', 0, 0, tiled=True)  3.69 us
  transfers between devices with their start and end apart: 7, of which 5 were waited for; matrix products, arithmetic and copies ran while one was open for 2% of the time, Pallas kernels for 15%

profile of v5, /device:TPU:0, one launch (start us, length us, event | category | flops | bytes accessed | tf_op | source)
XLA Modules:
  0.0 137.3 jit_solution(5722610302986616692)
XLA Ops:
  0.6 3.1 %pack.1 = bf16[32,40,512]{2,1,0:T(8,128)(2,1)} custom-call(bf16[20,64,512]{2,1,0:T(8,128)(2,1)} %wind_ref.1), custom_call_target="tpu_custom_call" | custom-call | tf_op jit(solution)/shard_map/pack/pallas_call | solution.py:75
  3.8 7.5 %all-to-all-start = ((bf16[32,40,512]{2,1,0:T(8,128)(2,1)}), bf16[32,40,512]{2,1,0:T(8,128)(2,1)S(1)}, u32[]{:S(2)}, u32[]{:S(2)}) async-start(bf16[32,40,512]{2,1,0:T(8,128)(2,1)} %pack.1), calls=%async_computation | async-start | bytes 2621440 | tf_op jit(solution)/shard_map/all_to_all | solution.py:430
  11.3 0.6 fusion.6
  18.0 0.3 select_reduce_fusion
  18.7 9.5 %keep.1.table = bf16[1280,2688]{1,0:T(8,128)(2,1)} custom-call(s32[15]{0:T(128)S(1)} %concatenate.16.meta, bf16[640,640]{1,0:T(8,128)(2,1)S(1)} %fusion.select, bf16[2,640,2560]{2,1,0:T(8,128)(2,1)} %p_ref.1, bf16[2,640,2560]{2,1,0:T(8,128)(2,1)} %h_ref.1), custom_call_target="tpu_custom_call" | custom-call | tf_op jit(solution)/shard_map/keep/pallas_call | solution.py:179
  28.4 3.7 %all-to-all-done.recv = bf16[32,40,512]{2,1,0:T(8,128)(2,1)S(1)} async-done(((bf16[32,40,512]{2,1,0:T(8,128)(2,1)}), bf16[32,40,512]{2,1,0:T(8,128)(2,1)S(1)}, u32[]{:S(2)}, u32[]{:S(2)}) %all-to-all-start) | async-done | bytes 1310752 | tf_op jit(solution)/shard_map/all_to_all | solution.py:430
  32.1 6.1 %forward.3 = (f32[128,2560]{1,0:T(8,128)S(1)}, bf16[128,2560]{1,0:T(8,128)(2,1)S(1)}) custom-call(s32[15]{0:T(128)S(1)} %concatenate.16.meta, f32[2]{0:T(128)S(1)} %get-tuple-element.20.rate, f32[1,2688]{1,0:T(1,128)S(1)} %bitcast.21, f32[640,1]{1,0:T(8,128)S(1)} %broadcast_in_dim.44.weight, bf16[32,40,512]{2,1,0:T(8,128)(2,1)S(1)} %all-to-all-done.recv, ...), custom_call_target="tpu_custom_call" | custom-call | flops 5000000000 | bytes 10000000 | tf_op jit(solution)/shard_map/forward/pallas_call | solution.py:265
  38.2 2.0 %collective-permute-start.3 = (bf16[128,2560]{1,0:T(8,128)(2,1)S(1)}, bf16[128,2560]{1,0:T(8,128)(2,1)S(1)}, u32[]{:S(2)}, u32[]{:S(2)}) collective-permute-start(bf16[128,2560]{1,0:T(8,128)(2,1)S(1)} %get-tuple-element.17), channel_id=1, source_target_pairs={{0,1},{1,0},{2,3},{3,2},{4,7},{5,6},{6,5},{7,4},{8,9},{9,8},{10,11... | collective-permute-start | bytes 1966088 | tf_op jit(solution)/shard_map/ppermute | solution.py:428
  40.2 5.8 %forward.2 = (f32[128,2560]{1,0:T(8,128)S(1)}, bf16[128,2560]{1,0:T(8,128)(2,1)S(1)}, bf16[1280,2688]{1,0:T(8,128)(2,1)S(1)}) custom-call(s32[15]{0:T(128)S(1)} %concatenate.16.meta, f32[2]{0:T(128)S(1)} %get-tuple-element.21.rate, f32[1,2688]{1,0:T(1,128)S(1)} %bitcast.22, f32[640,1]{1,0:T(8,128)S(1)} %broadcast_in_dim.44.weight, ...), custom_call_target="tpu_custom_call" | custom-call | flops 5000000000 | bytes 10000000 | tf_op jit(solution)/shard_map/forward/pallas_call | solution.py:265
  46.1 0.4 collective-permute-start
  46.4 2.5 %collective-permute-done.3.got = bf16[128,2560]{1,0:T(8,128)(2,1)S(1)} collective-permute-done((bf16[128,2560]{1,0:T(8,128)(2,1)S(1)}, bf16[128,2560]{1,0:T(8,128)(2,1)S(1)}, u32[]{:S(2)}, u32[]{:S(2)}) %collective-permute-start.3) | collective-permute-done | bytes 655392 | tf_op jit(solution)/shard_map/ppermute | solution.py:428
  48.9 0.2 add.121
  49.1 4.1 %collective-permute-start.4 = (bf16[128,2560]{1,0:T(8,128)(2,1)S(1)}, bf16[128,2560]{1,0:T(8,128)(2,1)S(1)}, u32[]{:S(2)}, u32[]{:S(2)}) collective-permute-start(bf16[128,2560]{1,0:T(8,128)(2,1)S(1)} %get-tuple-element.19), channel_id=1, source_target_pairs={{0,3},{1,2},{2,1},{3,0},{4,5},{5,4},{6,7},{7,6},{8,11},{9,10},{10,... | collective-permute-start | bytes 1966088 | tf_op jit(solution)/shard_map/ppermute | solution.py:428
  53.2 9.0 %collective-permute-done.got = bf16[128,2560]{1,0:T(8,128)(2,1)S(1)} collective-permute-done((bf16[128,2560]{1,0:T(8,128)(2,1)S(1)}, bf16[128,2560]{1,0:T(8,128)(2,1)S(1)}, u32[]{:S(2)}, u32[]{:S(2)}) %collective-permute-start) | collective-permute-done | bytes 655392 | tf_op jit(solution)/shard_map/ppermute | solution.py:428
  62.3 0.2 add.120
  62.5 3.2 %collective-permute-start.1 = (bf16[128,2560]{1,0:T(8,128)(2,1)S(1)}, bf16[128,2560]{1,0:T(8,128)(2,1)S(1)}, u32[]{:S(2)}, u32[]{:S(2)}) collective-permute-start(bf16[128,2560]{1,0:T(8,128)(2,1)S(1)} %get-tuple-element.14), channel_id=1, source_target_pairs={{0,3},{1,2},{2,1},{3,0},{4,5},{5,4},{6,7},{7,6},{8,11},{9,10},{10,... | collective-permute-start | bytes 1966088 | tf_op jit(solution)/shard_map/ppermute | solution.py:428
  65.9 1.5 %collective-permute-start.5 = (bf16[128,2560]{1,0:T(8,128)(2,1)S(1)}, bf16[128,2560]{1,0:T(8,128)(2,1)S(1)}, u32[]{:S(2)}, u32[]{:S(2)}) collective-permute-start(bf16[128,2560]{1,0:T(8,128)(2,1)S(1)} %scale.3.mine), channel_id=1, source_target_pairs={{0,1},{1,0},{2,3},{3,2},{4,7},{5,6},{6,5},{7,4},{8,9},{9,8},{10,11... | collective-permute-start | bytes 1966088 | tf_op jit(solution)/shard_map/ppermute | solution.py:428
  67.4 13.3 %collective-permute-done.1.got = bf16[128,2560]{1,0:T(8,128)(2,1)S(1)} collective-permute-done((bf16[128,2560]{1,0:T(8,128)(2,1)S(1)}, bf16[128,2560]{1,0:T(8,128)(2,1)S(1)}, u32[]{:S(2)}, u32[]{:S(2)}) %collective-permute-start.1) | collective-permute-done | bytes 655392 | tf_op jit(solution)/shard_map/ppermute | solution.py:428
  80.8 2.1 %collective-permute-start.2 = (bf16[128,2560]{1,0:T(8,128)(2,1)S(1)}, bf16[128,2560]{1,0:T(8,128)(2,1)S(1)}, u32[]{:S(2)}, u32[]{:S(2)}) collective-permute-start(bf16[128,2560]{1,0:T(8,128)(2,1)S(1)} %scale.2.mine), channel_id=1, source_target_pairs={{0,1},{1,0},{2,3},{3,2},{4,7},{5,6},{6,5},{7,4},{8,9},{9,8},{10,11... | collective-permute-start | bytes 1966088 | tf_op jit(solution)/shard_map/ppermute | solution.py:428
  83.0 4.7 %backward.2.refs_0_ = bf16[32,40,1024]{2,1,0:T(8,128)(2,1)} custom-call(s32[15]{0:T(128)S(1)} %concatenate.16.meta, f32[2]{0:T(128)S(1)} %get-tuple-element.20.rate, f32[1,2688]{1,0:T(1,128)S(1)} %bitcast.23, bf16[128,2560]{1,0:T(8,128)(2,1)S(1)} %scale.3.mine, bf16[128,2560]{1,0:T(8,128)(2,1)S(1)} %collective-permute-done.5.theirs, ...), custom_call_target="tpu_custom_call" | custom-call | tf_op jit(solution)/shard_map/backward/pallas_call | solution.py:343
  87.7 3.8 %collective-permute-done.2.theirs = bf16[128,2560]{1,0:T(8,128)(2,1)S(1)} collective-permute-done((bf16[128,2560]{1,0:T(8,128)(2,1)S(1)}, bf16[128,2560]{1,0:T(8,128)(2,1)S(1)}, u32[]{:S(2)}, u32[]{:S(2)}) %collective-permute-start.2) | collective-permute-done | bytes 655392 | tf_op jit(solution)/shard_map/ppermute | solution.py:428
  91.5 4.7 %backward.3 = bf16[32,40,1024]{2,1,0:T(8,128)(2,1)} custom-call(s32[15]{0:T(128)S(1)} %concatenate.16.meta, f32[2]{0:T(128)S(1)} %get-tuple-element.21.rate, f32[1,2688]{1,0:T(1,128)S(1)} %bitcast.24, bf16[128,2560]{1,0:T(8,128)(2,1)S(1)} %scale.2.mine, bf16[128,2560]{1,0:T(8,128)(2,1)S(1)} %collective-permute-done.2.theirs, ...), custom_call_target="tpu_custom_call", output_to_operand_aliasing={{}: (6, {})} | custom-call | tf_op jit(solution)/shard_map/backward/pallas_call | solution.py:343
  96.3 38.3 %all_to_all.10.payload = bf16[32,40,1024]{2,1,0:T(8,128)(2,1)S(1)} all-to-all(bf16[32,40,1024]{2,1,0:T(8,128)(2,1)} %backward.3), channel_id=1, replica_groups=mesh['ma'=32,'oct'=4] {'ma'}, dimensions={0} | all-to-all | bytes 5242880 | tf_op jit(solution)/shard_map/all_to_all | solution.py:452
  134.6 2.6 %unpack.1 = (bf16[20,64,512]{2,1,0:T(8,128)(2,1)}, bf16[20,64,512]{2,1,0:T(8,128)(2,1)}) custom-call(bf16[32,40,1024]{2,1,0:T(8,128)(2,1)S(1)} %all_to_all.10.payload), custom_call_target="tpu_custom_call" | custom-call | tf_op jit(solution)/shard_map/unpack/pallas_call | solution.py:127
  (35 shorter events, 1.6 us)
Async XLA Ops:
  3.8 7.6 %copy-start.2 = (s32[2]{0:T(128)S(1)}, s32[2]{0:T(128)}, u32[]{:S(2)}) copy-start(s32[2]{0:T(128)} %param.10) | copy-start | bytes 28
  3.8 13.3 %copy-start = (s32[2560]{0:T(1024)S(1)}, s32[2560]{0:T(1024)}, u32[]{:S(2)}) copy-start(s32[2560]{0:T(1024)} %param.11) | copy-start | bytes 30724
  3.8 14.2 %copy-start.1 = (f32[640]{0:T(1024)S(1)}, f32[640]{0:T(1024)}, u32[]{:S(2)}) copy-start(f32[640]{0:T(1024)} %param.7) | copy-start | bytes 7684
  3.8 28.3 %all-to-all-start = ((bf16[32,40,512]{2,1,0:T(8,128)(2,1)}), bf16[32,40,512]{2,1,0:T(8,128)(2,1)S(1)}, u32[]{:S(2)}, u32[]{:S(2)}) async-start(bf16[32,40,512]{2,1,0:T(8,128)(2,1)} %pack.1), calls=%async_computation | async-start | bytes 2621440 | tf_op jit(solution)/shard_map/all_to_all | solution.py:430
  38.2 10.7 %collective-permute-start.3 = (bf16[128,2560]{1,0:T(8,128)(2,1)S(1)}, bf16[128,2560]{1,0:T(8,128)(2,1)S(1)}, u32[]{:S(2)}, u32[]{:S(2)}) collective-permute-start(bf16[128,2560]{1,0:T(8,128)(2,1)S(1)} %get-tuple-element.17), channel_id=1, source_target_pairs={{0,1},{1,0},{2,3},{3,2},{4,7},{5,6},{6,5},{7,4},{8,9},{9,8},{10,11... | collective-permute-start | bytes 1966088 | tf_op jit(solution)/shard_map/ppermute | solution.py:428
  46.1 16.2 %collective-permute-start = (bf16[128,2560]{1,0:T(8,128)(2,1)S(1)}, bf16[128,2560]{1,0:T(8,128)(2,1)S(1)}, u32[]{:S(2)}, u32[]{:S(2)}) collective-permute-start(bf16[128,2560]{1,0:T(8,128)(2,1)S(1)} %get-tuple-element.12), channel_id=1, source_target_pairs={{0,1},{1,0},{2,3},{3,2},{4,7},{5,6},{6,5},{7,4},{8,9},{9,8},{10,11... | collective-permute-start | bytes 1966088 | tf_op jit(solution)/shard_map/ppermute | solution.py:428
  49.1 16.6 %collective-permute-start.4 = (bf16[128,2560]{1,0:T(8,128)(2,1)S(1)}, bf16[128,2560]{1,0:T(8,128)(2,1)S(1)}, u32[]{:S(2)}, u32[]{:S(2)}) collective-permute-start(bf16[128,2560]{1,0:T(8,128)(2,1)S(1)} %get-tuple-element.19), channel_id=1, source_target_pairs={{0,3},{1,2},{2,1},{3,0},{4,5},{5,4},{6,7},{7,6},{8,11},{9,10},{10,... | collective-permute-start | bytes 1966088 | tf_op jit(solution)/shard_map/ppermute | solution.py:428
  62.5 18.2 %collective-permute-start.1 = (bf16[128,2560]{1,0:T(8,128)(2,1)S(1)}, bf16[128,2560]{1,0:T(8,128)(2,1)S(1)}, u32[]{:S(2)}, u32[]{:S(2)}) collective-permute-start(bf16[128,2560]{1,0:T(8,128)(2,1)S(1)} %get-tuple-element.14), channel_id=1, source_target_pairs={{0,3},{1,2},{2,1},{3,0},{4,5},{5,4},{6,7},{7,6},{8,11},{9,10},{10,... | collective-permute-start | bytes 1966088 | tf_op jit(solution)/shard_map/ppermute | solution.py:428
  65.9 17.1 %collective-permute-start.5 = (bf16[128,2560]{1,0:T(8,128)(2,1)S(1)}, bf16[128,2560]{1,0:T(8,128)(2,1)S(1)}, u32[]{:S(2)}, u32[]{:S(2)}) collective-permute-start(bf16[128,2560]{1,0:T(8,128)(2,1)S(1)} %scale.3.mine), channel_id=1, source_target_pairs={{0,1},{1,0},{2,3},{3,2},{4,7},{5,6},{6,5},{7,4},{8,9},{9,8},{10,11... | collective-permute-start | bytes 1966088 | tf_op jit(solution)/shard_map/ppermute | solution.py:428
  80.8 10.7 %collective-permute-start.2 = (bf16[128,2560]{1,0:T(8,128)(2,1)S(1)}, bf16[128,2560]{1,0:T(8,128)(2,1)S(1)}, u32[]{:S(2)}, u32[]{:S(2)}) collective-permute-start(bf16[128,2560]{1,0:T(8,128)(2,1)S(1)} %scale.2.mine), channel_id=1, source_target_pairs={{0,1},{1,0},{2,3},{3,2},{4,7},{5,6},{6,5},{7,4},{8,9},{9,8},{10,11... | collective-permute-start | bytes 1966088 | tf_op jit(solution)/shard_map/ppermute | solution.py:428

commit v6 on v5

--- a/solution.py
+++ b/solution.py
@@ -273,17 +273,16 @@
     )(meta, rate, mask, weight, recv, *in_hbm(table), factor)
 
 
-def backward_kernel(part, meta, rate, mask, mine, theirs, table, *refs):
+def backward_kernel(meta, halves, rate, mask, first_part, second_part, table, *refs):
     out_ref, every, masked, last, out, sems = refs[-6:]
-    levels = mine.shape[0]
+    levels = first_part.shape[0]
     quarter = table.shape[0] // 2
-    owners, both, width = out.shape
+    owners = out.shape[1]
     main = owners * 16
     split = (SURE[0] + SHARED) * TILE
     degrees = KEPT * TILE
-    at = meta[HALF] * levels
-    every[pl.ds(pl.multiple_of(at, levels), levels), :] = mine[...]
-    every[pl.ds(pl.multiple_of(levels - at, levels), levels), :] = theirs[...]
+    every[:levels] = first_part[...]
+    every[levels:] = second_part[...]
     shared = slice(SURE[0] * TILE, split)
     cut = CUT - shared.start
     first = mask[:, shared.start:CUT] > 0.5
@@ -313,48 +312,46 @@
     for slot in range(2):
         low, high = (0, split) if slot == 0 else (shared.start, degrees)
         pot = masked[slot, :, :high - low]
-        sums = [dot(table[n * quarter:(n + 1) * quarter, low:high], pot, NT) for n in range(2)]
-        r = rate[slot]
-        fields = (-sums[1][:, :levels], -r * sums[0][:, levels:], r * sums[0][:, :levels], sums[1][:, levels:])
-        for n, field in enumerate(fields):
-            field = field.astype(BF16)
-            cols = slice(n * levels, (n + 1) * levels)
-            out[:, 16 * slot:16 * slot + 16, cols] = field[:main].reshape(owners, 16, levels)
-            last[slot, :, cols] = field[main:]
+        sum_p, sum_h = [dot(table[n * quarter:(n + 1) * quarter, low:high], pot, NT) for n in range(2)]
+        for part in range(2):
+            cols = slice(part * levels, (part + 1) * levels)
+            r = rate[slot] if part == 0 else -rate[slot]
+            p, h = r * sum_p[:, cols], sum_h[:, cols]
+            of_psi = halves[part] == 0
+            for n, field in enumerate((jnp.where(of_psi, -h, -p), jnp.where(of_psi, p, h))):
+                field = field.astype(BF16)
+                out[2 * part + n, :, 16 * slot:16 * slot + 16] = field[:main].reshape(owners, 16, levels)
+                last[slot, :, (2 * part + n) * levels:(2 * part + n + 1) * levels] = field[main:]
     mixed = dot(last_rows(0, owners), last[0], TN) + dot(last_rows(1, owners), last[1], TN)
-    out[:, 32:] = mixed.reshape(owners, 8, width).astype(BF16)
     sent = []
     for n in range(4):
-        some = owners // 4
-        sent.append(pltpu.make_async_copy(
-            out.at[pl.ds(n * some, some)],
-            out_ref.at[pl.ds(n * some, some), :, pl.ds(part * width, width)],
-            sems.at[n],
-        ))
+        some = mixed[:, n * levels:(n + 1) * levels]
+        out[n, :, 32:] = some.reshape(owners, 8, levels).astype(BF16)
+        column = pl.multiple_of((2 * n + halves[n // 2]) * levels, levels)
+        sent.append(pltpu.make_async_copy(out.at[n], out_ref.at[:, :, pl.ds(column, levels)], sems.at[n]))
         sent[n].start()
     for copy in sent:
         copy.wait()
 
 
-def backward(part, meta, rate, mask, mine, theirs, table, payload, filled=()):
-    levels = mine.shape[0]
+def backward(meta, halves, rate, mask, first_part, second_part, table, payload, filled=()):
+    levels = first_part.shape[0]
     owners, both, width = payload
-    piece = (owners, both, width // 2)
-    return call(
-        functools.partial(backward_kernel, part),
+    return call(
+        backward_kernel,
         "backward",
-        in_specs=[IN_SMEM] * 2 + [IN_VMEM] * 4 + [IN_PLACE] * len(filled),
+        in_specs=[IN_SMEM] * 3 + [IN_VMEM] * 4 + [IN_PLACE] * len(filled),
         out_specs=IN_PLACE,
         out_shape=pltpu.HBM(payload, BF16),
-        input_output_aliases={6: 0} if filled else {},
+        input_output_aliases={7: 0} if filled else {},
         scratch_shapes=[
             pltpu.VMEM((2 * levels, SENT), BF16),
             pltpu.VMEM((2, 2 * levels, (SURE[0] + SHARED) * TILE), BF16),
-            pltpu.VMEM((2, owners * 4, width // 2), BF16),
-            pltpu.VMEM(piece, BF16),
+            pltpu.VMEM((2, owners * 4, 4 * levels), BF16),
+            pltpu.VMEM((4, owners, both, levels), BF16),
             pltpu.SemaphoreType.DMA((4,)),
         ],
-    )(meta, rate, mask, mine, theirs, table, *filled)
+    )(meta, halves, rate, mask, first_part, second_part, table, *filled)
 
 
 def add_kernel(kept, got, total, sent):
@@ -418,18 +415,22 @@
     quarter = p_table.shape[1]
     count = p_table.shape[2] // TILE
     flip, turn = [z ^ 1 for z in range(groups)], [groups - 1 - z for z in range(groups)]
-    first = [
-        (d * groups + z, d * groups + (flip, turn)[d % 2][z]) for d in range(owners) for z in range(groups)]
-    second = [
-        (d * groups + z, d * groups + (turn, flip)[d % 2][z]) for d in range(owners) for z in range(groups)]
-    half = jnp.where(lax.axis_index("ma") % 2 == 0, ((me + 1) // 2) % 2, me // 2)
+    ways = [
+        [(d * groups + z, d * groups + (flip, turn)[(d + n) % 2][z]) for d in range(owners) for z in range(groups)]
+        for n in range(2)]
+    halves = ((me + 1) // 2) % 2, me // 2
+    odd = lax.axis_index("ma") % 2
 
     def swap(x, pairs):
         return lax.ppermute(x, ("ma", "oct"), pairs)
 
     received = lax.all_to_all(pack(fourier_wind), "ma", 0, 0, tiled=True)
 
-    meta, mask, factor = layout(wavenumbers, count, half)
+    metas = []
+    for n in range(2):
+        half = jnp.where(odd == n, *halves)
+        meta, mask, factor = layout(wavenumbers, count, half)
+        metas.append(meta)
     rate = wavenumbers.astype(F32) / LMAX
 
     local = lax.dynamic_index_in_dim(row_latitude.reshape(owners, groups, rows), me, 1, keepdims=False) - me * quarter
@@ -440,15 +441,17 @@
     owners, both, width = received.shape
     payload = (owners, both, 2 * width)
     signs = (rate, -rate)
-    kept_a, sent_a = forward(0, meta, signs[0], mask, weight, received, table, factor)
-    kept_b, sent_b, table = forward(1, meta, signs[1], mask, weight, received, table, factor)
+    kept_a, sent_a = forward(0, metas[0], signs[0], mask, weight, received, table, factor)
+    kept_b, sent_b, table = forward(1, metas[1], signs[1], mask, weight, received, table, factor)
     table = pltpu.with_memory_space_constraint(table, pltpu.VMEM)
-    kept_a, sent_a = add(kept_a, swap(sent_a, first))
-    kept_b, sent_b = add(kept_b, swap(sent_b, first))
-    mine_a = scale(kept_a, swap(sent_a, second), factor)
-    mine_b = scale(kept_b, swap(sent_b, second), factor)
-    out = backward(0, meta, signs[0], mask, mine_a, swap(mine_a, first), table, payload)
-    out = backward(1, meta, signs[1], mask, mine_b, swap(mine_b, first), table, payload, (out,))
+    kept_a, sent_a = add(kept_a, swap(sent_a, ways[0]))
+    kept_b, sent_b = add(kept_b, swap(sent_b, ways[1]))
+    mine_a = scale(kept_a, swap(sent_a, ways[1]), factor)
+    mine_b = scale(kept_b, swap(sent_b, ways[0]), factor)
+    theirs_a, theirs_b = swap(mine_a, ways[0]), swap(mine_b, ways[1])
+    halves = jnp.stack([meta[HALF] for meta in metas])
+    out = backward(metas[0], halves, rate, mask, mine_a, mine_b, table, payload)
+    out = backward(metas[0], 1 - halves, rate, mask, theirs_a, theirs_b, table, payload, (out,))
     return tuple(unpack(lax.all_to_all(out, "ma", 0, 0, tiled=True), rows))
 
 

time: 139 us -> 133 us (0.957)
  waiting for transfers between devices: 32.2 us -> 23.7 us
  starting transfers between devices: 20.9 us -> 24.1 us
    ppermute x6, waiting for transfers between devices: 28.6 us -> 20 us  [swap(): return lax.ppermute(x, ('ma', 'oct'), pairs)]
    ppermute x6, starting transfers between devices: 13.3 us -> 16.5 us  [swap(): return lax.ppermute(x, ('ma', 'oct'), pairs)]
  transfers between devices with their start and end apart: 7 -> 7, of which waited for: 5 -> 7; matrix products, arithmetic and copies ran while one was open for 2% -> 2% of each run, Pallas kernels for 15% -> 16%
where the time goes in v6:
time: 133 us; the launch traced here: 132 us
  blocking collectives  38.3 us (29%)
  Pallas kernels  37.3 us (28%)
  starting transfers between devices  24.1 us (18%)
  waiting for transfers between devices  23.7 us (18%)
  between operations  6.21 us (5%)
  local copies, waits for them, and re-layouts  1.38 us (1%)
    all_to_all x1, blocking collectives, on_device(): return tuple(unpack(lax.all_to_all(out, 'ma', 0, 0, tiled=True), rows))  38.3 us
    ppermute x6, waiting for transfers between devices, swap(): return lax.ppermute(x, ('ma', 'oct'), pairs)  20 us
    ppermute x6, starting transfers between devices, swap(): return lax.ppermute(x, ('ma', 'oct'), pairs)  16.5 us
    pallas_call x2, Pallas kernels, forward(): call(functools.partial(forward_kernel, part), 'forward', in_specs=[IN_SME...  11.9 us
    pallas_call x1, Pallas kernels, keep(): call(keep_kernel, 'keep', out_shape=pltpu.HBM(shape, BF16), in_specs=[IN_...  9.51 us
    pallas_call x2, Pallas kernels, backward(): call(backward_kernel, 'backward', in_specs=[IN_SMEM] * 3 + [IN_VMEM] * 4...  9.4 us
    all_to_all x1, starting transfers between devices, on_device(): received = lax.all_to_all(pack(fourier_wind), 'ma', 0, 0, tiled=True)  7.54 us
    all_to_all x1, waiting for transfers between devices, on_device(): received = lax.all_to_all(pack(fourier_wind), 'ma', 0, 0, tiled=True)  3.68 us
  transfers between devices with their start and end apart: 7, of which 7 were waited for; matrix products, arithmetic and copies ran while one was open for 2% of the time, Pallas kernels for 16%

profile of v6, /device:TPU:0, one launch (start us, length us, event | category | flops | bytes accessed | tf_op | source)
XLA Modules:
  0.0 132.0 jit_solution(6464582630611466527)
XLA Ops:
  0.6 3.1 %pack.1 = bf16[32,40,512]{2,1,0:T(8,128)(2,1)} custom-call(bf16[20,64,512]{2,1,0:T(8,128)(2,1)} %wind_ref.1), custom_call_target="tpu_custom_call" | custom-call | tf_op jit(solution)/shard_map/pack/pallas_call | solution.py:75
  3.8 7.5 %all-to-all-start = ((bf16[32,40,512]{2,1,0:T(8,128)(2,1)}), bf16[32,40,512]{2,1,0:T(8,128)(2,1)S(1)}, u32[]{:S(2)}, u32[]{:S(2)}) async-start(bf16[32,40,512]{2,1,0:T(8,128)(2,1)} %pack.1), calls=%async_computation | async-start | bytes 2621440 | tf_op jit(solution)/shard_map/all_to_all | solution.py:427
  11.3 0.6 fusion.6
  17.9 0.3 select_reduce_fusion
  18.7 9.5 %keep.1.table = bf16[1280,2688]{1,0:T(8,128)(2,1)} custom-call(s32[15]{0:T(128)S(1)} %concatenate.22.meta, bf16[640,640]{1,0:T(8,128)(2,1)S(1)} %fusion.select, bf16[2,640,2560]{2,1,0:T(8,128)(2,1)} %p_ref.1, bf16[2,640,2560]{2,1,0:T(8,128)(2,1)} %h_ref.1), custom_call_target="tpu_custom_call" | custom-call | tf_op jit(solution)/shard_map/keep/pallas_call | solution.py:179
  28.4 3.7 %all-to-all-done.recv = bf16[32,40,512]{2,1,0:T(8,128)(2,1)S(1)} async-done(((bf16[32,40,512]{2,1,0:T(8,128)(2,1)}), bf16[32,40,512]{2,1,0:T(8,128)(2,1)S(1)}, u32[]{:S(2)}, u32[]{:S(2)}) %all-to-all-start) | async-done | bytes 1310752 | tf_op jit(solution)/shard_map/all_to_all | solution.py:427
  32.1 6.1 %forward.2 = (f32[128,2560]{1,0:T(8,128)S(1)}, bf16[128,2560]{1,0:T(8,128)(2,1)S(1)}) custom-call(s32[15]{0:T(128)S(1)} %concatenate.19.meta, f32[2]{0:T(128)S(1)} %get-tuple-element.23.rate, f32[1,2688]{1,0:T(1,128)S(1)} %bitcast.22, f32[640,1]{1,0:T(8,128)S(1)} %broadcast_in_dim.44.weight, bf16[32,40,512]{2,1,0:T(8,128)(2,1)S(1)} %all-to-all-done.recv, ...), custom_call_target="tpu_custom_call" | custom-call | flops 5000000000 | bytes 10000000 | tf_op jit(solution)/shard_map/forward/pallas_call | solution.py:265
  38.2 2.0 %collective-permute-start = (bf16[128,2560]{1,0:T(8,128)(2,1)S(1)}, bf16[128,2560]{1,0:T(8,128)(2,1)S(1)}, u32[]{:S(2)}, u32[]{:S(2)}) collective-permute-start(bf16[128,2560]{1,0:T(8,128)(2,1)S(1)} %get-tuple-element.12), channel_id=1, source_target_pairs={{0,1},{1,0},{2,3},{3,2},{4,7},{5,6},{6,5},{7,4},{8,9},{9,8},{10,11... | collective-permute-start | bytes 1966088 | tf_op jit(solution)/shard_map/ppermute | solution.py:425
  40.2 5.8 %forward.3 = (f32[128,2560]{1,0:T(8,128)S(1)}, bf16[128,2560]{1,0:T(8,128)(2,1)S(1)}, bf16[1280,2688]{1,0:T(8,128)(2,1)S(1)}) custom-call(s32[15]{0:T(128)S(1)} %concatenate.22.meta, f32[2]{0:T(128)S(1)} %get-tuple-element.22.rate, f32[1,2688]{1,0:T(1,128)S(1)} %bitcast.23, f32[640,1]{1,0:T(8,128)S(1)} %broadcast_in_dim.44.weight, ...), custom_call_target="tpu_custom_call" | custom-call | flops 5000000000 | bytes 10000000 | tf_op jit(solution)/shard_map/forward/pallas_call | solution.py:265
  46.1 2.8 %collective-permute-start.3 = (bf16[128,2560]{1,0:T(8,128)(2,1)S(1)}, bf16[128,2560]{1,0:T(8,128)(2,1)S(1)}, u32[]{:S(2)}, u32[]{:S(2)}) collective-permute-start(bf16[128,2560]{1,0:T(8,128)(2,1)S(1)} %get-tuple-element.16), channel_id=1, source_target_pairs={{0,3},{1,2},{2,1},{3,0},{4,5},{5,4},{6,7},{7,6},{8,11},{9,10},{10,... | collective-permute-start | bytes 1966088 | tf_op jit(solution)/shard_map/ppermute | solution.py:425
  48.9 0.6 collective-permute-done.got
  49.7 6.8 %collective-permute-start.1 = (bf16[128,2560]{1,0:T(8,128)(2,1)S(1)}, bf16[128,2560]{1,0:T(8,128)(2,1)S(1)}, u32[]{:S(2)}, u32[]{:S(2)}) collective-permute-start(bf16[128,2560]{1,0:T(8,128)(2,1)S(1)} %get-tuple-element.14), channel_id=1, source_target_pairs={{0,3},{1,2},{2,1},{3,0},{4,5},{5,4},{6,7},{7,6},{8,11},{9,10},{10,... | collective-permute-start | bytes 1966088 | tf_op jit(solution)/shard_map/ppermute | solution.py:425
  56.5 1.7 %collective-permute-done.3.got = bf16[128,2560]{1,0:T(8,128)(2,1)S(1)} collective-permute-done((bf16[128,2560]{1,0:T(8,128)(2,1)S(1)}, bf16[128,2560]{1,0:T(8,128)(2,1)S(1)}, u32[]{:S(2)}, u32[]{:S(2)}) %collective-permute-start.3) | collective-permute-done | bytes 655392 | tf_op jit(solution)/shard_map/ppermute | solution.py:425
  58.3 0.4 collective-permute-start.4
  58.7 10.3 %collective-permute-done.1.got = bf16[128,2560]{1,0:T(8,128)(2,1)S(1)} collective-permute-done((bf16[128,2560]{1,0:T(8,128)(2,1)S(1)}, bf16[128,2560]{1,0:T(8,128)(2,1)S(1)}, u32[]{:S(2)}, u32[]{:S(2)}) %collective-permute-start.1) | collective-permute-done | bytes 655392 | tf_op jit(solution)/shard_map/ppermute | solution.py:425
  69.2 0.9 collective-permute-start.2
  70.1 0.3 collective-permute-done.4.got
  70.6 3.7 %collective-permute-start.5 = (bf16[128,2560]{1,0:T(8,128)(2,1)S(1)}, bf16[128,2560]{1,0:T(8,128)(2,1)S(1)}, u32[]{:S(2)}, u32[]{:S(2)}) collective-permute-start(bf16[128,2560]{1,0:T(8,128)(2,1)S(1)} %scale.3.second_part), channel_id=1, source_target_pairs={{0,3},{1,2},{2,1},{3,0},{4,5},{5,4},{6,7},{7,6},{8,11},{9,10},{10,... | collective-permute-start | bytes 1966088 | tf_op jit(solution)/shard_map/ppermute | solution.py:425
  74.3 4.7 %backward.2.refs_0_ = bf16[32,40,1024]{2,1,0:T(8,128)(2,1)} custom-call(s32[15]{0:T(128)S(1)} %concatenate.19.meta, s32[2]{0:T(128)S(1)} %get-tuple-element.21.halves, f32[2]{0:T(128)S(1)} %get-tuple-element.23.rate, f32[1,2688]{1,0:T(1,128)S(1)} %bitcast.24, bf16[128,2560]{1,0:T(8,128)(2,1)S(1)} %scale.2.first_part, ...), custom_call_target="tpu_custom_call" | custom-call | tf_op jit(solution)/shard_map/backward/pallas_call | solution.py:340
  79.0 5.7 %collective-permute-done.2.first_part = bf16[128,2560]{1,0:T(8,128)(2,1)S(1)} collective-permute-done((bf16[128,2560]{1,0:T(8,128)(2,1)S(1)}, bf16[128,2560]{1,0:T(8,128)(2,1)S(1)}, u32[]{:S(2)}, u32[]{:S(2)}) %collective-permute-start.2) | collective-permute-done | bytes 655392 | tf_op jit(solution)/shard_map/ppermute | solution.py:425
  84.8 1.4 %collective-permute-done.5.second_part = bf16[128,2560]{1,0:T(8,128)(2,1)S(1)} collective-permute-done((bf16[128,2560]{1,0:T(8,128)(2,1)S(1)}, bf16[128,2560]{1,0:T(8,128)(2,1)S(1)}, u32[]{:S(2)}, u32[]{:S(2)}) %collective-permute-start.5) | collective-permute-done | bytes 655392 | tf_op jit(solution)/shard_map/ppermute | solution.py:425
  86.2 4.7 %backward.3 = bf16[32,40,1024]{2,1,0:T(8,128)(2,1)} custom-call(s32[15]{0:T(128)S(1)} %concatenate.19.meta, s32[2]{0:T(128)S(1)} %get-tuple-element.20.halves, f32[2]{0:T(128)S(1)} %get-tuple-element.23.rate, f32[1,2688]{1,0:T(1,128)S(1)} %bitcast.25, bf16[128,2560]{1,0:T(8,128)(2,1)S(1)} %collective-permute-done.2.first_part, ...), custom_call_target="tpu_custom_call", output_to_operand_aliasing={{}: (7, {})} | custom-call | tf_op jit(solution)/shard_map/backward/pallas_call | solution.py:340
  90.9 38.3 %all_to_all.10.payload = bf16[32,40,1024]{2,1,0:T(8,128)(2,1)S(1)} all-to-all(bf16[32,40,1024]{2,1,0:T(8,128)(2,1)} %backward.3), channel_id=1, replica_groups=mesh['ma'=32,'oct'=4] {'ma'}, dimensions={0} | all-to-all | bytes 5242880 | tf_op jit(solution)/shard_map/all_to_all | solution.py:455
  129.2 2.6 %unpack.1 = (bf16[20,64,512]{2,1,0:T(8,128)(2,1)}, bf16[20,64,512]{2,1,0:T(8,128)(2,1)}) custom-call(bf16[32,40,1024]{2,1,0:T(8,128)(2,1)S(1)} %all_to_all.10.payload), custom_call_target="tpu_custom_call" | custom-call | tf_op jit(solution)/shard_map/unpack/pallas_call | solution.py:127
  (37 shorter events, 2.2 us)
Async XLA Ops:
  3.8 7.6 %copy-start.2 = (s32[2]{0:T(128)S(1)}, s32[2]{0:T(128)}, u32[]{:S(2)}) copy-start(s32[2]{0:T(128)} %param.10) | copy-start | bytes 28
  3.8 13.5 %copy-start = (s32[2560]{0:T(1024)S(1)}, s32[2560]{0:T(1024)}, u32[]{:S(2)}) copy-start(s32[2560]{0:T(1024)} %param.11) | copy-start | bytes 30724
  3.8 14.1 %copy-start.1 = (f32[640]{0:T(1024)S(1)}, f32[640]{0:T(1024)}, u32[]{:S(2)}) copy-start(f32[640]{0:T(1024)} %param.7) | copy-start | bytes 7684
  3.8 28.3 %all-to-all-start = ((bf16[32,40,512]{2,1,0:T(8,128)(2,1)}), bf16[32,40,512]{2,1,0:T(8,128)(2,1)S(1)}, u32[]{:S(2)}, u32[]{:S(2)}) async-start(bf16[32,40,512]{2,1,0:T(8,128)(2,1)} %pack.1), calls=%async_computation | async-start | bytes 2621440 | tf_op jit(solution)/shard_map/all_to_all | solution.py:427
  38.2 11.2 %collective-permute-start = (bf16[128,2560]{1,0:T(8,128)(2,1)S(1)}, bf16[128,2560]{1,0:T(8,128)(2,1)S(1)}, u32[]{:S(2)}, u32[]{:S(2)}) collective-permute-start(bf16[128,2560]{1,0:T(8,128)(2,1)S(1)} %get-tuple-element.12), channel_id=1, source_target_pairs={{0,1},{1,0},{2,3},{3,2},{4,7},{5,6},{6,5},{7,4},{8,9},{9,8},{10,11... | collective-permute-start | bytes 1966088 | tf_op jit(solution)/shard_map/ppermute | solution.py:425
  46.1 12.1 %collective-permute-start.3 = (bf16[128,2560]{1,0:T(8,128)(2,1)S(1)}, bf16[128,2560]{1,0:T(8,128)(2,1)S(1)}, u32[]{:S(2)}, u32[]{:S(2)}) collective-permute-start(bf16[128,2560]{1,0:T(8,128)(2,1)S(1)} %get-tuple-element.16), channel_id=1, source_target_pairs={{0,3},{1,2},{2,1},{3,0},{4,5},{5,4},{6,7},{7,6},{8,11},{9,10},{10,... | collective-permute-start | bytes 1966088 | tf_op jit(solution)/shard_map/ppermute | solution.py:425
  49.7 19.3 %collective-permute-start.1 = (bf16[128,2560]{1,0:T(8,128)(2,1)S(1)}, bf16[128,2560]{1,0:T(8,128)(2,1)S(1)}, u32[]{:S(2)}, u32[]{:S(2)}) collective-permute-start(bf16[128,2560]{1,0:T(8,128)(2,1)S(1)} %get-tuple-element.14), channel_id=1, source_target_pairs={{0,3},{1,2},{2,1},{3,0},{4,5},{5,4},{6,7},{7,6},{8,11},{9,10},{10,... | collective-permute-start | bytes 1966088 | tf_op jit(solution)/shard_map/ppermute | solution.py:425
  58.3 12.1 %collective-permute-start.4 = (bf16[128,2560]{1,0:T(8,128)(2,1)S(1)}, bf16[128,2560]{1,0:T(8,128)(2,1)S(1)}, u32[]{:S(2)}, u32[]{:S(2)}) collective-permute-start(bf16[128,2560]{1,0:T(8,128)(2,1)S(1)} %get-tuple-element.18), channel_id=1, source_target_pairs={{0,1},{1,0},{2,3},{3,2},{4,7},{5,6},{6,5},{7,4},{8,9},{9,8},{10,11... | collective-permute-start | bytes 1966088 | tf_op jit(solution)/shard_map/ppermute | solution.py:425
  69.2 15.6 %collective-permute-start.2 = (bf16[128,2560]{1,0:T(8,128)(2,1)S(1)}, bf16[128,2560]{1,0:T(8,128)(2,1)S(1)}, u32[]{:S(2)}, u32[]{:S(2)}) collective-permute-start(bf16[128,2560]{1,0:T(8,128)(2,1)S(1)} %scale.2.first_part), channel_id=1, source_target_pairs={{0,1},{1,0},{2,3},{3,2},{4,7},{5,6},{6,5},{7,4},{8,9},{9,8},{10,11... | collective-permute-start | bytes 1966088 | tf_op jit(solution)/shard_map/ppermute | solution.py:425
  70.6 15.6 %collective-permute-start.5 = (bf16[128,2560]{1,0:T(8,128)(2,1)S(1)}, bf16[128,2560]{1,0:T(8,128)(2,1)S(1)}, u32[]{:S(2)}, u32[]{:S(2)}) collective-permute-start(bf16[128,2560]{1,0:T(8,128)(2,1)S(1)} %scale.3.second_part), channel_id=1, source_target_pairs={{0,3},{1,2},{2,1},{3,0},{4,5},{5,4},{6,7},{7,6},{8,11},{9,10},{10,... | collective-permute-start | bytes 1966088 | tf_op jit(solution)/shard_map/ppermute | solution.py:425

commit v7 on v6

--- a/solution.py
+++ b/solution.py
@@ -1,5 +1,3 @@
-import functools
-
 import jax
 import jax.numpy as jnp
 from jax import lax
@@ -14,7 +12,7 @@
 KEPT = SURE[0] + SHARED + SURE[1]
 CUT = (SURE[0] + SHARED - 1) * TILE
 SENT = (KEPT - 1) * TILE
-HALF, ALL_FIRST, LANE, AT, AT_SENT = range(2 * SHARED, 2 * SHARED + 5)
+HALF, ALL_FIRST, LANE, AT, AT_SENT, PART = range(2 * SHARED, 2 * SHARED + 6)
 BLOCK = 512
 STREAM = 512
 N_BLOCKS = -(-KEPT * TILE // STREAM)
@@ -86,9 +84,9 @@
     )(*in_hbm(wind))
 
 
-def unpack_kernel(payload, rot_ref, div_ref, outs, order8, order4, sems):
-    _, rows, slots, width = outs.shape
-    lanes = width // 4
+def unpack_kernel(halves, payload, *refs):
+    rot_ref, div_ref, outs, order8, order4, sems = refs[-6:]
+    _, rows, slots, lanes = outs.shape
     for count, order in ((8, order8), (4, order4)):
         c = log2(count)
 
@@ -98,8 +96,8 @@
 
         fill_order(order, source)
     copies = []
-    for n, component in enumerate((0, 3, 1, 2)):
-        cols = slice(2 * n * lanes, 2 * (n + 1) * lanes)
+    for part in range(2):
+        cols = slice(2 * part * lanes, 2 * (part + 1) * lanes)
         mains = [payload[:, 16 * slot:16 * slot + 16, cols].astype(F32) for slot in range(2)]
         for start in (0, 8, 16):
             if start < 16:
@@ -110,33 +108,36 @@
                 count, order = 4, order4
             moved = dot(order[...], block.reshape(count * slots, 2 * lanes).astype(BF16), NN)
             moved = moved.reshape(count, slots, 2 * lanes).astype(BF16)
-            for k, ref in enumerate((rot_ref, div_ref)):
-                outs[k, start:start + count, :, component * lanes:(component + 1) * lanes] = (
-                    moved[:, :, k * lanes:(k + 1) * lanes])
-                at = (pl.ds(start, count), slice(None), pl.ds(component * lanes, lanes))
-                copies.append(pltpu.make_async_copy(outs.at[(k, *at)], ref.at[at], sems.at[len(copies)]))
-                copies[-1].start()
-    for copy in copies:
-        copy.wait()
-
-
-def unpack(payload, rows):
+            for k in range(2):
+                outs[2 * part + k, start:start + count] = moved[:, :, k * lanes:(k + 1) * lanes]
+        for k, component in enumerate((part, 3 - part)):
+            n = 2 * part + k
+            at = (slice(None), slice(None), pl.ds(component * lanes, lanes))
+            copies.append([pltpu.make_async_copy(outs.at[n], ref.at[at], sems.at[n]) for ref in (rot_ref, div_ref)])
+            for half in range(2):
+                pl.when(halves[part] == half)(copies[n][half].start)
+    for to_rot, _ in copies:
+        to_rot.wait()
+
+
+def unpack(halves, payload, rows, filled=()):
     pairs, both, width = payload.shape
     slots = pairs * 2
-    shape = (rows, slots, width // 2)
+    shape = (rows, slots, width)
     return call(
         unpack_kernel,
         "unpack",
         out_shape=(pltpu.HBM(shape, BF16), pltpu.HBM(shape, BF16)),
-        in_specs=[IN_VMEM],
+        in_specs=[IN_SMEM, IN_VMEM] + [IN_PLACE] * len(filled),
         out_specs=(IN_PLACE, IN_PLACE),
+        input_output_aliases={2: 0, 3: 1} if filled else {},
         scratch_shapes=[
-            pltpu.VMEM((2, *shape), BF16),
+            pltpu.VMEM((4, rows, slots, width // 4), BF16),
             pltpu.VMEM((8 * slots, 8 * slots), BF16),
             pltpu.VMEM((4 * slots, 4 * slots), BF16),
-            pltpu.SemaphoreType.DMA((24,)),
+            pltpu.SemaphoreType.DMA((4,)),
         ],
-    )(payload)
+    )(halves, payload, *filled)
 
 
 def in_hbm(*arrays):
@@ -197,7 +198,7 @@
     return jnp.where(hit, 1.0, 0.0).astype(BF16)
 
 
-def forward_kernel(part, meta, rate, mask, weight, recv, table, factor, keep, send, *refs):
+def forward_kernel(meta, rate, mask, weight, recv, table, factor, keep, send, *refs):
     del factor
     owners, both, width = recv.shape
     source, (table, wind, spec, sems) = table, refs
@@ -210,7 +211,7 @@
     quarter = weight.shape[0]
     levels = width // 4
     main = owners * 16
-    columns = [slice(at * levels, (at + 1) * levels) for at in (part, 3 - part)]
+    columns = [pl.ds(pl.multiple_of(at * levels, levels), levels) for at in (meta[PART], 3 - meta[PART])]
     mixed = [recv[:, 32:, cols].astype(F32).reshape(owners * 8, levels).astype(BF16) for cols in columns]
     mixed = jnp.concatenate(mixed, axis=1)
     for slot in range(2):
@@ -251,7 +252,7 @@
         ref[:, CUT:] = spec[rows, CUT + TILE:].astype(ref.dtype)
 
 
-def forward(part, meta, rate, mask, weight, recv, table, factor):
+def forward(last, meta, rate, mask, weight, recv, table, factor):
     owners, both, width = recv.shape
     levels = width // 4
     quarter = weight.shape[0]
@@ -261,9 +262,9 @@
         pltpu.VMEM((2 * levels, KEPT * TILE), F32),
         pltpu.SemaphoreType.DMA((N_BLOCKS,)),
     ]
-    (scratch, out_shape)[part].insert((0, 2)[part], pltpu.VMEM(table.shape, BF16))
-    return call(
-        functools.partial(forward_kernel, part),
+    (scratch, out_shape)[last].insert((0, 2)[last], pltpu.VMEM(table.shape, BF16))
+    return call(
+        forward_kernel,
         "forward",
         in_specs=[IN_SMEM] * 2 + [IN_VMEM] * 3 + [IN_PLACE] * 2,
         out_specs=[IN_VMEM] * len(out_shape),
@@ -273,11 +274,10 @@
     )(meta, rate, mask, weight, recv, *in_hbm(table), factor)
 
 
-def backward_kernel(meta, halves, rate, mask, first_part, second_part, table, *refs):
-    out_ref, every, masked, last, out, sems = refs[-6:]
+def backward_kernel(meta, halves, rate, mask, first_part, second_part, table, out_ref, every, masked, last, out, sems):
     levels = first_part.shape[0]
     quarter = table.shape[0] // 2
-    owners = out.shape[1]
+    owners = out.shape[0]
     main = owners * 16
     split = (SURE[0] + SHARED) * TILE
     degrees = KEPT * TILE
@@ -320,38 +320,39 @@
             of_psi = halves[part] == 0
             for n, field in enumerate((jnp.where(of_psi, -h, -p), jnp.where(of_psi, p, h))):
                 field = field.astype(BF16)
-                out[2 * part + n, :, 16 * slot:16 * slot + 16] = field[:main].reshape(owners, 16, levels)
-                last[slot, :, (2 * part + n) * levels:(2 * part + n + 1) * levels] = field[main:]
+                at = slice((2 * part + n) * levels, (2 * part + n + 1) * levels)
+                out[:, 16 * slot:16 * slot + 16, at] = field[:main].reshape(owners, 16, levels)
+                last[slot, :, at] = field[main:]
     mixed = dot(last_rows(0, owners), last[0], TN) + dot(last_rows(1, owners), last[1], TN)
+    out[:, 32:] = mixed.reshape(owners, 8, 4 * levels).astype(BF16)
     sent = []
-    for n in range(4):
-        some = mixed[:, n * levels:(n + 1) * levels]
-        out[n, :, 32:] = some.reshape(owners, 8, levels).astype(BF16)
-        column = pl.multiple_of((2 * n + halves[n // 2]) * levels, levels)
-        sent.append(pltpu.make_async_copy(out.at[n], out_ref.at[:, :, pl.ds(column, levels)], sems.at[n]))
+    for n, part in enumerate((meta[PART], 1 - meta[PART])):
+        column = pl.multiple_of(part * 2 * levels, 2 * levels)
+        sent.append(pltpu.make_async_copy(
+            out.at[:, :, pl.ds(n * 2 * levels, 2 * levels)], out_ref.at[:, :, pl.ds(column, 2 * levels)], sems.at[n]))
         sent[n].start()
     for copy in sent:
         copy.wait()
 
 
-def backward(meta, halves, rate, mask, first_part, second_part, table, payload, filled=()):
+def backward(meta, halves, rate, mask, first_part, second_part, table, payload, flops):
     levels = first_part.shape[0]
     owners, both, width = payload
     return call(
         backward_kernel,
         "backward",
-        in_specs=[IN_SMEM] * 3 + [IN_VMEM] * 4 + [IN_PLACE] * len(filled),
+        in_specs=[IN_SMEM] * 3 + [IN_VMEM] * 4,
         out_specs=IN_PLACE,
         out_shape=pltpu.HBM(payload, BF16),
-        input_output_aliases={7: 0} if filled else {},
         scratch_shapes=[
             pltpu.VMEM((2 * levels, SENT), BF16),
             pltpu.VMEM((2, 2 * levels, (SURE[0] + SHARED) * TILE), BF16),
             pltpu.VMEM((2, owners * 4, 4 * levels), BF16),
-            pltpu.VMEM((4, owners, both, levels), BF16),
-            pltpu.SemaphoreType.DMA((4,)),
+            pltpu.VMEM(payload, BF16),
+            pltpu.SemaphoreType.DMA((2,)),
         ],
-    )(meta, halves, rate, mask, first_part, second_part, table, *filled)
+        cost_estimate=pl.CostEstimate(flops=flops, bytes_accessed=10**7, transcendentals=0),
+    )(meta, halves, rate, mask, first_part, second_part, table)
 
 
 def add_kernel(kept, got, total, sent):
@@ -383,7 +384,7 @@
     )(kept, got, factor)
 
 
-def layout(wavenumbers, count, half):
+def layout(wavenumbers, count, half, part):
     low_first, low_second = wavenumbers[0] // TILE, wavenumbers[1] // TILE
     n_first = count - low_first - SURE[0]
     k = jnp.arange(SHARED)
@@ -395,7 +396,7 @@
     at = jnp.where(n_first == 0, 0, SURE[0] - 1 + n_first)
     at, at_sent = jnp.where(all_first, SURE[0] + SHARED, at), jnp.where(all_first, SURE[0] + SHARED - 1, at)
     lane_first = wavenumbers[0] % TILE
-    scalars = jnp.stack([half, all_first.astype(jnp.int32), lane_first, at, at_sent])
+    scalars = jnp.stack([half, all_first.astype(jnp.int32), lane_first, at, at_sent, part])
     meta = jnp.concatenate([shared_slot, shared_tile, scalars]).astype(jnp.int32)
     tile = jnp.concatenate([jnp.arange(count - SURE[0], count), shared_tile[:-1], jnp.arange(count - SURE[1], count)])
     joint = jnp.arange(tile.shape[0]) == at_sent
@@ -429,7 +430,7 @@
     metas = []
     for n in range(2):
         half = jnp.where(odd == n, *halves)
-        meta, mask, factor = layout(wavenumbers, count, half)
+        meta, mask, factor = layout(wavenumbers, count, half, odd ^ n)
         metas.append(meta)
     rate = wavenumbers.astype(F32) / LMAX
 
@@ -439,7 +440,7 @@
     weight = jnp.sum(jnp.where(hit, quad_weight[None, :], 0.0), axis=1, keepdims=True)
     table = keep(meta, hit.astype(BF16), p_table, h_table)
     owners, both, width = received.shape
-    payload = (owners, both, 2 * width)
+    rate = jnp.where(odd == 0, rate, -rate)
     signs = (rate, -rate)
     kept_a, sent_a = forward(0, metas[0], signs[0], mask, weight, received, table, factor)
     kept_b, sent_b, table = forward(1, metas[1], signs[1], mask, weight, received, table, factor)
@@ -449,10 +450,12 @@
     mine_a = scale(kept_a, swap(sent_a, ways[1]), factor)
     mine_b = scale(kept_b, swap(sent_b, ways[0]), factor)
     theirs_a, theirs_b = swap(mine_a, ways[0]), swap(mine_b, ways[1])
-    halves = jnp.stack([meta[HALF] for meta in metas])
-    out = backward(metas[0], halves, rate, mask, mine_a, mine_b, table, payload)
-    out = backward(metas[0], 1 - halves, rate, mask, theirs_a, theirs_b, table, payload, (out,))
-    return tuple(unpack(lax.all_to_all(out, "ma", 0, 0, tiled=True), rows))
+    kept_halves = jnp.stack([meta[HALF] for meta in metas])
+    kept = backward(metas[0], kept_halves, rate, mask, mine_a, mine_b, table, received.shape, 50000000000)
+    others = backward(metas[0], 1 - kept_halves, rate, mask, theirs_a, theirs_b, table, received.shape, 600000000000)
+    kept, others = (lax.all_to_all(x, "ma", 0, 0, tiled=True) for x in (kept, others))
+    halves = jnp.stack(halves).astype(jnp.int32)
+    return tuple(unpack(1 - halves, others, rows, unpack(halves, kept, rows)))
 
 
 def solution(mesh):

time: 133 us -> 132 us (level)
  blocking collectives: 38.3 us -> 0 us
  waiting for transfers between devices: 23.7 us -> 47.2 us
  starting transfers between devices: 24.1 us -> 32.4 us
  Pallas kernels: 37.3 us -> 40.3 us
  local copies, waits for them, and re-layouts: 1.38 us -> 4.33 us
    all_to_all x1 -> x0, blocking collectives: 38.3 us -> none  [on_device(): return tuple(unpack(lax.all_to_all(out, 'ma', 0, 0, tiled=True), rows))]
    all_to_all x0 -> x2, waiting for transfers between devices: none -> 28 us  [on_device(): lax.all_to_all(x, 'ma', 0, 0, tiled=True)]
    all_to_all x0 -> x2, starting transfers between devices: none -> 8.64 us  [on_device(): lax.all_to_all(x, 'ma', 0, 0, tiled=True)]
    ppermute x6, waiting for transfers between devices: 20 us -> 15.7 us  [swap(): return lax.ppermute(x, ('ma', 'oct'), pairs)]
    unnamed x8 -> x12, local copies, waits for them, and re-layouts: 0.1 us -> 3.05 us
    pallas_call x1 -> x2, Pallas kernels: 2.58 us -> 5.27 us  [unpack(): call(unpack_kernel, 'unpack', out_shape=(pltpu.HBM(shape, BF16), pltpu.HB...]
  transfers between devices with their start and end apart: 7 -> 9, of which waited for: 7 -> 7; matrix products, arithmetic and copies ran while one was open for 2% -> 2% of each run, Pallas kernels for 16% -> 22%
where the time goes in v7:
time: 132 us
  waiting for transfers between devices  47.2 us (36%)
  Pallas kernels  40.3 us (31%)
  starting transfers between devices  32.4 us (25%)
  between operations  6.26 us (5%)
  local copies, waits for them, and re-layouts  4.33 us (3%)
    all_to_all x2, waiting for transfers between devices, on_device(): lax.all_to_all(x, 'ma', 0, 0, tiled=True)  28 us
    ppermute x6, starting transfers between devices, swap(): return lax.ppermute(x, ('ma', 'oct'), pairs)  16.3 us
    ppermute x6, waiting for transfers between devices, swap(): return lax.ppermute(x, ('ma', 'oct'), pairs)  15.7 us
    pallas_call x2, Pallas kernels, forward(): call(forward_kernel, 'forward', in_specs=[IN_SMEM] * 2 + [IN_VMEM] * 3 +...  12.2 us
    pallas_call x1, Pallas kernels, keep(): call(keep_kernel, 'keep', out_shape=pltpu.HBM(shape, BF16), in_specs=[IN_...  9.56 us
    pallas_call x2, Pallas kernels, backward(): call(backward_kernel, 'backward', in_specs=[IN_SMEM] * 3 + [IN_VMEM] * 4,...  9.3 us
    all_to_all x2, starting transfers between devices, on_device(): lax.all_to_all(x, 'ma', 0, 0, tiled=True)  8.64 us
    all_to_all x1, starting transfers between devices, on_device(): received = lax.all_to_all(pack(fourier_wind), 'ma', 0, 0, tiled=True)  7.54 us
  transfers between devices with their start and end apart: 9, of which 7 were waited for; matrix products, arithmetic and copies ran while one was open for 2% of the time, Pallas kernels for 22%

profile of v7, /device:TPU:0, one launch (start us, length us, event | category | flops | bytes accessed | tf_op | source)
XLA Modules:
  0.0 131.6 jit_solution(14896448730058995143)
XLA Ops:
  0.6 3.1 %pack.1 = bf16[32,40,512]{2,1,0:T(8,128)(2,1)} custom-call(bf16[20,64,512]{2,1,0:T(8,128)(2,1)} %wind_ref.1), custom_call_target="tpu_custom_call" | custom-call | tf_op jit(solution)/shard_map/pack/pallas_call | solution.py:73
  3.8 7.5 %all-to-all-start = ((bf16[32,40,512]{2,1,0:T(8,128)(2,1)}), bf16[32,40,512]{2,1,0:T(8,128)(2,1)S(1)}, u32[]{:S(2)}, u32[]{:S(2)}) async-start(bf16[32,40,512]{2,1,0:T(8,128)(2,1)} %pack.1), calls=%async_computation | async-start | bytes 2621440 | tf_op jit(solution)/shard_map/all_to_all | solution.py:428
  18.8 9.6 %keep.1.table = bf16[1280,2688]{1,0:T(8,128)(2,1)} custom-call(s32[16]{0:T(128)S(1)} %concatenate.22.meta, bf16[640,640]{1,0:T(8,128)(2,1)S(1)} %fusion.select, bf16[2,640,2560]{2,1,0:T(8,128)(2,1)} %p_ref.1, bf16[2,640,2560]{2,1,0:T(8,128)(2,1)} %h_ref.1), custom_call_target="tpu_custom_call" | custom-call | tf_op jit(solution)/shard_map/keep/pallas_call | solution.py:180
  28.5 3.6 %all-to-all-done.recv = bf16[32,40,512]{2,1,0:T(8,128)(2,1)S(1)} async-done(((bf16[32,40,512]{2,1,0:T(8,128)(2,1)}), bf16[32,40,512]{2,1,0:T(8,128)(2,1)S(1)}, u32[]{:S(2)}, u32[]{:S(2)}) %all-to-all-start) | async-done | bytes 1310752 | tf_op jit(solution)/shard_map/all_to_all | solution.py:428
  32.1 6.1 %forward.2 = (f32[128,2560]{1,0:T(8,128)S(1)}, bf16[128,2560]{1,0:T(8,128)(2,1)S(1)}) custom-call(s32[16]{0:T(128)S(1)} %concatenate.19.meta, f32[2]{0:T(128)S(1)} %get-tuple-element.25.rate, f32[1,2688]{1,0:T(1,128)S(1)} %bitcast.26, f32[640,1]{1,0:T(8,128)S(1)} %broadcast_in_dim.44.weight, bf16[32,40,512]{2,1,0:T(8,128)(2,1)S(1)} %all-to-all-done.recv, ...), custom_call_target="tpu_custom_call" | custom-call | flops 5000000000 | bytes 10000000 | tf_op jit(solution)/shard_map/forward/pallas_call | solution.py:266
  38.2 2.0 %collective-permute-start = (bf16[128,2560]{1,0:T(8,128)(2,1)S(1)}, bf16[128,2560]{1,0:T(8,128)(2,1)S(1)}, u32[]{:S(2)}, u32[]{:S(2)}) collective-permute-start(bf16[128,2560]{1,0:T(8,128)(2,1)S(1)} %get-tuple-element.14), channel_id=1, source_target_pairs={{0,1},{1,0},{2,3},{3,2},{4,7},{5,6},{6,5},{7,4},{8,9},{9,8},{10,11... | collective-permute-start | bytes 1966088 | tf_op jit(solution)/shard_map/ppermute | solution.py:426
  40.2 6.1 %forward.3 = (f32[128,2560]{1,0:T(8,128)S(1)}, bf16[128,2560]{1,0:T(8,128)(2,1)S(1)}, bf16[1280,2688]{1,0:T(8,128)(2,1)S(1)}) custom-call(s32[16]{0:T(128)S(1)} %concatenate.22.meta, f32[2]{0:T(128)S(1)} %get-tuple-element.24.rate, f32[1,2688]{1,0:T(1,128)S(1)} %bitcast.27, f32[640,1]{1,0:T(8,128)S(1)} %broadcast_in_dim.44.weight, ...), custom_call_target="tpu_custom_call" | custom-call | flops 5000000000 | bytes 10000000 | tf_op jit(solution)/shard_map/forward/pallas_call | solution.py:266
  46.4 2.8 %collective-permute-start.3 = (bf16[128,2560]{1,0:T(8,128)(2,1)S(1)}, bf16[128,2560]{1,0:T(8,128)(2,1)S(1)}, u32[]{:S(2)}, u32[]{:S(2)}) collective-permute-start(bf16[128,2560]{1,0:T(8,128)(2,1)S(1)} %get-tuple-element.18), channel_id=1, source_target_pairs={{0,3},{1,2},{2,1},{3,0},{4,5},{5,4},{6,7},{7,6},{8,11},{9,10},{10,... | collective-permute-start | bytes 1966088 | tf_op jit(solution)/shard_map/ppermute | solution.py:426
  49.4 6.8 %collective-permute-start.1 = (bf16[128,2560]{1,0:T(8,128)(2,1)S(1)}, bf16[128,2560]{1,0:T(8,128)(2,1)S(1)}, u32[]{:S(2)}, u32[]{:S(2)}) collective-permute-start(bf16[128,2560]{1,0:T(8,128)(2,1)S(1)} %get-tuple-element.16), channel_id=1, source_target_pairs={{0,3},{1,2},{2,1},{3,0},{4,5},{5,4},{6,7},{7,6},{8,11},{9,10},{10,... | collective-permute-start | bytes 1966088 | tf_op jit(solution)/shard_map/ppermute | solution.py:426
  56.2 2.2 %collective-permute-done.3.got = bf16[128,2560]{1,0:T(8,128)(2,1)S(1)} collective-permute-done((bf16[128,2560]{1,0:T(8,128)(2,1)S(1)}, bf16[128,2560]{1,0:T(8,128)(2,1)S(1)}, u32[]{:S(2)}, u32[]{:S(2)}) %collective-permute-start.3) | collective-permute-done | bytes 655392 | tf_op jit(solution)/shard_map/ppermute | solution.py:426
  59.1 10.5 %collective-permute-done.1.got = bf16[128,2560]{1,0:T(8,128)(2,1)S(1)} collective-permute-done((bf16[128,2560]{1,0:T(8,128)(2,1)S(1)}, bf16[128,2560]{1,0:T(8,128)(2,1)S(1)}, u32[]{:S(2)}, u32[]{:S(2)}) %collective-permute-start.1) | collective-permute-done | bytes 655392 | tf_op jit(solution)/shard_map/ppermute | solution.py:426
  69.8 0.9 collective-permute-start.2
  70.9 3.4 %collective-permute-start.5 = (bf16[128,2560]{1,0:T(8,128)(2,1)S(1)}, bf16[128,2560]{1,0:T(8,128)(2,1)S(1)}, u32[]{:S(2)}, u32[]{:S(2)}) collective-permute-start(bf16[128,2560]{1,0:T(8,128)(2,1)S(1)} %scale.3.second_part), channel_id=1, source_target_pairs={{0,3},{1,2},{2,1},{3,0},{4,5},{5,4},{6,7},{7,6},{8,11},{9,10},{10,... | collective-permute-start | bytes 1966088 | tf_op jit(solution)/shard_map/ppermute | solution.py:426
  74.3 4.6 %backward.3 = bf16[32,40,512]{2,1,0:T(8,128)(2,1)} custom-call(s32[16]{0:T(128)S(1)} %concatenate.19.meta, s32[2]{0:T(128)S(1)} %get-tuple-element.27.halves, f32[2]{0:T(128)S(1)} %get-tuple-element.25.rate, f32[1,2688]{1,0:T(1,128)S(1)} %bitcast.28, bf16[128,2560]{1,0:T(8,128)(2,1)S(1)} %scale.2.first_part, bf16[128,2560]{1,0:T(8,128)(2,1)S(1)} %scale.3.second_part, ...), custom_call_target="tpu_custom_call" | custom-call | flops 49999998976 | bytes 10000000 | tf_op jit(solution)/shard_map/backward/pallas_call | solution.py:341
  78.9 4.7 %all-to-all-start.2 = ((bf16[32,40,512]{2,1,0:T(8,128)(2,1)}), bf16[32,40,512]{2,1,0:T(8,128)(2,1)}, u32[]{:S(2)}, u32[]{:S(2)}) async-start(bf16[32,40,512]{2,1,0:T(8,128)(2,1)} %backward.3), calls=%async_computation.2 | async-start | bytes 2621440 | tf_op jit(solution)/shard_map/all_to_all | solution.py:456
  83.6 2.0 %collective-permute-done.2.first_part = bf16[128,2560]{1,0:T(8,128)(2,1)S(1)} collective-permute-done((bf16[128,2560]{1,0:T(8,128)(2,1)S(1)}, bf16[128,2560]{1,0:T(8,128)(2,1)S(1)}, u32[]{:S(2)}, u32[]{:S(2)}) %collective-permute-start.2) | collective-permute-done | bytes 655392 | tf_op jit(solution)/shard_map/ppermute | solution.py:426
  85.7 0.9 collective-permute-done.5.second_part
  86.5 3.0 %copy-done.1 = bf16[1280,2688]{1,0:T(8,128)(2,1)S(1)} copy-done((bf16[1280,2688]{1,0:T(8,128)(2,1)S(1)}, bf16[1280,2688]{1,0:T(8,128)(2,1)}, u32[]{:S(2)}) %copy-start.1) | copy-done | bytes 6881304
  89.5 4.7 %backward.2 = bf16[32,40,512]{2,1,0:T(8,128)(2,1)} custom-call(s32[16]{0:T(128)S(1)} %concatenate.19.meta, s32[2]{0:T(128)S(1)} %get-tuple-element.26.halves, f32[2]{0:T(128)S(1)} %get-tuple-element.25.rate, f32[1,2688]{1,0:T(1,128)S(1)} %bitcast.29, bf16[128,2560]{1,0:T(8,128)(2,1)S(1)} %collective-permute-done.2.first_part, ...), custom_call_target="tpu_custom_call" | custom-call | flops 599999971328 | bytes 10000000 | tf_op jit(solution)/shard_map/backward/pallas_call | solution.py:341
  94.1 10.3 %all-to-all-done.2.payload = bf16[32,40,512]{2,1,0:T(8,128)(2,1)} async-done(((bf16[32,40,512]{2,1,0:T(8,128)(2,1)}), bf16[32,40,512]{2,1,0:T(8,128)(2,1)}, u32[]{:S(2)}, u32[]{:S(2)}) %all-to-all-start.2) | async-done | bytes 1310752 | tf_op jit(solution)/shard_map/all_to_all | solution.py:456
  104.4 4.0 %all-to-all-start.1 = ((bf16[32,40,512]{2,1,0:T(8,128)(2,1)}), bf16[32,40,512]{2,1,0:T(8,128)(2,1)S(1)}, u32[]{:S(2)}, u32[]{:S(2)}) async-start(bf16[32,40,512]{2,1,0:T(8,128)(2,1)} %backward.2), calls=%async_computation.1 | async-start | bytes 2621440 | tf_op jit(solution)/shard_map/all_to_all | solution.py:456
  108.4 3.0 %unpack.2 = (bf16[20,64,512]{2,1,0:T(8,128)(2,1)}, bf16[20,64,512]{2,1,0:T(8,128)(2,1)}) custom-call(s32[2]{0:T(128)S(1)} %get-tuple-element.29.halves, bf16[32,40,512]{2,1,0:T(8,128)(2,1)} %all-to-all-done.2.payload), custom_call_target="tpu_custom_call" | custom-call | tf_op jit(solution)/shard_map/unpack/pallas_call | solution.py:127
  111.5 17.7 %all-to-all-done.1.payload = bf16[32,40,512]{2,1,0:T(8,128)(2,1)S(1)} async-done(((bf16[32,40,512]{2,1,0:T(8,128)(2,1)}), bf16[32,40,512]{2,1,0:T(8,128)(2,1)S(1)}, u32[]{:S(2)}, u32[]{:S(2)}) %all-to-all-start.1) | async-done | bytes 1310752 | tf_op jit(solution)/shard_map/all_to_all | solution.py:456
  129.2 2.2 %unpack.3 = (bf16[20,64,512]{2,1,0:T(8,128)(2,1)}, bf16[20,64,512]{2,1,0:T(8,128)(2,1)}) custom-call(s32[2]{0:T(128)S(1)} %get-tuple-element.28.halves, bf16[32,40,512]{2,1,0:T(8,128)(2,1)S(1)} %all-to-all-done.1.payload, bf16[20,64,512]{2,1,0:T(8,128)(2,1)} %get-tuple-element.22.refs_0_, ...), custom_call_target="tpu_custom_call", output_to_operand_aliasing={{0}: (2, {}), {1}: (3, {})} | custom-call | tf_op jit(solution)/shard_map/unpack/pallas_call | solution.py:127
  (46 shorter events, 3.6 us)
Async XLA Ops:
  3.8 7.6 %copy-start.3 = (s32[2]{0:T(128)S(1)}, s32[2]{0:T(128)}, u32[]{:S(2)}) copy-start(s32[2]{0:T(128)} %param.10) | copy-start | bytes 28
  3.8 13.5 %copy-start.2 = (s32[2560]{0:T(1024)S(1)}, s32[2560]{0:T(1024)}, u32[]{:S(2)}) copy-start(s32[2560]{0:T(1024)} %param.11) | copy-start | bytes 30724
  3.8 14.2 %copy-start.4 = (f32[640]{0:T(1024)S(1)}, f32[640]{0:T(1024)}, u32[]{:S(2)}) copy-start(f32[640]{0:T(1024)} %param.7) | copy-start | bytes 7684
  3.8 28.3 %all-to-all-start = ((bf16[32,40,512]{2,1,0:T(8,128)(2,1)}), bf16[32,40,512]{2,1,0:T(8,128)(2,1)S(1)}, u32[]{:S(2)}, u32[]{:S(2)}) async-start(bf16[32,40,512]{2,1,0:T(8,128)(2,1)} %pack.1), calls=%async_computation | async-start | bytes 2621440 | tf_op jit(solution)/shard_map/all_to_all | solution.py:428
  38.2 10.9 %collective-permute-start = (bf16[128,2560]{1,0:T(8,128)(2,1)S(1)}, bf16[128,2560]{1,0:T(8,128)(2,1)S(1)}, u32[]{:S(2)}, u32[]{:S(2)}) collective-permute-start(bf16[128,2560]{1,0:T(8,128)(2,1)S(1)} %get-tuple-element.14), channel_id=1, source_target_pairs={{0,1},{1,0},{2,3},{3,2},{4,7},{5,6},{6,5},{7,4},{8,9},{9,8},{10,11... | collective-permute-start | bytes 1966088 | tf_op jit(solution)/shard_map/ppermute | solution.py:426
  46.4 27.9 %copy-start = (bf16[1280,2688]{1,0:T(8,128)(2,1)}, bf16[1280,2688]{1,0:T(8,128)(2,1)S(1)}, u32[]{:S(2)}) copy-start(bf16[1280,2688]{1,0:T(8,128)(2,1)S(1)} %get-tuple-element.21.table) | copy-start | bytes 20643844
  46.4 12.1 %collective-permute-start.3 = (bf16[128,2560]{1,0:T(8,128)(2,1)S(1)}, bf16[128,2560]{1,0:T(8,128)(2,1)S(1)}, u32[]{:S(2)}, u32[]{:S(2)}) collective-permute-start(bf16[128,2560]{1,0:T(8,128)(2,1)S(1)} %get-tuple-element.18), channel_id=1, source_target_pairs={{0,3},{1,2},{2,1},{3,0},{4,5},{5,4},{6,7},{7,6},{8,11},{9,10},{10,... | collective-permute-start | bytes 1966088 | tf_op jit(solution)/shard_map/ppermute | solution.py:426
  49.4 20.2 %collective-permute-start.1 = (bf16[128,2560]{1,0:T(8,128)(2,1)S(1)}, bf16[128,2560]{1,0:T(8,128)(2,1)S(1)}, u32[]{:S(2)}, u32[]{:S(2)}) collective-permute-start(bf16[128,2560]{1,0:T(8,128)(2,1)S(1)} %get-tuple-element.16), channel_id=1, source_target_pairs={{0,3},{1,2},{2,1},{3,0},{4,5},{5,4},{6,7},{7,6},{8,11},{9,10},{10,... | collective-permute-start | bytes 1966088 | tf_op jit(solution)/shard_map/ppermute | solution.py:426
  58.7 12.1 %collective-permute-start.4 = (bf16[128,2560]{1,0:T(8,128)(2,1)S(1)}, bf16[128,2560]{1,0:T(8,128)(2,1)S(1)}, u32[]{:S(2)}, u32[]{:S(2)}) collective-permute-start(bf16[128,2560]{1,0:T(8,128)(2,1)S(1)} %get-tuple-element.20), channel_id=1, source_target_pairs={{0,1},{1,0},{2,3},{3,2},{4,7},{5,6},{6,5},{7,4},{8,9},{9,8},{10,11... | collective-permute-start | bytes 1966088 | tf_op jit(solution)/shard_map/ppermute | solution.py:426
  69.8 15.9 %collective-permute-start.2 = (bf16[128,2560]{1,0:T(8,128)(2,1)S(1)}, bf16[128,2560]{1,0:T(8,128)(2,1)S(1)}, u32[]{:S(2)}, u32[]{:S(2)}) collective-permute-start(bf16[128,2560]{1,0:T(8,128)(2,1)S(1)} %scale.2.first_part), channel_id=1, source_target_pairs={{0,1},{1,0},{2,3},{3,2},{4,7},{5,6},{6,5},{7,4},{8,9},{9,8},{10,11... | collective-permute-start | bytes 1966088 | tf_op jit(solution)/shard_map/ppermute | solution.py:426
  70.9 15.6 %collective-permute-start.5 = (bf16[128,2560]{1,0:T(8,128)(2,1)S(1)}, bf16[128,2560]{1,0:T(8,128)(2,1)S(1)}, u32[]{:S(2)}, u32[]{:S(2)}) collective-permute-start(bf16[128,2560]{1,0:T(8,128)(2,1)S(1)} %scale.3.second_part), channel_id=1, source_target_pairs={{0,3},{1,2},{2,1},{3,0},{4,5},{5,4},{6,7},{7,6},{8,11},{9,10},{10,... | collective-permute-start | bytes 1966088 | tf_op jit(solution)/shard_map/ppermute | solution.py:426
  78.9 25.5 %all-to-all-start.2 = ((bf16[32,40,512]{2,1,0:T(8,128)(2,1)}), bf16[32,40,512]{2,1,0:T(8,128)(2,1)}, u32[]{:S(2)}, u32[]{:S(2)}) async-start(bf16[32,40,512]{2,1,0:T(8,128)(2,1)} %backward.3), calls=%async_computation.2 | async-start | bytes 2621440 | tf_op jit(solution)/shard_map/all_to_all | solution.py:456
  86.5 3.0 %copy-start.1 = (bf16[1280,2688]{1,0:T(8,128)(2,1)S(1)}, bf16[1280,2688]{1,0:T(8,128)(2,1)}, u32[]{:S(2)}) copy-start(bf16[1280,2688]{1,0:T(8,128)(2,1)} %copy-done) | copy-start | bytes 20643844
  104.4 24.8 %all-to-all-start.1 = ((bf16[32,40,512]{2,1,0:T(8,128)(2,1)}), bf16[32,40,512]{2,1,0:T(8,128)(2,1)S(1)}, u32[]{:S(2)}, u32[]{:S(2)}) async-start(bf16[32,40,512]{2,1,0:T(8,128)(2,1)} %backward.2), calls=%async_computation.1 | async-start | bytes 2621440 | tf_op jit(solution)/shard_map/all_to_all | solution.py:456

commit v8 on v7

--- a/solution.py
+++ b/solution.py
@@ -384,6 +384,21 @@
     )(kept, got, factor)
 
 
+def relay_kernel(x, out):
+    out[...] = x[...]
+
+
+def relay(x):
+    return call(
+        relay_kernel,
+        "relay",
+        in_specs=[IN_VMEM],
+        out_specs=IN_VMEM,
+        out_shape=jax.ShapeDtypeStruct(x.shape, x.dtype),
+        cost_estimate=pl.CostEstimate(flops=10**10, bytes_accessed=10**6, transcendentals=0),
+    )(x)
+
+
 def layout(wavenumbers, count, half, part):
     low_first, low_second = wavenumbers[0] // TILE, wavenumbers[1] // TILE
     n_first = count - low_first - SURE[0]
@@ -449,10 +464,13 @@
     kept_b, sent_b = add(kept_b, swap(sent_b, ways[1]))
     mine_a = scale(kept_a, swap(sent_a, ways[1]), factor)
     mine_b = scale(kept_b, swap(sent_b, ways[0]), factor)
-    theirs_a, theirs_b = swap(mine_a, ways[0]), swap(mine_b, ways[1])
     kept_halves = jnp.stack([meta[HALF] for meta in metas])
+    theirs_a = swap(mine_a, ways[0])
     kept = backward(metas[0], kept_halves, rate, mask, mine_a, mine_b, table, received.shape, 50000000000)
-    others = backward(metas[0], 1 - kept_halves, rate, mask, theirs_a, theirs_b, table, received.shape, 600000000000)
+    mine_b, kept = lax.optimization_barrier((mine_b, kept))
+    theirs_b = swap(mine_b, ways[1])
+    theirs_a = relay(theirs_a)
+    others = backward(metas[0], 1 - kept_halves, rate, mask, theirs_a, theirs_b, table, received.shape, 2000000000)
     kept, others = (lax.all_to_all(x, "ma", 0, 0, tiled=True) for x in (kept, others))
     halves = jnp.stack(halves).astype(jnp.int32)
     return tuple(unpack(1 - halves, others, rows, unpack(halves, kept, rows)))

time: 132 us -> 131 us (level)
  local copies, waits for them, and re-layouts: 4.33 us -> 2.21 us
    all_to_all x2, waiting for transfers between devices: 28 us -> 21.7 us  [on_device(): lax.all_to_all(x, 'ma', 0, 0, tiled=True)]
    ppermute x6, waiting for transfers between devices: 15.7 us -> 21.4 us  [swap(): return lax.ppermute(x, ('ma', 'oct'), pairs)]
    unnamed x12 -> x16, local copies, waits for them, and re-layouts: 3.05 us -> 0.93 us
  transfers between devices with their start and end apart: 9 -> 9, of which waited for: 7 -> 6; matrix products, arithmetic and copies ran while one was open for 2% -> 2% of each run, Pallas kernels for 22% -> 23%
where the time goes in v8:
time: 131 us; the launch traced here: 130 us
  waiting for transfers between devices  46.5 us (35%)
  Pallas kernels  41.5 us (32%)
  starting transfers between devices  32.6 us (25%)
  between operations  6.5 us (5%)
  local copies, waits for them, and re-layouts  2.21 us (2%)
    all_to_all x2, waiting for transfers between devices, on_device(): lax.all_to_all(x, 'ma', 0, 0, tiled=True)  21.7 us
    ppermute x6, waiting for transfers between devices, swap(): return lax.ppermute(x, ('ma', 'oct'), pairs)  21.4 us
    ppermute x6, starting transfers between devices, swap(): return lax.ppermute(x, ('ma', 'oct'), pairs)  15.2 us
    pallas_call x2, Pallas kernels, forward(): call(forward_kernel, 'forward', in_specs=[IN_SMEM] * 2 + [IN_VMEM] * 3 +...  12.3 us
    all_to_all x2, starting transfers between devices, on_device(): lax.all_to_all(x, 'ma', 0, 0, tiled=True)  9.87 us
    pallas_call x1, Pallas kernels, keep(): call(keep_kernel, 'keep', out_shape=pltpu.HBM(shape, BF16), in_specs=[IN_...  9.55 us
    pallas_call x2, Pallas kernels, backward(): call(backward_kernel, 'backward', in_specs=[IN_SMEM] * 3 + [IN_VMEM] * 4,...  9.29 us
    all_to_all x1, starting transfers between devices, on_device(): received = lax.all_to_all(pack(fourier_wind), 'ma', 0, 0, tiled=True)  7.54 us
  transfers between devices with their start and end apart: 9, of which 6 were waited for; matrix products, arithmetic and copies ran while one was open for 2% of the time, Pallas kernels for 23%

profile of v8, /device:TPU:0, one launch (start us, length us, event | category | flops | bytes accessed | tf_op | source)
XLA Modules:
  0.0 130.3 jit_solution(9189853691894448259)
XLA Ops:
  0.6 3.1 %pack.1 = bf16[32,40,512]{2,1,0:T(8,128)(2,1)} custom-call(bf16[20,64,512]{2,1,0:T(8,128)(2,1)} %wind_ref.1), custom_call_target="tpu_custom_call" | custom-call | tf_op jit(solution)/shard_map/pack/pallas_call | solution.py:73
  3.8 7.5 %all-to-all-start = ((bf16[32,40,512]{2,1,0:T(8,128)(2,1)}), bf16[32,40,512]{2,1,0:T(8,128)(2,1)S(1)}, u32[]{:S(2)}, u32[]{:S(2)}) async-start(bf16[32,40,512]{2,1,0:T(8,128)(2,1)} %pack.1), calls=%async_computation | async-start | bytes 2621440 | tf_op jit(solution)/shard_map/all_to_all | solution.py:443
  19.0 9.5 %keep.1.table = bf16[1280,2688]{1,0:T(8,128)(2,1)} custom-call(s32[16]{0:T(128)S(1)} %concatenate.22.meta, bf16[640,640]{1,0:T(8,128)(2,1)S(1)} %fusion.select, bf16[2,640,2560]{2,1,0:T(8,128)(2,1)} %p_ref.1, bf16[2,640,2560]{2,1,0:T(8,128)(2,1)} %h_ref.1), custom_call_target="tpu_custom_call" | custom-call | tf_op jit(solution)/shard_map/keep/pallas_call | solution.py:180
  28.7 3.4 %all-to-all-done.recv = bf16[32,40,512]{2,1,0:T(8,128)(2,1)S(1)} async-done(((bf16[32,40,512]{2,1,0:T(8,128)(2,1)}), bf16[32,40,512]{2,1,0:T(8,128)(2,1)S(1)}, u32[]{:S(2)}, u32[]{:S(2)}) %all-to-all-start) | async-done | bytes 1310752 | tf_op jit(solution)/shard_map/all_to_all | solution.py:443
  32.1 6.1 %forward.2 = (f32[128,2560]{1,0:T(8,128)S(1)}, bf16[128,2560]{1,0:T(8,128)(2,1)S(1)}) custom-call(s32[16]{0:T(128)S(1)} %concatenate.19.meta, f32[2]{0:T(128)S(1)} %get-tuple-element.29.rate, f32[1,2688]{1,0:T(1,128)S(1)} %bitcast.28, f32[640,1]{1,0:T(8,128)S(1)} %broadcast_in_dim.44.weight, bf16[32,40,512]{2,1,0:T(8,128)(2,1)S(1)} %all-to-all-done.recv, ...), custom_call_target="tpu_custom_call" | custom-call | flops 5000000000 | bytes 10000000 | tf_op jit(solution)/shard_map/forward/pallas_call | solution.py:266
  38.2 2.0 %collective-permute-start = (bf16[128,2560]{1,0:T(8,128)(2,1)S(1)}, bf16[128,2560]{1,0:T(8,128)(2,1)S(1)}, u32[]{:S(2)}, u32[]{:S(2)}) collective-permute-start(bf16[128,2560]{1,0:T(8,128)(2,1)S(1)} %get-tuple-element.16), channel_id=1, source_target_pairs={{0,1},{1,0},{2,3},{3,2},{4,7},{5,6},{6,5},{7,4},{8,9},{9,8},{10,11... | collective-permute-start | bytes 1966088 | tf_op jit(solution)/shard_map/ppermute | solution.py:441
  40.2 6.2 %forward.3 = (f32[128,2560]{1,0:T(8,128)S(1)}, bf16[128,2560]{1,0:T(8,128)(2,1)S(1)}, bf16[1280,2688]{1,0:T(8,128)(2,1)S(1)}) custom-call(s32[16]{0:T(128)S(1)} %concatenate.22.meta, f32[2]{0:T(128)S(1)} %get-tuple-element.28.rate, f32[1,2688]{1,0:T(1,128)S(1)} %bitcast.29, f32[640,1]{1,0:T(8,128)S(1)} %broadcast_in_dim.44.weight, ...), custom_call_target="tpu_custom_call" | custom-call | flops 5000000000 | bytes 10000000 | tf_op jit(solution)/shard_map/forward/pallas_call | solution.py:266
  46.4 2.8 %collective-permute-start.3 = (bf16[128,2560]{1,0:T(8,128)(2,1)S(1)}, bf16[128,2560]{1,0:T(8,128)(2,1)S(1)}, u32[]{:S(2)}, u32[]{:S(2)}) collective-permute-start(bf16[128,2560]{1,0:T(8,128)(2,1)S(1)} %get-tuple-element.20), channel_id=1, source_target_pairs={{0,3},{1,2},{2,1},{3,0},{4,5},{5,4},{6,7},{7,6},{8,11},{9,10},{10,... | collective-permute-start | bytes 1966088 | tf_op jit(solution)/shard_map/ppermute | solution.py:441
  49.4 6.7 %collective-permute-start.1 = (bf16[128,2560]{1,0:T(8,128)(2,1)S(1)}, bf16[128,2560]{1,0:T(8,128)(2,1)S(1)}, u32[]{:S(2)}, u32[]{:S(2)}) collective-permute-start(bf16[128,2560]{1,0:T(8,128)(2,1)S(1)} %get-tuple-element.18), channel_id=1, source_target_pairs={{0,3},{1,2},{2,1},{3,0},{4,5},{5,4},{6,7},{7,6},{8,11},{9,10},{10,... | collective-permute-start | bytes 1966088 | tf_op jit(solution)/shard_map/ppermute | solution.py:441
  56.2 2.3 %collective-permute-done.3.got = bf16[128,2560]{1,0:T(8,128)(2,1)S(1)} collective-permute-done((bf16[128,2560]{1,0:T(8,128)(2,1)S(1)}, bf16[128,2560]{1,0:T(8,128)(2,1)S(1)}, u32[]{:S(2)}, u32[]{:S(2)}) %collective-permute-start.3) | collective-permute-done | bytes 655392 | tf_op jit(solution)/shard_map/ppermute | solution.py:441
  59.2 10.5 %collective-permute-done.1.got = bf16[128,2560]{1,0:T(8,128)(2,1)S(1)} collective-permute-done((bf16[128,2560]{1,0:T(8,128)(2,1)S(1)}, bf16[128,2560]{1,0:T(8,128)(2,1)S(1)}, u32[]{:S(2)}, u32[]{:S(2)}) %collective-permute-start.1) | collective-permute-done | bytes 655392 | tf_op jit(solution)/shard_map/ppermute | solution.py:441
  69.9 0.9 collective-permute-start.2
  71.0 0.8 copy-done.1
  71.8 4.6 %backward.2 = bf16[32,40,512]{2,1,0:T(8,128)(2,1)} custom-call(s32[16]{0:T(128)S(1)} %concatenate.19.meta, s32[2]{0:T(128)S(1)} %get-tuple-element.31.halves, f32[2]{0:T(128)S(1)} %get-tuple-element.29.rate, f32[1,2688]{1,0:T(1,128)S(1)} %bitcast.30, bf16[128,2560]{1,0:T(8,128)(2,1)S(1)} %scale.2.first_part, bf16[128,2560]{1,0:T(8,128)(2,1)S(1)} %scale.3.second_part, ...), custom_call_target="tpu_custom_call" | custom-call | flops 49999998976 | bytes 10000000 | tf_op jit(solution)/shard_map/backward/pallas_call | solution.py:341
  76.5 5.9 %all-to-all-start.2 = ((bf16[32,40,512]{2,1,0:T(8,128)(2,1)}), bf16[32,40,512]{2,1,0:T(8,128)(2,1)}, u32[]{:S(2)}, u32[]{:S(2)}) async-start(bf16[32,40,512]{2,1,0:T(8,128)(2,1)} %backward.2), calls=%async_computation.2 | async-start | bytes 2621440 | tf_op jit(solution)/shard_map/all_to_all | solution.py:474
  82.4 2.4 %collective-permute-start.5 = (bf16[128,2560]{1,0:T(8,128)(2,1)}, bf16[128,2560]{1,0:T(8,128)(2,1)S(1)}, u32[]{:S(2)}, u32[]{:S(2)}) collective-permute-start(bf16[128,2560]{1,0:T(8,128)(2,1)} %copy-done.1), channel_id=1, source_target_pairs={{0,3},{1,2},{2,1},{3,0},{4,5},{5,4},{6,7},{7,6},{8,11},{9,10},{10,... | collective-permute-start | bytes 1966088 | tf_op jit(solution)/shard_map/ppermute | solution.py:441
  84.8 1.1 relay.1.first_part
  85.9 8.6 %collective-permute-done.5.second_part = bf16[128,2560]{1,0:T(8,128)(2,1)S(1)} collective-permute-done((bf16[128,2560]{1,0:T(8,128)(2,1)}, bf16[128,2560]{1,0:T(8,128)(2,1)S(1)}, u32[]{:S(2)}, u32[]{:S(2)}) %collective-permute-start.5) | collective-permute-done | bytes 655392 | tf_op jit(solution)/shard_map/ppermute | solution.py:441
  94.5 4.7 %backward.3 = bf16[32,40,512]{2,1,0:T(8,128)(2,1)} custom-call(s32[16]{0:T(128)S(1)} %concatenate.19.meta, s32[2]{0:T(128)S(1)} %get-tuple-element.30.halves, f32[2]{0:T(128)S(1)} %get-tuple-element.29.rate, f32[1,2688]{1,0:T(1,128)S(1)} %bitcast.31, bf16[128,2560]{1,0:T(8,128)(2,1)S(1)} %relay.1.first_part, ...), custom_call_target="tpu_custom_call" | custom-call | flops 2000000000 | bytes 10000000 | tf_op jit(solution)/shard_map/backward/pallas_call | solution.py:341
  99.2 4.0 %all-to-all-done.2.payload = bf16[32,40,512]{2,1,0:T(8,128)(2,1)} async-done(((bf16[32,40,512]{2,1,0:T(8,128)(2,1)}), bf16[32,40,512]{2,1,0:T(8,128)(2,1)}, u32[]{:S(2)}, u32[]{:S(2)}) %all-to-all-start.2) | async-done | bytes 1310752 | tf_op jit(solution)/shard_map/all_to_all | solution.py:474
  103.2 4.0 %all-to-all-start.1 = ((bf16[32,40,512]{2,1,0:T(8,128)(2,1)}), bf16[32,40,512]{2,1,0:T(8,128)(2,1)S(1)}, u32[]{:S(2)}, u32[]{:S(2)}) async-start(bf16[32,40,512]{2,1,0:T(8,128)(2,1)} %backward.3), calls=%async_computation.1 | async-start | bytes 2621440 | tf_op jit(solution)/shard_map/all_to_all | solution.py:474
  107.2 3.0 %unpack.2 = (bf16[20,64,512]{2,1,0:T(8,128)(2,1)}, bf16[20,64,512]{2,1,0:T(8,128)(2,1)}) custom-call(s32[2]{0:T(128)S(1)} %get-tuple-element.33.halves, bf16[32,40,512]{2,1,0:T(8,128)(2,1)} %all-to-all-done.2.payload), custom_call_target="tpu_custom_call" | custom-call | tf_op jit(solution)/shard_map/unpack/pallas_call | solution.py:127
  110.2 17.7 %all-to-all-done.1.payload = bf16[32,40,512]{2,1,0:T(8,128)(2,1)S(1)} async-done(((bf16[32,40,512]{2,1,0:T(8,128)(2,1)}), bf16[32,40,512]{2,1,0:T(8,128)(2,1)S(1)}, u32[]{:S(2)}, u32[]{:S(2)}) %all-to-all-start.1) | async-done | bytes 1310752 | tf_op jit(solution)/shard_map/all_to_all | solution.py:474
  127.9 2.2 %unpack.3 = (bf16[20,64,512]{2,1,0:T(8,128)(2,1)}, bf16[20,64,512]{2,1,0:T(8,128)(2,1)}) custom-call(s32[2]{0:T(128)S(1)} %get-tuple-element.32.halves, bf16[32,40,512]{2,1,0:T(8,128)(2,1)S(1)} %all-to-all-done.1.payload, bf16[20,64,512]{2,1,0:T(8,128)(2,1)} %get-tuple-element.26.refs_0_, ...), custom_call_target="tpu_custom_call", output_to_operand_aliasing={{0}: (2, {}), {1}: (3, {})} | custom-call | tf_op jit(solution)/shard_map/unpack/pallas_call | solution.py:127
  (52 shorter events, 3.6 us)
Async XLA Ops:
  3.8 7.6 %copy-start.3 = (s32[2]{0:T(128)S(1)}, s32[2]{0:T(128)}, u32[]{:S(2)}) copy-start(s32[2]{0:T(128)} %param.10) | copy-start | bytes 28
  3.8 13.7 %copy-start.2 = (s32[2560]{0:T(1024)S(1)}, s32[2560]{0:T(1024)}, u32[]{:S(2)}) copy-start(s32[2560]{0:T(1024)} %param.11) | copy-start | bytes 30724
  3.8 14.4 %copy-start.4 = (f32[640]{0:T(1024)S(1)}, f32[640]{0:T(1024)}, u32[]{:S(2)}) copy-start(f32[640]{0:T(1024)} %param.7) | copy-start | bytes 7684
  3.8 28.3 %all-to-all-start = ((bf16[32,40,512]{2,1,0:T(8,128)(2,1)}), bf16[32,40,512]{2,1,0:T(8,128)(2,1)S(1)}, u32[]{:S(2)}, u32[]{:S(2)}) async-start(bf16[32,40,512]{2,1,0:T(8,128)(2,1)} %pack.1), calls=%async_computation | async-start | bytes 2621440 | tf_op jit(solution)/shard_map/all_to_all | solution.py:443
  38.2 10.9 %collective-permute-start = (bf16[128,2560]{1,0:T(8,128)(2,1)S(1)}, bf16[128,2560]{1,0:T(8,128)(2,1)S(1)}, u32[]{:S(2)}, u32[]{:S(2)}) collective-permute-start(bf16[128,2560]{1,0:T(8,128)(2,1)S(1)} %get-tuple-element.16), channel_id=1, source_target_pairs={{0,1},{1,0},{2,3},{3,2},{4,7},{5,6},{6,5},{7,4},{8,9},{9,8},{10,11... | collective-permute-start | bytes 1966088 | tf_op jit(solution)/shard_map/ppermute | solution.py:441
  46.4 24.6 %copy-start = (bf16[1280,2688]{1,0:T(8,128)(2,1)}, bf16[1280,2688]{1,0:T(8,128)(2,1)S(1)}, u32[]{:S(2)}) copy-start(bf16[1280,2688]{1,0:T(8,128)(2,1)S(1)} %get-tuple-element.23.table) | copy-start | bytes 20643844
  46.4 12.1 %collective-permute-start.3 = (bf16[128,2560]{1,0:T(8,128)(2,1)S(1)}, bf16[128,2560]{1,0:T(8,128)(2,1)S(1)}, u32[]{:S(2)}, u32[]{:S(2)}) collective-permute-start(bf16[128,2560]{1,0:T(8,128)(2,1)S(1)} %get-tuple-element.20), channel_id=1, source_target_pairs={{0,3},{1,2},{2,1},{3,0},{4,5},{5,4},{6,7},{7,6},{8,11},{9,10},{10,... | collective-permute-start | bytes 1966088 | tf_op jit(solution)/shard_map/ppermute | solution.py:441
  49.4 20.3 %collective-permute-start.1 = (bf16[128,2560]{1,0:T(8,128)(2,1)S(1)}, bf16[128,2560]{1,0:T(8,128)(2,1)S(1)}, u32[]{:S(2)}, u32[]{:S(2)}) collective-permute-start(bf16[128,2560]{1,0:T(8,128)(2,1)S(1)} %get-tuple-element.18), channel_id=1, source_target_pairs={{0,3},{1,2},{2,1},{3,0},{4,5},{5,4},{6,7},{7,6},{8,11},{9,10},{10,... | collective-permute-start | bytes 1966088 | tf_op jit(solution)/shard_map/ppermute | solution.py:441
  58.7 12.1 %collective-permute-start.4 = (bf16[128,2560]{1,0:T(8,128)(2,1)S(1)}, bf16[128,2560]{1,0:T(8,128)(2,1)S(1)}, u32[]{:S(2)}, u32[]{:S(2)}) collective-permute-start(bf16[128,2560]{1,0:T(8,128)(2,1)S(1)} %get-tuple-element.22), channel_id=1, source_target_pairs={{0,1},{1,0},{2,3},{3,2},{4,7},{5,6},{6,5},{7,4},{8,9},{9,8},{10,11... | collective-permute-start | bytes 1966088 | tf_op jit(solution)/shard_map/ppermute | solution.py:441
  69.9 14.9 %collective-permute-start.2 = (bf16[128,2560]{1,0:T(8,128)(2,1)S(1)}, bf16[128,2560]{1,0:T(8,128)(2,1)}, u32[]{:S(2)}, u32[]{:S(2)}) collective-permute-start(bf16[128,2560]{1,0:T(8,128)(2,1)S(1)} %scale.2.first_part), channel_id=1, source_target_pairs={{0,1},{1,0},{2,3},{3,2},{4,7},{5,6},{6,5},{7,4},{8,9},{9,8},{10,11... | collective-permute-start | bytes 1966088 | tf_op jit(solution)/shard_map/ppermute | solution.py:441
  71.0 0.8 copy-start.1
  76.5 18.0 %slice-start = ((s8[6881280]{0:T(1024)(128)(4,1)}), s8[2686976]{0:T(1024)(128)(4,1)S(1)}, s32[]{:S(2)}) async-start(s8[6881280]{0:T(1024)(128)(4,1)} %bitcast.26), calls=%async_computation.3 | async-start | bytes 5373952
  76.5 26.7 %all-to-all-start.2 = ((bf16[32,40,512]{2,1,0:T(8,128)(2,1)}), bf16[32,40,512]{2,1,0:T(8,128)(2,1)}, u32[]{:S(2)}, u32[]{:S(2)}) async-start(bf16[32,40,512]{2,1,0:T(8,128)(2,1)} %backward.2), calls=%async_computation.2 | async-start | bytes 2621440 | tf_op jit(solution)/shard_map/all_to_all | solution.py:474
  82.4 12.1 %slice-start.1 = ((s8[6881280]{0:T(1024)(128)(4,1)}), s8[4194304]{0:T(1024)(128)(4,1)S(1)}, s32[]{:S(2)}) async-start(s8[6881280]{0:T(1024)(128)(4,1)} %bitcast.26), calls=%async_computation.4 | async-start | bytes 8388608
  82.4 12.1 %collective-permute-start.5 = (bf16[128,2560]{1,0:T(8,128)(2,1)}, bf16[128,2560]{1,0:T(8,128)(2,1)S(1)}, u32[]{:S(2)}, u32[]{:S(2)}) collective-permute-start(bf16[128,2560]{1,0:T(8,128)(2,1)} %copy-done.1), channel_id=1, source_target_pairs={{0,3},{1,2},{2,1},{3,0},{4,5},{5,4},{6,7},{7,6},{8,11},{9,10},{10,... | collective-permute-start | bytes 1966088 | tf_op jit(solution)/shard_map/ppermute | solution.py:441
  103.2 24.8 %all-to-all-start.1 = ((bf16[32,40,512]{2,1,0:T(8,128)(2,1)}), bf16[32,40,512]{2,1,0:T(8,128)(2,1)S(1)}, u32[]{:S(2)}, u32[]{:S(2)}) async-start(bf16[32,40,512]{2,1,0:T(8,128)(2,1)} %backward.3), calls=%async_computation.1 | async-start | bytes 2621440 | tf_op jit(solution)/shard_map/all_to_all | solution.py:474

commit v9 on v8

--- a/solution.py
+++ b/solution.py
@@ -1,3 +1,5 @@
+import functools
+
 import jax
 import jax.numpy as jnp
 from jax import lax
@@ -274,7 +276,11 @@
     )(meta, rate, mask, weight, recv, *in_hbm(table), factor)
 
 
-def backward_kernel(meta, halves, rate, mask, first_part, second_part, table, out_ref, every, masked, last, out, sems):
+def backward_kernel(passes, meta, halves, rate, mask, first_part, second_part, table, out_ref, *refs):
+    every, masked, last, out, sems = refs[passes:passes + 5]
+    if passes:
+        passed = pltpu.make_async_copy(second_part, refs[0], refs[-1])
+        passed.start()
     levels = first_part.shape[0]
     quarter = table.shape[0] // 2
     owners = out.shape[0]
@@ -333,24 +339,26 @@
         sent[n].start()
     for copy in sent:
         copy.wait()
-
-
-def backward(meta, halves, rate, mask, first_part, second_part, table, payload, flops):
+    if passes:
+        passed.wait()
+
+
+def backward(passes, meta, halves, rate, mask, first_part, second_part, table, payload, flops):
     levels = first_part.shape[0]
     owners, both, width = payload
     return call(
-        backward_kernel,
+        functools.partial(backward_kernel, passes),
         "backward",
         in_specs=[IN_SMEM] * 3 + [IN_VMEM] * 4,
-        out_specs=IN_PLACE,
-        out_shape=pltpu.HBM(payload, BF16),
+        out_specs=[IN_PLACE] * (1 + passes),
+        out_shape=[pltpu.HBM(payload, BF16), pltpu.HBM(second_part.shape, BF16)][:1 + passes],
         scratch_shapes=[
             pltpu.VMEM((2 * levels, SENT), BF16),
             pltpu.VMEM((2, 2 * levels, (SURE[0] + SHARED) * TILE), BF16),
             pltpu.VMEM((2, owners * 4, 4 * levels), BF16),
             pltpu.VMEM(payload, BF16),
             pltpu.SemaphoreType.DMA((2,)),
-        ],
+        ] + [pltpu.SemaphoreType.DMA] * passes,
         cost_estimate=pl.CostEstimate(flops=flops, bytes_accessed=10**7, transcendentals=0),
     )(meta, halves, rate, mask, first_part, second_part, table)
 
@@ -466,11 +474,10 @@
     mine_b = scale(kept_b, swap(sent_b, ways[0]), factor)
     kept_halves = jnp.stack([meta[HALF] for meta in metas])
     theirs_a = swap(mine_a, ways[0])
-    kept = backward(metas[0], kept_halves, rate, mask, mine_a, mine_b, table, received.shape, 50000000000)
-    mine_b, kept = lax.optimization_barrier((mine_b, kept))
+    kept, mine_b = backward(1, metas[0], kept_halves, rate, mask, mine_a, mine_b, table, received.shape, 50000000000)
     theirs_b = swap(mine_b, ways[1])
     theirs_a = relay(theirs_a)
-    others = backward(metas[0], 1 - kept_halves, rate, mask, theirs_a, theirs_b, table, received.shape, 2000000000)
+    others, = backward(0, metas[0], 1 - kept_halves, rate, mask, theirs_a, theirs_b, table, received.shape, 2000000000)
     kept, others = (lax.all_to_all(x, "ma", 0, 0, tiled=True) for x in (kept, others))
     halves = jnp.stack(halves).astype(jnp.int32)
     return tuple(unpack(1 - halves, others, rows, unpack(halves, kept, rows)))

time: 131 us -> 130 us (level)
  no operation moved by 1% of the time
where the time goes in v9:
time: 130 us
  waiting for transfers between devices  46.5 us (36%)
  Pallas kernels  41.5 us (32%)
  starting transfers between devices  32.6 us (25%)
  between operations  6.49 us (5%)
  local copies, waits for them, and re-layouts  1.39 us (1%)
    all_to_all x2, waiting for transfers between devices, on_device(): lax.all_to_all(x, 'ma', 0, 0, tiled=True)  21.7 us
    ppermute x6, waiting for transfers between devices, swap(): return lax.ppermute(x, ('ma', 'oct'), pairs)  21.4 us
    ppermute x6, starting transfers between devices, swap(): return lax.ppermute(x, ('ma', 'oct'), pairs)  15.2 us
    pallas_call x2, Pallas kernels, forward(): call(forward_kernel, 'forward', in_specs=[IN_SMEM] * 2 + [IN_VMEM] * 3 +...  12.3 us
    all_to_all x2, starting transfers between devices, on_device(): lax.all_to_all(x, 'ma', 0, 0, tiled=True)  9.85 us
    pallas_call x1, Pallas kernels, keep(): call(keep_kernel, 'keep', out_shape=pltpu.HBM(shape, BF16), in_specs=[IN_...  9.55 us
    pallas_call x2, Pallas kernels, backward(): call(functools.partial(backward_kernel, passes), 'backward', in_specs=[IN...  9.32 us
    all_to_all x1, starting transfers between devices, on_device(): received = lax.all_to_all(pack(fourier_wind), 'ma', 0, 0, tiled=True)  7.54 us
  transfers between devices with their start and end apart: 9, of which 6 were waited for; matrix products, arithmetic and copies ran while one was open for 2% of the time, Pallas kernels for 23%

profile of v9, /device:TPU:0, one launch (start us, length us, event | category | flops | bytes accessed | tf_op | source)
XLA Modules:
  0.0 129.5 jit_solution(14918173729309546392)
XLA Ops:
  0.6 3.1 %pack.1 = bf16[32,40,512]{2,1,0:T(8,128)(2,1)} custom-call(bf16[20,64,512]{2,1,0:T(8,128)(2,1)} %wind_ref.1), custom_call_target="tpu_custom_call" | custom-call | tf_op jit(solution)/shard_map/pack/pallas_call | solution.py:75
  3.8 7.5 %all-to-all-start = ((bf16[32,40,512]{2,1,0:T(8,128)(2,1)}), bf16[32,40,512]{2,1,0:T(8,128)(2,1)S(1)}, u32[]{:S(2)}, u32[]{:S(2)}) async-start(bf16[32,40,512]{2,1,0:T(8,128)(2,1)} %pack.1), calls=%async_computation | async-start | bytes 2621440 | tf_op jit(solution)/shard_map/all_to_all | solution.py:451
  11.3 0.6 fusion.6
  19.0 9.5 %keep.1.table = bf16[1280,2688]{1,0:T(8,128)(2,1)} custom-call(s32[16]{0:T(128)S(1)} %concatenate.22.meta, bf16[640,640]{1,0:T(8,128)(2,1)S(1)} %fusion.select, bf16[2,640,2560]{2,1,0:T(8,128)(2,1)} %p_ref.1, bf16[2,640,2560]{2,1,0:T(8,128)(2,1)} %h_ref.1), custom_call_target="tpu_custom_call" | custom-call | tf_op jit(solution)/shard_map/keep/pallas_call | solution.py:182
  28.7 3.4 %all-to-all-done.recv = bf16[32,40,512]{2,1,0:T(8,128)(2,1)S(1)} async-done(((bf16[32,40,512]{2,1,0:T(8,128)(2,1)}), bf16[32,40,512]{2,1,0:T(8,128)(2,1)S(1)}, u32[]{:S(2)}, u32[]{:S(2)}) %all-to-all-start) | async-done | bytes 1310752 | tf_op jit(solution)/shard_map/all_to_all | solution.py:451
  32.1 6.1 %forward.2 = (f32[128,2560]{1,0:T(8,128)S(1)}, bf16[128,2560]{1,0:T(8,128)(2,1)S(1)}) custom-call(s32[16]{0:T(128)S(1)} %concatenate.19.meta, f32[2]{0:T(128)S(1)} %get-tuple-element.29.rate, f32[1,2688]{1,0:T(1,128)S(1)} %bitcast.28, f32[640,1]{1,0:T(8,128)S(1)} %broadcast_in_dim.44.weight, bf16[32,40,512]{2,1,0:T(8,128)(2,1)S(1)} %all-to-all-done.recv, ...), custom_call_target="tpu_custom_call" | custom-call | flops 5000000000 | bytes 10000000 | tf_op jit(solution)/shard_map/forward/pallas_call | solution.py:268
  38.3 2.0 %collective-permute-start = (bf16[128,2560]{1,0:T(8,128)(2,1)S(1)}, bf16[128,2560]{1,0:T(8,128)(2,1)S(1)}, u32[]{:S(2)}, u32[]{:S(2)}) collective-permute-start(bf16[128,2560]{1,0:T(8,128)(2,1)S(1)} %get-tuple-element.16), channel_id=1, source_target_pairs={{0,1},{1,0},{2,3},{3,2},{4,7},{5,6},{6,5},{7,4},{8,9},{9,8},{10,11... | collective-permute-start | bytes 1966088 | tf_op jit(solution)/shard_map/ppermute | solution.py:449
  40.2 6.2 %forward.3 = (f32[128,2560]{1,0:T(8,128)S(1)}, bf16[128,2560]{1,0:T(8,128)(2,1)S(1)}, bf16[1280,2688]{1,0:T(8,128)(2,1)S(1)}) custom-call(s32[16]{0:T(128)S(1)} %concatenate.22.meta, f32[2]{0:T(128)S(1)} %get-tuple-element.28.rate, f32[1,2688]{1,0:T(1,128)S(1)} %bitcast.29, f32[640,1]{1,0:T(8,128)S(1)} %broadcast_in_dim.44.weight, ...), custom_call_target="tpu_custom_call" | custom-call | flops 5000000000 | bytes 10000000 | tf_op jit(solution)/shard_map/forward/pallas_call | solution.py:268
  46.4 2.8 %collective-permute-start.3 = (bf16[128,2560]{1,0:T(8,128)(2,1)S(1)}, bf16[128,2560]{1,0:T(8,128)(2,1)S(1)}, u32[]{:S(2)}, u32[]{:S(2)}) collective-permute-start(bf16[128,2560]{1,0:T(8,128)(2,1)S(1)} %get-tuple-element.20), channel_id=1, source_target_pairs={{0,3},{1,2},{2,1},{3,0},{4,5},{5,4},{6,7},{7,6},{8,11},{9,10},{10,... | collective-permute-start | bytes 1966088 | tf_op jit(solution)/shard_map/ppermute | solution.py:449
  49.4 6.7 %collective-permute-start.1 = (bf16[128,2560]{1,0:T(8,128)(2,1)S(1)}, bf16[128,2560]{1,0:T(8,128)(2,1)S(1)}, u32[]{:S(2)}, u32[]{:S(2)}) collective-permute-start(bf16[128,2560]{1,0:T(8,128)(2,1)S(1)} %get-tuple-element.18), channel_id=1, source_target_pairs={{0,3},{1,2},{2,1},{3,0},{4,5},{5,4},{6,7},{7,6},{8,11},{9,10},{10,... | collective-permute-start | bytes 1966088 | tf_op jit(solution)/shard_map/ppermute | solution.py:449
  56.2 2.3 %collective-permute-done.3.got = bf16[128,2560]{1,0:T(8,128)(2,1)S(1)} collective-permute-done((bf16[128,2560]{1,0:T(8,128)(2,1)S(1)}, bf16[128,2560]{1,0:T(8,128)(2,1)S(1)}, u32[]{:S(2)}, u32[]{:S(2)}) %collective-permute-start.3) | collective-permute-done | bytes 655392 | tf_op jit(solution)/shard_map/ppermute | solution.py:449
  59.2 10.5 %collective-permute-done.1.got = bf16[128,2560]{1,0:T(8,128)(2,1)S(1)} collective-permute-done((bf16[128,2560]{1,0:T(8,128)(2,1)S(1)}, bf16[128,2560]{1,0:T(8,128)(2,1)S(1)}, u32[]{:S(2)}, u32[]{:S(2)}) %collective-permute-start.1) | collective-permute-done | bytes 655392 | tf_op jit(solution)/shard_map/ppermute | solution.py:449
  69.9 0.9 collective-permute-start.2
  71.0 4.7 %backward.2 = (bf16[32,40,512]{2,1,0:T(8,128)(2,1)}, bf16[128,2560]{1,0:T(8,128)(2,1)}) custom-call(s32[16]{0:T(128)S(1)} %concatenate.19.meta, s32[2]{0:T(128)S(1)} %get-tuple-element.31.halves, f32[2]{0:T(128)S(1)} %get-tuple-element.29.rate, f32[1,2688]{1,0:T(1,128)S(1)} %bitcast.30, bf16[128,2560]{1,0:T(8,128)(2,1)S(1)} %scale.2.first_part, ...), custom_call_target="tpu_custom_call" | custom-call | flops 49999998976 | bytes 10000000 | tf_op jit(solution)/shard_map/backward/pallas_call | solution.py:349
  75.7 5.9 %all-to-all-start.2 = ((bf16[32,40,512]{2,1,0:T(8,128)(2,1)}), bf16[32,40,512]{2,1,0:T(8,128)(2,1)}, u32[]{:S(2)}, u32[]{:S(2)}) async-start(bf16[32,40,512]{2,1,0:T(8,128)(2,1)} %get-tuple-element.25), calls=%async_computation.2 | async-start | bytes 2621440 | tf_op jit(solution)/shard_map/all_to_all | solution.py:481
  81.6 2.4 %collective-permute-start.5 = (bf16[128,2560]{1,0:T(8,128)(2,1)}, bf16[128,2560]{1,0:T(8,128)(2,1)S(1)}, u32[]{:S(2)}, u32[]{:S(2)}) collective-permute-start(bf16[128,2560]{1,0:T(8,128)(2,1)} %get-tuple-element.24), channel_id=1, source_target_pairs={{0,3},{1,2},{2,1},{3,0},{4,5},{5,4},{6,7},{7,6},{8,11},{9,10},{10,... | collective-permute-start | bytes 1966088 | tf_op jit(solution)/shard_map/ppermute | solution.py:449
  84.0 1.1 relay.1.first_part
  85.1 8.6 %collective-permute-done.5.second_part = bf16[128,2560]{1,0:T(8,128)(2,1)S(1)} collective-permute-done((bf16[128,2560]{1,0:T(8,128)(2,1)}, bf16[128,2560]{1,0:T(8,128)(2,1)S(1)}, u32[]{:S(2)}, u32[]{:S(2)}) %collective-permute-start.5) | collective-permute-done | bytes 655392 | tf_op jit(solution)/shard_map/ppermute | solution.py:449
  93.7 4.7 %backward.3 = bf16[32,40,512]{2,1,0:T(8,128)(2,1)} custom-call(s32[16]{0:T(128)S(1)} %concatenate.19.meta, s32[2]{0:T(128)S(1)} %get-tuple-element.30.halves, f32[2]{0:T(128)S(1)} %get-tuple-element.29.rate, f32[1,2688]{1,0:T(1,128)S(1)} %bitcast.31, bf16[128,2560]{1,0:T(8,128)(2,1)S(1)} %relay.1.first_part, ...), custom_call_target="tpu_custom_call" | custom-call | flops 2000000000 | bytes 10000000 | tf_op jit(solution)/shard_map/backward/pallas_call | solution.py:349
  98.3 4.0 %all-to-all-done.2.payload = bf16[32,40,512]{2,1,0:T(8,128)(2,1)} async-done(((bf16[32,40,512]{2,1,0:T(8,128)(2,1)}), bf16[32,40,512]{2,1,0:T(8,128)(2,1)}, u32[]{:S(2)}, u32[]{:S(2)}) %all-to-all-start.2) | async-done | bytes 1310752 | tf_op jit(solution)/shard_map/all_to_all | solution.py:481
  102.4 4.0 %all-to-all-start.1 = ((bf16[32,40,512]{2,1,0:T(8,128)(2,1)}), bf16[32,40,512]{2,1,0:T(8,128)(2,1)S(1)}, u32[]{:S(2)}, u32[]{:S(2)}) async-start(bf16[32,40,512]{2,1,0:T(8,128)(2,1)} %backward.3), calls=%async_computation.1 | async-start | bytes 2621440 | tf_op jit(solution)/shard_map/all_to_all | solution.py:481
  106.4 3.0 %unpack.2 = (bf16[20,64,512]{2,1,0:T(8,128)(2,1)}, bf16[20,64,512]{2,1,0:T(8,128)(2,1)}) custom-call(s32[2]{0:T(128)S(1)} %get-tuple-element.33.halves, bf16[32,40,512]{2,1,0:T(8,128)(2,1)} %all-to-all-done.2.payload), custom_call_target="tpu_custom_call" | custom-call | tf_op jit(solution)/shard_map/unpack/pallas_call | solution.py:129
  109.4 17.7 %all-to-all-done.1.payload = bf16[32,40,512]{2,1,0:T(8,128)(2,1)S(1)} async-done(((bf16[32,40,512]{2,1,0:T(8,128)(2,1)}), bf16[32,40,512]{2,1,0:T(8,128)(2,1)S(1)}, u32[]{:S(2)}, u32[]{:S(2)}) %all-to-all-start.1) | async-done | bytes 1310752 | tf_op jit(solution)/shard_map/all_to_all | solution.py:481
  127.1 2.2 %unpack.3 = (bf16[20,64,512]{2,1,0:T(8,128)(2,1)}, bf16[20,64,512]{2,1,0:T(8,128)(2,1)}) custom-call(s32[2]{0:T(128)S(1)} %get-tuple-element.32.halves, bf16[32,40,512]{2,1,0:T(8,128)(2,1)S(1)} %all-to-all-done.1.payload, bf16[20,64,512]{2,1,0:T(8,128)(2,1)} %get-tuple-element.26.refs_0_, ...), custom_call_target="tpu_custom_call", output_to_operand_aliasing={{0}: (2, {}), {1}: (3, {})} | custom-call | tf_op jit(solution)/shard_map/unpack/pallas_call | solution.py:129
  (50 shorter events, 3.1 us)
Async XLA Ops:
  3.8 7.6 %copy-start.2 = (s32[2]{0:T(128)S(1)}, s32[2]{0:T(128)}, u32[]{:S(2)}) copy-start(s32[2]{0:T(128)} %param.10) | copy-start | bytes 28
  3.8 13.7 %copy-start.1 = (s32[2560]{0:T(1024)S(1)}, s32[2560]{0:T(1024)}, u32[]{:S(2)}) copy-start(s32[2560]{0:T(1024)} %param.11) | copy-start | bytes 30724
  3.8 14.4 %copy-start.3 = (f32[640]{0:T(1024)S(1)}, f32[640]{0:T(1024)}, u32[]{:S(2)}) copy-start(f32[640]{0:T(1024)} %param.7) | copy-start | bytes 7684
  3.8 28.3 %all-to-all-start = ((bf16[32,40,512]{2,1,0:T(8,128)(2,1)}), bf16[32,40,512]{2,1,0:T(8,128)(2,1)S(1)}, u32[]{:S(2)}, u32[]{:S(2)}) async-start(bf16[32,40,512]{2,1,0:T(8,128)(2,1)} %pack.1), calls=%async_computation | async-start | bytes 2621440 | tf_op jit(solution)/shard_map/all_to_all | solution.py:451
  38.3 11.0 %collective-permute-start = (bf16[128,2560]{1,0:T(8,128)(2,1)S(1)}, bf16[128,2560]{1,0:T(8,128)(2,1)S(1)}, u32[]{:S(2)}, u32[]{:S(2)}) collective-permute-start(bf16[128,2560]{1,0:T(8,128)(2,1)S(1)} %get-tuple-element.16), channel_id=1, source_target_pairs={{0,1},{1,0},{2,3},{3,2},{4,7},{5,6},{6,5},{7,4},{8,9},{9,8},{10,11... | collective-permute-start | bytes 1966088 | tf_op jit(solution)/shard_map/ppermute | solution.py:449
  46.4 24.6 %copy-start = (bf16[1280,2688]{1,0:T(8,128)(2,1)}, bf16[1280,2688]{1,0:T(8,128)(2,1)S(1)}, u32[]{:S(2)}) copy-start(bf16[1280,2688]{1,0:T(8,128)(2,1)S(1)} %get-tuple-element.23.table) | copy-start | bytes 20643844
  46.4 12.1 %collective-permute-start.3 = (bf16[128,2560]{1,0:T(8,128)(2,1)S(1)}, bf16[128,2560]{1,0:T(8,128)(2,1)S(1)}, u32[]{:S(2)}, u32[]{:S(2)}) collective-permute-start(bf16[128,2560]{1,0:T(8,128)(2,1)S(1)} %get-tuple-element.20), channel_id=1, source_target_pairs={{0,3},{1,2},{2,1},{3,0},{4,5},{5,4},{6,7},{7,6},{8,11},{9,10},{10,... | collective-permute-start | bytes 1966088 | tf_op jit(solution)/shard_map/ppermute | solution.py:449
  49.4 20.3 %collective-permute-start.1 = (bf16[128,2560]{1,0:T(8,128)(2,1)S(1)}, bf16[128,2560]{1,0:T(8,128)(2,1)S(1)}, u32[]{:S(2)}, u32[]{:S(2)}) collective-permute-start(bf16[128,2560]{1,0:T(8,128)(2,1)S(1)} %get-tuple-element.18), channel_id=1, source_target_pairs={{0,3},{1,2},{2,1},{3,0},{4,5},{5,4},{6,7},{7,6},{8,11},{9,10},{10,... | collective-permute-start | bytes 1966088 | tf_op jit(solution)/shard_map/ppermute | solution.py:449
  58.7 12.1 %collective-permute-start.4 = (bf16[128,2560]{1,0:T(8,128)(2,1)S(1)}, bf16[128,2560]{1,0:T(8,128)(2,1)S(1)}, u32[]{:S(2)}, u32[]{:S(2)}) collective-permute-start(bf16[128,2560]{1,0:T(8,128)(2,1)S(1)} %get-tuple-element.22), channel_id=1, source_target_pairs={{0,1},{1,0},{2,3},{3,2},{4,7},{5,6},{6,5},{7,4},{8,9},{9,8},{10,11... | collective-permute-start | bytes 1966088 | tf_op jit(solution)/shard_map/ppermute | solution.py:449
  69.9 14.1 %collective-permute-start.2 = (bf16[128,2560]{1,0:T(8,128)(2,1)S(1)}, bf16[128,2560]{1,0:T(8,128)(2,1)}, u32[]{:S(2)}, u32[]{:S(2)}) collective-permute-start(bf16[128,2560]{1,0:T(8,128)(2,1)S(1)} %scale.2.first_part), channel_id=1, source_target_pairs={{0,1},{1,0},{2,3},{3,2},{4,7},{5,6},{6,5},{7,4},{8,9},{9,8},{10,11... | collective-permute-start | bytes 1966088 | tf_op jit(solution)/shard_map/ppermute | solution.py:449
  75.7 18.0 %slice-start = ((s8[6881280]{0:T(1024)(128)(4,1)}), s8[2686976]{0:T(1024)(128)(4,1)S(1)}, s32[]{:S(2)}) async-start(s8[6881280]{0:T(1024)(128)(4,1)} %bitcast.26), calls=%async_computation.3 | async-start | bytes 5373952
  75.7 26.7 %all-to-all-start.2 = ((bf16[32,40,512]{2,1,0:T(8,128)(2,1)}), bf16[32,40,512]{2,1,0:T(8,128)(2,1)}, u32[]{:S(2)}, u32[]{:S(2)}) async-start(bf16[32,40,512]{2,1,0:T(8,128)(2,1)} %get-tuple-element.25), calls=%async_computation.2 | async-start | bytes 2621440 | tf_op jit(solution)/shard_map/all_to_all | solution.py:481
  81.6 12.1 %slice-start.1 = ((s8[6881280]{0:T(1024)(128)(4,1)}), s8[4194304]{0:T(1024)(128)(4,1)S(1)}, s32[]{:S(2)}) async-start(s8[6881280]{0:T(1024)(128)(4,1)} %bitcast.26), calls=%async_computation.4 | async-start | bytes 8388608
  81.6 12.1 %collective-permute-start.5 = (bf16[128,2560]{1,0:T(8,128)(2,1)}, bf16[128,2560]{1,0:T(8,128)(2,1)S(1)}, u32[]{:S(2)}, u32[]{:S(2)}) collective-permute-start(bf16[128,2560]{1,0:T(8,128)(2,1)} %get-tuple-element.24), channel_id=1, source_target_pairs={{0,3},{1,2},{2,1},{3,0},{4,5},{5,4},{6,7},{7,6},{8,11},{9,10},{10,... | collective-permute-start | bytes 1966088 | tf_op jit(solution)/shard_map/ppermute | solution.py:449
  102.4 24.8 %all-to-all-start.1 = ((bf16[32,40,512]{2,1,0:T(8,128)(2,1)}), bf16[32,40,512]{2,1,0:T(8,128)(2,1)S(1)}, u32[]{:S(2)}, u32[]{:S(2)}) async-start(bf16[32,40,512]{2,1,0:T(8,128)(2,1)} %backward.3), calls=%async_computation.1 | async-start | bytes 2621440 | tf_op jit(solution)/shard_map/all_to_all | solution.py:481
